TPU v7x, 32 devices: a whole 2x2x4 slice. The times are simulated.
32 devices in a mesh: batch: 8 (over y, x, core), tensor: 4 (over z).
Axes of the slice: x: 2, y: 2, z: 4, core: 2. Of those that a mesh axis runs over, the one named last changes fastest.
Arguments:
- block_input: bfloat16 [75264, 256], P(('batch', 'tensor')), may hold values from -6 to 6
- cotangent: bfloat16 [75264, 256], P(('batch', 'tensor')), may hold values from -6 to 6
- qkv_master: float32 [3, 256, 256], P(None, 'batch', 'tensor'), may hold values from -0.375 to 0.375
- qkv_moments: float32 [2, 3, 256, 256], P(None, None, 'batch', 'tensor'), as said below
- proj_master: float32 [256, 256], P('tensor', 'batch'), may hold values from -0.75 to 0.75
- proj_moments: float32 [2, 256, 256], P(None, 'tensor', 'batch'), as said below
- fc1_master: float32 [256, 1024], P('batch', 'tensor'), may hold values from -0.375 to 0.375
- fc1_moments: float32 [2, 256, 1024], P(None, 'batch', 'tensor'), as said below
- fc2_master: float32 [1024, 256], P('tensor', 'batch'), may hold values from -0.25 to 0.25
- fc2_moments: float32 [2, 1024, 256], P(None, 'tensor', 'batch'), as said below
- norm_params: float32 [6, 256], replicated, may hold values from -1.3 to 1.3, as said below
- norm_moments: float32 [2, 6, 256], replicated, as said below
- lepe_params: float32 [10, 256], replicated, may hold values from -1 to 1
- lepe_moments: float32 [2, 10, 256], replicated, as said below
- fc1_bias: float32 [1024], replicated, may hold values from -1.5 to 1.5
- fc1_bias_moments: float32 [2, 1024], replicated, as said below
Outputs:
- output: bfloat16 [75264, 256], P(('batch', 'tensor'))
- input_grad: float32 [75264, 256], P(('batch', 'tensor'))
- qkv_grad: float32 [3, 256, 256], P(None, 'batch', 'tensor')
- qkv_new: float32 [3, 256, 256], P(None, 'batch', 'tensor')
- qkv_low: bfloat16 [3, 256, 256], P(None, 'batch', 'tensor')
- qkv_moments_new: float32 [2, 3, 256, 256], P(None, None, 'batch', 'tensor')
- proj_grad: float32 [256, 256], P('tensor', 'batch')
- proj_new: float32 [256, 256], P('tensor', 'batch')
- proj_low: bfloat16 [256, 256], P('tensor', 'batch')
- proj_moments_new: float32 [2, 256, 256], P(None, 'tensor', 'batch')
- fc1_grad: float32 [256, 1024], P('batch', 'tensor')
- fc1_new: float32 [256, 1024], P('batch', 'tensor')
- fc1_low: bfloat16 [256, 1024], P('batch', 'tensor')
- fc1_moments_new: float32 [2, 256, 1024], P(None, 'batch', 'tensor')
- fc2_grad: float32 [1024, 256], P('tensor', 'batch')
- fc2_new: float32 [1024, 256], P('tensor', 'batch')
- fc2_low: bfloat16 [1024, 256], P('tensor', 'batch')
- fc2_moments_new: float32 [2, 1024, 256], P(None, 'tensor', 'batch')
- norm_grad: float32 [6, 256], replicated
- norm_new: float32 [6, 256], replicated
- norm_moments_new: float32 [2, 6, 256], replicated
- lepe_grad: float32 [10, 256], replicated
- lepe_new: float32 [10, 256], replicated
- lepe_moments_new: float32 [2, 10, 256], replicated
- fc1_bias_grad: float32 [1024], replicated
- fc1_bias_new: float32 [1024], replicated
- fc1_bias_moments_new: float32 [2, 1024], replicated
- grad_norm: float32 [], replicated
- rms: float32 [4], replicated
Inputs may be any that keep to these rules, and one draw needn't show every extreme that they name: `qkv_moments`: member 0 holds first moments of both signs, member 1 positive second moments. `proj_moments`: member 0 holds first moments of both signs, member 1 positive second moments. `fc1_moments`: member 0 holds first moments of both signs, member 1 positive second moments. `fc2_moments`: member 0 holds first moments of both signs, member 1 positive second moments. `norm_moments`: member 0 holds first moments of both signs, member 1 positive second moments. `lepe_moments`: member 0 holds first moments of both signs, member 1 positive second moments. `fc1_bias_moments`: member 0 holds first moments of both signs, member 1 positive second moments. `norm_params`: rows 0 and 3 are gains near one, the others signed.
All inputs are finite; a program needn't handle non-finite values.
Results may differ from a plain program's by a relative error of at most 0.0078.
The roundings to bfloat16 on the way count: a program that leaves them out, or rounds other values in their place, can miss the bound.
Values may be sent and summed in bfloat16 or wider, within the bound.
A program may use at most 256 MiB of HBM per device.

v0:
```python
import math

import jax
import jax.numpy as jnp
from jax import lax
from jax.sharding import PartitionSpec as P

HD = 32
GRID = 14
SPLIT = 7
STEP = 10
NPARAM = 791552


CLIP_SCALE = 6.0
BETA_ONE = 0.9
BETA_TWO = 0.999
ADAM_EPS = 1e-08
DECAY_RATE = 0.05
RATE_MATRIX = 0.1
RATE_VECTOR = 0.6
NORM_EPS = 1e-05


def clip_limit():
    return CLIP_SCALE * math.sqrt(NPARAM)


def layer_norm(values, gain, shift_term):
    centre = jnp.mean(values, -1, keepdims=True)
    centred = values - centre
    spread = jnp.mean(centred * centred, -1, keepdims=True)
    return centred * lax.rsqrt(spread + NORM_EPS) * gain + shift_term


def gelu_exact(values):
    return jax.nn.gelu(values, approximate=False)


def to_windows(values, branch):
    trailing = values.shape[3:]
    images = values.shape[0]
    stripes = GRID // SPLIT
    if branch == 0:
        return values.reshape((images * stripes, SPLIT, GRID) + trailing)
    moved = jnp.swapaxes(values.reshape((images, GRID, stripes, SPLIT) + trailing), 1, 2)
    return moved.reshape((images * stripes, GRID, SPLIT) + trailing)


def from_windows(values, branch, images):
    trailing = values.shape[3:]
    stripes = GRID // SPLIT
    if branch == 0:
        return values.reshape((images, GRID, GRID) + trailing)
    moved = jnp.swapaxes(values.reshape((images, stripes, GRID, SPLIT) + trailing), 1, 2)
    return moved.reshape((images, GRID, GRID) + trailing)


def flat_rows(window):
    return window.reshape((window.shape[0], window.shape[1] * window.shape[2]) + window.shape[3:])


def position_term(window, kernel, bias_term):
    height = window.shape[1]
    across = window.shape[2]
    padded = jnp.pad(window, ((0, 0), (1, 1), (1, 1), (0, 0), (0, 0)))
    summed = jnp.zeros_like(window) + bias_term
    for offset in range(9):
        summed = (
            summed
            + padded[:, offset // 3 : offset // 3 + height, offset % 3 : offset % 3 + across]
            * kernel[offset]
        )
    return summed


def split_heads(rows_in, branch, images):
    halves = rows_in.shape[1] // (2 * HD)
    return to_windows(
        rows_in.reshape(images, GRID, GRID, halves, 2, HD)[:, :, :, :, branch], branch
    )


def branch_params(lepe_local, branch):
    halves = lepe_local.shape[1] // (2 * HD)
    shaped = lepe_local.reshape(10, halves, 2, HD)
    return (shaped[:9, :, branch], shaped[9, :, branch])


def join_heads(windows, images, channels):
    merged = [from_windows(window, branch, images) for branch, window in enumerate(windows)]
    return jnp.stack(merged, -2).reshape(images * GRID * GRID, channels)


def stripe_forward(queries, key_rows, value_rows, kernel, bias_term, factor):
    scores = (
        jnp.einsum(
            "sqhe,skhe->shqk",
            flat_rows(queries),
            flat_rows(key_rows),
            preferred_element_type=jnp.float32,
        )
        * factor
    )
    highest = jnp.max(scores, -1, keepdims=True)
    raised = jnp.exp(scores - highest)
    summed = jnp.sum(raised, -1, keepdims=True)
    attend = (raised / summed).astype(jnp.bfloat16)
    mixed = jnp.einsum(
        "shqk,skhe->sqhe", attend, flat_rows(value_rows), preferred_element_type=jnp.float32
    )
    local_term = position_term(value_rows.astype(jnp.float32), kernel, bias_term)
    return (mixed + flat_rows(local_term), highest + jnp.log(summed))


def stripe_backward(queries, key_rows, value_rows, kernel, bias_term, grad_out, logsum, factor):
    flat_query = flat_rows(queries)
    flat_key = flat_rows(key_rows)
    flat_value = flat_rows(value_rows)
    scores = (
        jnp.einsum("sqhe,skhe->shqk", flat_query, flat_key, preferred_element_type=jnp.float32)
        * factor
    )
    chances = jnp.exp(scores - logsum)
    attend = chances.astype(jnp.bfloat16)
    grad_value = jnp.einsum("shqk,sqhe->skhe", attend, grad_out, preferred_element_type=jnp.float32)
    grad_chance = jnp.einsum(
        "sqhe,skhe->shqk", grad_out, flat_value, preferred_element_type=jnp.float32
    )
    row_term = jnp.sum(grad_chance * chances, -1, keepdims=True)
    grad_score = (chances * (grad_chance - row_term)).astype(jnp.bfloat16)
    grad_query = (
        jnp.einsum("shqk,skhe->sqhe", grad_score, flat_key, preferred_element_type=jnp.float32)
        * factor
    )
    grad_key = (
        jnp.einsum("shqk,sqhe->skhe", grad_score, flat_query, preferred_element_type=jnp.float32)
        * factor
    )
    unused, pull_back = jax.vjp(position_term, value_rows.astype(jnp.float32), kernel, bias_term)
    grad_window, grad_kernel, grad_bias = pull_back(
        grad_out.astype(jnp.float32).reshape(value_rows.shape)
    )
    grad_value = grad_value + flat_rows(grad_window)
    return (grad_query, grad_key, grad_value, grad_kernel, grad_bias)


def attend_forward(query_rows, key_rows, value_rows, lepe_local):
    images = query_rows.shape[0] // (GRID * GRID)
    outputs = []
    logsums = []
    for branch in range(2):
        windows = [
            split_heads(source, branch, images) for source in (query_rows, key_rows, value_rows)
        ]
        kernel, bias_term = branch_params(lepe_local, branch)
        mixed, logsum = stripe_forward(
            windows[0], windows[1], windows[2], kernel, bias_term, HD ** (-0.5)
        )
        outputs.append(mixed.reshape(windows[2].shape))
        logsums.append(logsum)
    return (join_heads(outputs, images, query_rows.shape[1]), logsums)


def attend_backward(query_rows, key_rows, value_rows, lepe_local, grad_rows, logsums):
    images = query_rows.shape[0] // (GRID * GRID)
    channels = query_rows.shape[1]
    grads_query = []
    grads_key = []
    grads_value = []
    kernels = []
    biases = []
    for branch in range(2):
        windows = [
            split_heads(source, branch, images)
            for source in (query_rows, key_rows, value_rows, grad_rows)
        ]
        kernel, bias_term = branch_params(lepe_local, branch)
        grad_query, grad_key, grad_value, grad_kernel, grad_bias = stripe_backward(
            windows[0],
            windows[1],
            windows[2],
            kernel,
            bias_term,
            flat_rows(windows[3]),
            logsums[branch],
            HD ** (-0.5),
        )
        grads_query.append(grad_query.reshape(windows[0].shape))
        grads_key.append(grad_key.reshape(windows[0].shape))
        grads_value.append(grad_value.reshape(windows[0].shape))
        kernels.append(grad_kernel)
        biases.append(grad_bias)
    grad_lepe = jnp.concatenate(
        [jnp.stack(kernels, 2).reshape(9, channels), jnp.stack(biases, 1).reshape(1, channels)], 0
    )
    return (
        join_heads(grads_query, images, channels),
        join_heads(grads_key, images, channels),
        join_heads(grads_value, images, channels),
        grad_lepe,
    )


def adam_step(master, moments, clipped, learn_rate, decay_term):
    first = BETA_ONE * moments[0] + (1.0 - BETA_ONE) * clipped
    second = BETA_TWO * moments[1] + (1.0 - BETA_TWO) * clipped * clipped
    first_hat = first / (1.0 - BETA_ONE**STEP)
    second_hat = second / (1.0 - BETA_TWO**STEP)
    updated = master - learn_rate * (
        first_hat / (jnp.sqrt(second_hat) + ADAM_EPS) + decay_term * master
    )
    return (updated, jnp.stack([first, second]))


def shards(
    block_input,
    cotangent,
    qkv_master,
    qkv_moments,
    proj_master,
    proj_moments,
    fc1_master,
    fc1_moments,
    fc2_master,
    fc2_moments,
    norm_params,
    norm_moments,
    lepe_params,
    lepe_moments,
    fc1_bias,
    fc1_bias_moments,
):
    qkv_full, proj_full, fc1_full, fc2_full = (
        lax.all_gather(qkv_master.astype(jnp.bfloat16), "batch", axis=1, tiled=True),
        lax.all_gather(proj_master.astype(jnp.bfloat16), "batch", axis=1, tiled=True),
        lax.all_gather(fc1_master.astype(jnp.bfloat16), "batch", axis=0, tiled=True),
        lax.all_gather(fc2_master.astype(jnp.bfloat16), "batch", axis=1, tiled=True),
    )
    qkv_full, proj_full, fc1_full, fc2_full = (
        lax.all_gather(qkv_full, "tensor", axis=2, tiled=True),
        lax.all_gather(proj_full, "tensor", axis=0, tiled=True),
        lax.all_gather(fc1_full, "tensor", axis=1, tiled=True),
        lax.all_gather(fc2_full, "tensor", axis=0, tiled=True),
    )
    own_rows = block_input.shape[0]
    input_float = block_input.astype(jnp.float32)
    normed_float, norm_back_one = jax.vjp(layer_norm, input_float, norm_params[0], norm_params[1])
    normed = normed_float.astype(jnp.bfloat16)
    query_rows = jnp.dot(normed, qkv_full[0], preferred_element_type=jnp.float32).astype(
        jnp.bfloat16
    )
    key_rows = jnp.dot(normed, qkv_full[1], preferred_element_type=jnp.float32).astype(jnp.bfloat16)
    value_rows = jnp.dot(normed, qkv_full[2], preferred_element_type=jnp.float32).astype(
        jnp.bfloat16
    )
    attended_float, logsums = attend_forward(query_rows, key_rows, value_rows, lepe_params)
    attended = attended_float.astype(jnp.bfloat16)
    branch_one = jnp.dot(attended, proj_full, preferred_element_type=jnp.float32)
    branch_one = branch_one + norm_params[2]
    middle = input_float + branch_one
    normed_two_float, norm_back_two = jax.vjp(layer_norm, middle, norm_params[3], norm_params[4])
    normed_two = normed_two_float.astype(jnp.bfloat16)
    hidden = jnp.dot(normed_two, fc1_full, preferred_element_type=jnp.float32) + fc1_bias
    activated_float, gelu_back = jax.vjp(gelu_exact, hidden)
    activated = activated_float.astype(jnp.bfloat16)
    branch_two = jnp.dot(activated, fc2_full, preferred_element_type=jnp.float32)
    branch_two = branch_two + norm_params[5]
    result = middle + branch_two
    output = result.astype(jnp.bfloat16)
    grad_result = cotangent.astype(jnp.float32)
    grad_fc2 = jnp.einsum("tf,td->fd", activated, cotangent, preferred_element_type=jnp.float32)
    grad_act = jnp.einsum("td,fd->tf", cotangent, fc2_full, preferred_element_type=jnp.float32)
    grad_hidden = gelu_back(grad_act)[0].astype(jnp.bfloat16)
    grad_fc1 = jnp.einsum("td,tf->df", normed_two, grad_hidden, preferred_element_type=jnp.float32)
    grad_fc1_bias = jnp.sum(grad_hidden.astype(jnp.float32), 0)
    grad_normed_two = jnp.einsum(
        "tf,df->td", grad_hidden, fc1_full, preferred_element_type=jnp.float32
    )
    grad_mid_part, grad_gain_two, grad_shift_two = norm_back_two(grad_normed_two)
    grad_middle = grad_result + grad_mid_part
    grad_branch = grad_middle.astype(jnp.bfloat16)
    grad_proj_bias = jnp.sum(grad_branch.astype(jnp.float32), 0)
    grad_fc2_bias = jnp.sum(grad_result, 0)
    grad_proj = jnp.einsum("tc,td->cd", attended, grad_branch, preferred_element_type=jnp.float32)
    grad_attended = jnp.einsum(
        "td,cd->tc", grad_branch, proj_full, preferred_element_type=jnp.float32
    ).astype(jnp.bfloat16)
    grad_query, grad_key, grad_value, grad_lepe = attend_backward(
        query_rows, key_rows, value_rows, lepe_params, grad_attended, logsums
    )
    grad_qkv_low = jnp.stack([grad_query, grad_key, grad_value], 0).astype(jnp.bfloat16)
    grad_qkv = jnp.einsum("td,jtc->jdc", normed, grad_qkv_low, preferred_element_type=jnp.float32)
    grad_normed = jnp.einsum(
        "jtc,jdc->td", grad_qkv_low, qkv_full, preferred_element_type=jnp.float32
    )
    grad_input_part, grad_gain_one, grad_shift_one = norm_back_one(grad_normed)
    input_grad = grad_middle + grad_input_part
    square_sums = jnp.stack(
        [
            jnp.sum(branch_one * branch_one),
            jnp.sum(middle * middle),
            jnp.sum(branch_two * branch_two),
            jnp.sum(result * result),
        ]
    )
    norm_grads = jnp.stack(
        [
            grad_gain_one,
            grad_shift_one,
            grad_proj_bias,
            grad_gain_two,
            grad_shift_two,
            grad_fc2_bias,
        ]
    )
    norm_summed, lepe_summed, bias_summed, square_summed = lax.psum(
        (norm_grads, grad_lepe, grad_fc1_bias, square_sums), ("batch", "tensor")
    )
    grad_qkv, grad_proj, grad_fc1, grad_fc2 = (
        lax.psum_scatter(grad_qkv, "tensor", scatter_dimension=2, tiled=True),
        lax.psum_scatter(grad_proj, "tensor", scatter_dimension=0, tiled=True),
        lax.psum_scatter(grad_fc1, "tensor", scatter_dimension=1, tiled=True),
        lax.psum_scatter(grad_fc2, "tensor", scatter_dimension=0, tiled=True),
    )
    qkv_shard, proj_shard, fc1_shard, fc2_shard = (
        lax.psum_scatter(grad_qkv, "batch", scatter_dimension=1, tiled=True),
        lax.psum_scatter(grad_proj, "batch", scatter_dimension=1, tiled=True),
        lax.psum_scatter(grad_fc1, "batch", scatter_dimension=0, tiled=True),
        lax.psum_scatter(grad_fc2, "batch", scatter_dimension=1, tiled=True),
    )
    matrix_square = (
        jnp.sum(qkv_shard * qkv_shard)
        + jnp.sum(proj_shard * proj_shard)
        + jnp.sum(fc1_shard * fc1_shard)
        + jnp.sum(fc2_shard * fc2_shard)
    )
    small_square = (
        jnp.sum(norm_summed * norm_summed)
        + jnp.sum(lepe_summed * lepe_summed)
        + jnp.sum(bias_summed * bias_summed)
    )
    grad_norm = jnp.sqrt(lax.psum(matrix_square, ("batch", "tensor")) + small_square)
    factor = jnp.minimum(1.0, clip_limit() / (grad_norm + 1e-06))
    qkv_clip = qkv_shard * factor
    proj_clip = proj_shard * factor
    fc1_clip = fc1_shard * factor
    fc2_clip = fc2_shard * factor
    norm_clip = norm_summed * factor
    lepe_clip = lepe_summed * factor
    bias_clip = bias_summed * factor
    qkv_new, qkv_moments_new = adam_step(qkv_master, qkv_moments, qkv_clip, RATE_MATRIX, DECAY_RATE)
    proj_new, proj_moments_new = adam_step(
        proj_master, proj_moments, proj_clip, RATE_MATRIX, DECAY_RATE
    )
    fc1_new, fc1_moments_new = adam_step(fc1_master, fc1_moments, fc1_clip, RATE_MATRIX, DECAY_RATE)
    fc2_new, fc2_moments_new = adam_step(fc2_master, fc2_moments, fc2_clip, RATE_MATRIX, DECAY_RATE)
    norm_new, norm_moments_new = adam_step(norm_params, norm_moments, norm_clip, RATE_VECTOR, 0.0)
    lepe_new, lepe_moments_new = adam_step(lepe_params, lepe_moments, lepe_clip, RATE_VECTOR, 0.0)
    bias_new, bias_moments_new = adam_step(fc1_bias, fc1_bias_moments, bias_clip, RATE_VECTOR, 0.0)
    all_tokens = own_rows * lax.axis_size("batch") * lax.axis_size("tensor")
    rms_values = jnp.sqrt(square_summed / (all_tokens * block_input.shape[1]))
    return (
        output,
        input_grad,
        qkv_clip,
        qkv_new,
        qkv_new.astype(jnp.bfloat16),
        qkv_moments_new,
        proj_clip,
        proj_new,
        proj_new.astype(jnp.bfloat16),
        proj_moments_new,
        fc1_clip,
        fc1_new,
        fc1_new.astype(jnp.bfloat16),
        fc1_moments_new,
        fc2_clip,
        fc2_new,
        fc2_new.astype(jnp.bfloat16),
        fc2_moments_new,
        norm_clip,
        norm_new,
        norm_moments_new,
        lepe_clip,
        lepe_new,
        lepe_moments_new,
        bias_clip,
        bias_new,
        bias_moments_new,
        grad_norm,
        rms_values,
    )


def solution(mesh):
    return jax.shard_map(
        shards,
        mesh=mesh,
        in_specs=(
            P(("batch", "tensor"), None),
            P(("batch", "tensor"), None),
            P(None, "batch", "tensor"),
            P(None, None, "batch", "tensor"),
            P("tensor", "batch"),
            P(None, "tensor", "batch"),
            P("batch", "tensor"),
            P(None, "batch", "tensor"),
            P("tensor", "batch"),
            P(None, "tensor", "batch"),
            P(),
            P(),
            P(),
            P(),
            P(),
            P(),
        ),
        out_specs=(
            P(("batch", "tensor"), None),
            P(("batch", "tensor"), None),
            P(None, "batch", "tensor"),
            P(None, "batch", "tensor"),
            P(None, "batch", "tensor"),
            P(None, None, "batch", "tensor"),
            P("tensor", "batch"),
            P("tensor", "batch"),
            P("tensor", "batch"),
            P(None, "tensor", "batch"),
            P("batch", "tensor"),
            P("batch", "tensor"),
            P("batch", "tensor"),
            P(None, "batch", "tensor"),
            P("tensor", "batch"),
            P("tensor", "batch"),
            P("tensor", "batch"),
            P(None, "tensor", "batch"),
            P(),
            P(),
            P(),
            P(),
            P(),
            P(),
            P(),
            P(),
            P(),
            P(),
            P(),
        ),
        check_vma=False,
    )
```

profile of v0, /device:TPU:0, one launch (start us, length us, event | category | flops | bytes accessed | tf_op | source)
XLA Modules:
  0.0 1002.5 jit_solution(12349785939137506228)
XLA Ops:
  15.1 10.7 %all_gather.24 = bf16[3,256,64]{2,1,0:T(8,128)(2,1)S(1)} all-gather(bf16[3,32,64]{2,1,0:T(8,128)(2,1)S(1)} %convert_element_type.141), channel_id=1, replica_groups=mesh['batch'=8,'tensor'=4] {'batch'}, dimensions={1}, use_global_device_ids=true | all-gather | bytes 110592 | tf_op jit(solution)/shard_map/all_gather | solution.py:235
  25.9 15.1 %all_gather.25 = bf16[3,256,256]{1,2,0:T(8,128)(2,1)S(1)} all-gather(bf16[3,256,64]{1,2,0:T(8,128)(2,1)S(1)} %copy.464), channel_id=1, replica_groups=mesh['batch'=8,'tensor'=4] {'tensor'}, dimensions={2}, use_global_device_ids=true | all-gather | bytes 491520 | tf_op jit(solution)/shard_map/all_gather | solution.py:241
  48.1 11.1 %reshape.375 = bf16[12,14,14,4,2,32]{5,4,3,2,1,0:T(2,128)(2,1)} reshape(bf16[2352,256]{1,0:T(8,128)(2,1)} %convolution_convert_fusion.3) | data formatting | bytes 2408448 | tf_op jit(solution)/shard_map/reshape | solution.py:80
  59.2 12.0 %fusion.99 = (bf16[12,14,14,4,1,32]{5,4,3,2,1,0:T(2,128)(2,1)}, bf16[12,14,14,4,1,32]{5,4,3,2,1,0:T(2,128)(2,1)S(1)}) fusion(bf16[12,14,14,4,2,32]{5,4,3,2,1,0:T(2,128)(2,1)} %reshape.375), kind=kLoop, calls=%fused_computation.291 | loop fusion | bytes 2408448 | tf_op jit(solution)/shard_map/slice | solution.py:80
  79.6 9.2 all_gather.26
  88.9 13.6 %all_gather.27 = bf16[256,256]{1,0:T(8,128)(2,1)S(1)} all-gather(bf16[64,256]{1,0:T(8,128)(2,1)S(1)} %copy.510), channel_id=1, replica_groups=mesh['batch'=8,'tensor'=4] {'tensor'}, dimensions={0}, use_global_device_ids=true | all-gather | bytes 163840 | tf_op jit(solution)/shard_map/all_gather | solution.py:242
  102.5 8.4 all_gather.30
  111.0 9.2 all_gather.28
  120.1 16.6 %all_gather.29 = bf16[256,1024]{1,0:T(8,128)(2,1)S(1)} all-gather(bf16[256,256]{1,0:T(8,128)(2,1)S(1)} %all_gather.28), channel_id=1, replica_groups=mesh['batch'=8,'tensor'=4] {'tensor'}, dimensions={1}, use_global_device_ids=true | all-gather | bytes 655360 | tf_op jit(solution)/shard_map/all_gather | solution.py:243
  136.8 16.4 %all_gather.31 = bf16[1024,256]{0,1:T(8,128)(2,1)} all-gather(bf16[256,256]{0,1:T(8,128)(2,1)S(1)} %all_gather.30), channel_id=1, replica_groups=mesh['batch'=8,'tensor'=4] {'tensor'}, dimensions={0}, use_global_device_ids=true | all-gather | bytes 655360 | tf_op jit(solution)/shard_map/all_gather | solution.py:244
  153.2 11.1 %reshape.376 = bf16[12,14,14,4,2,32]{5,4,3,2,1,0:T(2,128)(2,1)} reshape(bf16[2352,256]{1,0:T(8,128)(2,1)} %convolution_convert_fusion.2) | data formatting | bytes 2408448 | tf_op jit(solution)/shard_map/reshape | solution.py:80
  167.9 12.0 %fusion.97 = (bf16[12,14,14,4,1,32]{5,4,3,2,1,0:T(2,128)(2,1)S(1)}, bf16[12,14,14,4,1,32]{5,4,3,2,1,0:T(2,128)(2,1)}) fusion(bf16[12,14,14,4,2,32]{5,4,3,2,1,0:T(2,128)(2,1)} %reshape.377), kind=kLoop, calls=%fused_computation.289 | loop fusion | bytes 2408448 | tf_op jit(solution)/shard_map/slice | solution.py:80
  196.7 12.1 %fusion.98 = (bf16[12,14,14,4,1,32]{5,4,3,2,1,0:T(2,128)(2,1)S(1)}, bf16[12,14,14,4,1,32]{5,4,3,2,1,0:T(2,128)(2,1)}) fusion(bf16[12,14,14,4,2,32]{5,4,3,2,1,0:T(2,128)(2,1)} %reshape.376), kind=kLoop, calls=%fused_computation.290 | loop fusion | bytes 2408448 | tf_op jit(solution)/shard_map/slice | solution.py:80
  241.8 8.4 multiply_add_fusion.1
  255.3 16.4 %multiply_add_fusion = f32[24,14,7,4,32]{4,0,3,2,1:T(8,128)} fusion(f32[24,14,7,4,32]{4,0,3,2,1:T(8,128)} %bitcast.383, f32[4,32]{1,0:T(4,128)S(1)} %bitcast.465, f32[4,32]{1,0:T(4,128)S(1)} %bitcast.449, f32[4,32]{1,0:T(4,128)S(1)} %bitcast.451, f32[4,32]{1,0:T(4,128)S(1)} %bitcast.453, f32[4,32]{1,0:T(4,128)S(1)} %bitcast.455, f32[4,32]{1,0:T(4,128)S(1)} %bitcast.457, ...), kind=kLoop, calls=%fused_computation.80 | loop fusion | flops 5419008 | bytes 2413568 | tf_op jit(solution)/shard_map/add | solution.py:70
  271.6 5.7 copy.506
  303.2 8.6 pad_maximum_fusion
  311.8 12.4 %copy.509 = bf16[12,14,14,4,2,32]{5,4,3,2,1,0:T(2,128)(2,1)} copy(bf16[12,14,14,4,2,32]{5,3,2,1,0,4:T(4,128)(2,1)} %pad_maximum_fusion) | data formatting | bytes 2408448 | tf_op jit(solution)/shard_map/stack | solution.py:92
  324.1 12.5 %convert_element_type.151 = bf16[2352,256]{1,0:T(8,128)(2,1)S(1)} reshape(bf16[12,14,14,4,2,32]{5,4,3,2,1,0:T(2,128)(2,1)} %copy.509) | data formatting | bytes 2408448 | tf_op jit(solution)/shard_map/convert_element_type | solution.py:258
  339.0 24.9 %multiply_convert_fusion = (bf16[2352,1024]{1,0:T(8,128)(2,1)S(1)}, f32[2352,1024]{1,0:T(8,128)S(1)}, f32[2352,1024]{1,0:T(8,128)}) fusion(f32[1024]{0:T(1024)S(1)} %copy-done.117, bf16[256,1024]{1,0:T(8,128)(2,1)S(1)} %all_gather.29, f32[2352,256]{1,0:T(8,128)S(1)} %get-tuple-element.244, f32[256]{0:T(256)S(1)} %bitcast.539, f32[256]{0:T(256)S(1)} %bitcast.532, ...), kind=kOutput, calls=%fused_computation.12 | convolution fusion | flops 1395093504 | bytes 27042176 | tf_op jit(solution)/shard_map/dot_general | solution.py:264
  363.9 9.9 convert_reduce_fusion
  389.3 11.9 %fusion.96 = (bf16[12,14,14,4,1,32]{5,4,3,2,1,0:T(2,128)(2,1)}, bf16[12,14,14,4,1,32]{5,4,3,2,1,0:T(2,128)(2,1)S(1)}) fusion(bf16[12,14,14,4,2,32]{5,4,3,2,1,0:T(2,128)(2,1)} %reshape.381), kind=kLoop, calls=%fused_computation.288 | loop fusion | bytes 2408448 | tf_op jit(solution)/shard_map/slice | solution.py:80
  438.9 12.7 %multiply_reduce_fusion.19 = (f32[4,32]{1,0:T(4,128)S(1)}, f32[4,32]{1,0:T(4,128)S(1)}, f32[4,32]{1,0:T(4,128)S(1)}, f32[4,32]{1,0:T(4,128)S(1)}, f32[4,32]{1,0:...) fusion(f32[24,7,14,4,32]{4,3,2,1,0:T(4,128)S(1)} %bitcast.386, ...), kind=kLoop, calls=%fused_computation.79 | loop fusion | flops 5116928 | bytes 3014656 | tf_op jit(solution)/shard_map/transpose(jvp())/reduce_sum | solution.py:71
  469.1 8.6 pad_maximum_fusion.1
  477.7 12.3 %copy.525 = bf16[12,14,14,4,2,32]{5,4,3,2,1,0:T(2,128)(2,1)} copy(bf16[12,14,14,4,2,32]{5,3,2,1,0,4:T(4,128)(2,1)} %pad_maximum_fusion.1) | data formatting | bytes 2408448 | tf_op jit(solution)/shard_map/stack | solution.py:92
  490.1 13.3 %stack_reshape.30 = bf16[1,2352,256]{2,1,0:T(8,128)(2,1)} reshape(bf16[12,14,14,4,2,32]{5,4,3,2,1,0:T(2,128)(2,1)} %copy.525) | data formatting | bytes 2408448 | tf_op jit(solution)/shard_map/stack;reshape | solution.py:292
  506.0 7.9 pad_maximum_fusion.2
  513.9 12.1 %copy.533 = bf16[12,14,14,4,2,32]{5,4,3,2,1,0:T(2,128)(2,1)} copy(bf16[12,14,14,4,2,32]{5,3,2,1,0,4:T(4,128)(2,1)} %pad_maximum_fusion.2) | data formatting | bytes 2408448 | tf_op jit(solution)/shard_map/stack | solution.py:92
  526.1 13.3 %stack_reshape.32 = bf16[1,2352,256]{2,1,0:T(8,128)(2,1)} reshape(bf16[12,14,14,4,2,32]{5,4,3,2,1,0:T(2,128)(2,1)} %copy.533) | data formatting | bytes 2408448 | tf_op jit(solution)/shard_map/stack;reshape | solution.py:292
  540.6 23.9 %multiply_reduce_fusion.10 = (f32[4,32]{1,0:T(4,128)S(1)}, f32[4,32]{1,0:T(4,128)S(1)}, f32[4,32]{1,0:T(4,128)S(1)}, f32[4,32]{1,0:T(4,128)S(1)}, f32[4,32]{1,0:...) fusion(f32[24,14,7,4,32]{4,0,3,2,1:T(8,128)} %bitcast.399, ...), kind=kLoop, calls=%fused_computation.70 | loop fusion | flops 7525376 | bytes 13255168 | tf_op jit(solution)/shard_map/transpose(jvp())/reduce_sum | solution.py:71
  564.5 6.2 pad_add_fusion
  570.7 8.8 pad_add_fusion.2
  595.8 14.1 %broadcast_multiply_fusion.9 = (f32[24,7,7,8,32]{4,3,2,1,0:T(8,128)}, f32[24,7,7,8,32]{4,3,2,1,0:T(8,128)S(1)}, f32[24,7,7,8,32]{4,3,2,1,0:T(8,128)}, f32[24,7,7...) fusion(f32[24,7,7,8,32]{4,3,2,1,0:T(8,128)} %bitcast.404, ...), kind=kLoop, calls=%fused_computation.142 | loop fusion | flops 2709504 | bytes 12051456 | tf_op jit(solution)/shard_map/transpose(jvp())/mul | solution.py:71
  609.9 8.3 pad_add_fusion.1
  618.2 10.1 %pad_add_fusion.8 = f32[24,7,14,4,32]{4,3,2,1,0:T(4,128)} fusion(f32[24,7,14,4,32]{4,3,2,1,0:T(4,128)S(1)} %bitcast.407, f32[24,7,14,4,32]{4,3,2,1,0:T(4,128)S(1)} %bitcast.408, f32[24,7,14,4,32]{4,3,2,1,0:T(4,128)S(1)} %bitcast.409, f32[24,7,14,4,32]{4,3,2,1,0:T(4,128)} %bitcast.410, f32[24,7,14,4,32]{4,3,2,1,0:T(4,128)} %bitcast.411, ...), kind=kLoop, calls=%fused_computation.52 | loop fusion | flops 1806336 | bytes 9633792 | tf_op jit(solution)/shard_map/transpose(jvp())/add_any | solution.py:71
  633.3 5.3 fusion.32
  643.2 7.9 pad_maximum_fusion.3
  651.1 12.2 %copy.545 = bf16[12,14,14,4,2,32]{5,4,3,2,1,0:T(2,128)(2,1)} copy(bf16[12,14,14,4,2,32]{5,3,2,1,0,4:T(4,128)(2,1)} %pad_maximum_fusion.3) | data formatting | bytes 2408448 | tf_op jit(solution)/shard_map/stack | solution.py:92
  663.4 13.4 %stack_reshape.34 = bf16[1,2352,256]{2,1,0:T(8,128)(2,1)} reshape(bf16[12,14,14,4,2,32]{5,4,3,2,1,0:T(2,128)(2,1)} %copy.545) | data formatting | bytes 2408448 | tf_op jit(solution)/shard_map/stack;reshape | solution.py:292
  690.5 6.5 fusion.80
  710.9 26.8 %reduce-scatter.20.cloned.1.call-done = f32[256,256]{1,0:T(8,128)} async-done(((f32[1024,256]{1,0:T(8,128)}), f32[256,256]{1,0:T(8,128)}) %reduce-scatter.20.cloned.1.call-update) | async-done | bytes 262160 | tf_op jit(solution)/shard_map/reduce_scatter | solution.py:324
  739.7 5.3 convert_reduce_fusion.2
  745.0 20.6 %reduce-scatter.16.cloned.1.call-done = f32[256,256]{1,0:T(8,128)} async-done(((f32[256,1024]{1,0:T(8,128)}), f32[256,256]{1,0:T(8,128)}) %reduce-scatter.16.cloned.1.call-update) | async-done | bytes 262160 | tf_op jit(solution)/shard_map/reduce_scatter | solution.py:323
  770.5 30.4 %reduce-scatter.22.cloned.1.call-done = f32[32,64]{1,0:T(8,128)} async-done(((f32[256,64]{1,0:T(8,128)}), f32[32,64]{1,0:T(8,128)}) %reduce-scatter.22.cloned.1.call-update) | async-done | bytes 8208
  802.3 56.1 %all-reduce.42.cloned.1.call-done = f32[3,256,64]{2,0,1:T(4,128)} async-done(((f32[3,256,64]{2,0,1:T(4,128)}), f32[3,256,64]{2,0,1:T(4,128)}) %all-reduce.42.cloned.1.call-update) | async-done | bytes 196624
  861.2 33.5 %reduce-scatter.24.cloned.1.call-done = f32[32,256]{1,0:T(8,128)} async-done(((f32[256,256]{1,0:T(8,128)}), f32[32,256]{1,0:T(8,128)}) %reduce-scatter.24.cloned.1.call-update) | async-done | bytes 32784
  896.1 35.2 %reduce-scatter.18.cloned.1.call-done = f32[32,256]{1,0:T(8,128)} async-done(((f32[256,256]{1,0:T(8,128)}), f32[32,256]{1,0:T(8,128)}) %reduce-scatter.18.cloned.1.call-update) | async-done | bytes 32784 | tf_op jit(solution)/shard_map/reduce_scatter | solution.py:329
  934.0 40.0 %all-reduce.39 = (f32[]{:T(128)}, f32[6,256]{1,0:T(8,128)S(1)}, f32[10,256]{1,0:T(8,128)S(1)}, f32[1024]{0:T(1024)S(1)}, f32[4]{0:T(128)S(1)}) all-reduce(f32[]{:T(128)S(6)} %add.454, f32[6,256]{1,0:T(8,128)S(1)} %stack.136, f32[10,256]{1,0:T(8,128)S(1)} %pad_maximum_fusion.10, ...), channel_id=1, replica_groups=mesh['batch'=8,'tensor'=4] {'batch','tensor'}, use_global_device_ids=true, to_apply=%region_26.27 | all-reduce | flops 5125 | bytes 41000 | tf_op jit(solution)/shard_map/psum | solution.py:343
  (483 shorter events, 265.5 us)
Async XLA Ops:
  7.2 36.1 %copy-start.6 = (bf16[2352,256]{1,0:T(8,128)(2,1)S(1)}, bf16[2352,256]{1,0:T(8,128)(2,1)}, u32[]{:S(2)}) copy-start(bf16[2352,256]{1,0:T(8,128)(2,1)} %param.16) | copy-start | bytes 3612676
  7.2 697.9 %reduce-scatter.14.cloned.1.call-start = ((), (), s32[]{:S(2)}) async-start(), calls=%async_computation.8 | async-start | bytes 327680 | tf_op jit(solution)/shard_map/reduce_scatter | solution.py:322
  8.2 247.0 %copy-start.92 = (f32[1,4,1,32]{3,2,1,0:T(1,128)}, f32[1,4,1,32]{3,2,1,0:T(1,128)S(1)}, u32[]{:S(2)}) copy-start(f32[1,4,1,32]{3,2,1,0:T(1,128)S(1)} %slice.382) | copy-start | bytes 1540
  8.2 233.5 %copy-start.94 = (f32[1,4,1,32]{3,2,1,0:T(1,128)}, f32[1,4,1,32]{3,2,1,0:T(1,128)S(1)}, u32[]{:S(2)}) copy-start(f32[1,4,1,32]{3,2,1,0:T(1,128)S(1)} %get-tuple-element.301) | copy-start | bytes 1540
  8.2 233.5 %copy-start.96 = (f32[1,4,1,32]{3,2,1,0:T(1,128)}, f32[1,4,1,32]{3,2,1,0:T(1,128)S(1)}, u32[]{:S(2)}) copy-start(f32[1,4,1,32]{3,2,1,0:T(1,128)S(1)} %get-tuple-element.300) | copy-start | bytes 1540
  8.3 233.5 %copy-start.98 = (f32[1,4,1,32]{3,2,1,0:T(1,128)}, f32[1,4,1,32]{3,2,1,0:T(1,128)S(1)}, u32[]{:S(2)}) copy-start(f32[1,4,1,32]{3,2,1,0:T(1,128)S(1)} %get-tuple-element.299) | copy-start | bytes 1540
  8.3 233.5 %copy-start.100 = (f32[1,4,1,32]{3,2,1,0:T(1,128)}, f32[1,4,1,32]{3,2,1,0:T(1,128)S(1)}, u32[]{:S(2)}) copy-start(f32[1,4,1,32]{3,2,1,0:T(1,128)S(1)} %get-tuple-element.298) | copy-start | bytes 1540
  8.3 233.5 %copy-start.102 = (f32[1,4,1,32]{3,2,1,0:T(1,128)}, f32[1,4,1,32]{3,2,1,0:T(1,128)S(1)}, u32[]{:S(2)}) copy-start(f32[1,4,1,32]{3,2,1,0:T(1,128)S(1)} %get-tuple-element.297) | copy-start | bytes 1540
  8.3 233.5 %copy-start.104 = (f32[1,4,1,32]{3,2,1,0:T(1,128)}, f32[1,4,1,32]{3,2,1,0:T(1,128)S(1)}, u32[]{:S(2)}) copy-start(f32[1,4,1,32]{3,2,1,0:T(1,128)S(1)} %get-tuple-element.296) | copy-start | bytes 1540
  8.3 233.5 %copy-start.106 = (f32[1,4,1,32]{3,2,1,0:T(1,128)}, f32[1,4,1,32]{3,2,1,0:T(1,128)S(1)}, u32[]{:S(2)}) copy-start(f32[1,4,1,32]{3,2,1,0:T(1,128)S(1)} %get-tuple-element.295) | copy-start | bytes 1540
  8.3 233.5 %copy-start.108 = (f32[1,4,1,32]{3,2,1,0:T(1,128)}, f32[1,4,1,32]{3,2,1,0:T(1,128)S(1)}, u32[]{:S(2)}) copy-start(f32[1,4,1,32]{3,2,1,0:T(1,128)S(1)} %get-tuple-element.294) | copy-start | bytes 1540
  8.3 233.5 %copy-start.110 = (f32[1,4,1,32]{3,2,1,0:T(1,128)}, f32[1,4,1,32]{3,2,1,0:T(1,128)S(1)}, u32[]{:S(2)}) copy-start(f32[1,4,1,32]{3,2,1,0:T(1,128)S(1)} %get-tuple-element.293) | copy-start | bytes 1540
  8.3 246.9 %copy-start.76 = (f32[1,4,1,32]{3,2,1,0:T(1,128)}, f32[1,4,1,32]{3,2,1,0:T(1,128)S(1)}, u32[]{:S(2)}) copy-start(f32[1,4,1,32]{3,2,1,0:T(1,128)S(1)} %get-tuple-element.284) | copy-start | bytes 1540
  8.3 246.9 %copy-start.78 = (f32[1,4,1,32]{3,2,1,0:T(1,128)}, f32[1,4,1,32]{3,2,1,0:T(1,128)S(1)}, u32[]{:S(2)}) copy-start(f32[1,4,1,32]{3,2,1,0:T(1,128)S(1)} %get-tuple-element.285) | copy-start | bytes 1540
  8.4 246.8 %copy-start.80 = (f32[1,4,1,32]{3,2,1,0:T(1,128)}, f32[1,4,1,32]{3,2,1,0:T(1,128)S(1)}, u32[]{:S(2)}) copy-start(f32[1,4,1,32]{3,2,1,0:T(1,128)S(1)} %get-tuple-element.286) | copy-start | bytes 1540
  8.4 246.8 %copy-start.82 = (f32[1,4,1,32]{3,2,1,0:T(1,128)}, f32[1,4,1,32]{3,2,1,0:T(1,128)S(1)}, u32[]{:S(2)}) copy-start(f32[1,4,1,32]{3,2,1,0:T(1,128)S(1)} %get-tuple-element.287) | copy-start | bytes 1540
  8.4 246.8 %copy-start.84 = (f32[1,4,1,32]{3,2,1,0:T(1,128)}, f32[1,4,1,32]{3,2,1,0:T(1,128)S(1)}, u32[]{:S(2)}) copy-start(f32[1,4,1,32]{3,2,1,0:T(1,128)S(1)} %get-tuple-element.288) | copy-start | bytes 1540
  8.4 246.8 %copy-start.86 = (f32[1,4,1,32]{3,2,1,0:T(1,128)}, f32[1,4,1,32]{3,2,1,0:T(1,128)S(1)}, u32[]{:S(2)}) copy-start(f32[1,4,1,32]{3,2,1,0:T(1,128)S(1)} %get-tuple-element.289) | copy-start | bytes 1540
  8.4 246.8 %copy-start.88 = (f32[1,4,1,32]{3,2,1,0:T(1,128)}, f32[1,4,1,32]{3,2,1,0:T(1,128)S(1)}, u32[]{:S(2)}) copy-start(f32[1,4,1,32]{3,2,1,0:T(1,128)S(1)} %get-tuple-element.290) | copy-start | bytes 1540
  8.4 246.8 %copy-start.90 = (f32[1,4,1,32]{3,2,1,0:T(1,128)}, f32[1,4,1,32]{3,2,1,0:T(1,128)S(1)}, u32[]{:S(2)}) copy-start(f32[1,4,1,32]{3,2,1,0:T(1,128)S(1)} %get-tuple-element.291) | copy-start | bytes 1540
  9.9 35.8 %copy-start.113 = (f32[1,256]{1,0:T(1,128)}, f32[1,256]{1,0:T(1,128)S(1)}, u32[]{:S(2)}) copy-start(f32[1,256]{1,0:T(1,128)S(1)} %get-tuple-element.319) | copy-start | bytes 3076
  9.9 35.8 %copy-start.126 = (f32[1,256]{1,0:T(1,128)}, f32[1,256]{1,0:T(1,128)S(1)}, u32[]{:S(2)}) copy-start(f32[1,256]{1,0:T(1,128)S(1)} %get-tuple-element.318) | copy-start | bytes 3076
  9.9 329.0 %copy-start.124 = (f32[1,256]{1,0:T(1,128)}, f32[1,256]{1,0:T(1,128)S(1)}, u32[]{:S(2)}) copy-start(f32[1,256]{1,0:T(1,128)S(1)} %get-tuple-element.315) | copy-start | bytes 3076
  9.9 369.6 %copy-start.120 = (f32[1,256]{1,0:T(1,128)}, f32[1,256]{1,0:T(1,128)S(1)}, u32[]{:S(2)}) copy-start(f32[1,256]{1,0:T(1,128)S(1)} %get-tuple-element.316) | copy-start | bytes 3076
  11.6 34.0 %copy-start.43 = (f32[2352]{0:T(1024)}, f32[2352]{0:T(1024)S(1)}, u32[]{:S(2)}) copy-start(f32[2352]{0:T(1024)S(1)} %broadcast_multiply_fusion.23) | copy-start | bytes 28228
  14.3 33.8 %copy-start.56 = (f32[2352]{0:T(1024)}, f32[2352]{0:T(1024)S(1)}, u32[]{:S(2)}) copy-start(f32[2352]{0:T(1024)S(1)} %fusion.59) | copy-start | bytes 28228
  185.3 109.8 %copy-start.15 = (bf16[24,98,4,32]{1,3,2,0:T(8,128)(2,1)}, bf16[24,98,4,32]{1,3,2,0:T(8,128)(2,1)S(1)}, u32[]{:S(2)}) copy-start(bf16[24,98,4,32]{1,3,2,0:T(8,128)(2,1)S(1)} %copy.469) | copy-start | bytes 1806340
  214.6 80.5 %copy-start.17 = (bf16[24,98,4,32]{1,3,2,0:T(8,128)(2,1)}, bf16[24,98,4,32]{1,3,2,0:T(8,128)(2,1)S(1)}, u32[]{:S(2)}) copy-start(bf16[24,98,4,32]{1,3,2,0:T(8,128)(2,1)S(1)} %copy.468) | copy-start | bytes 1806340
  338.2 41.3 %copy-start.10 = (f32[2352,256]{1,0:T(8,128)}, f32[2352,256]{1,0:T(8,128)S(1)}, u32[]{:S(2)}) copy-start(f32[2352,256]{1,0:T(8,128)S(1)} %get-tuple-element.244) | copy-start | bytes 7225348
  338.2 41.3 %copy-start.62 = (f32[2352]{0:T(1024)}, f32[2352]{0:T(1024)S(1)}, u32[]{:S(2)}) copy-start(f32[2352]{0:T(1024)S(1)} %broadcast_multiply_fusion.22) | copy-start | bytes 28228
  338.9 40.6 %copy-start.70 = (f32[2352]{0:T(1024)}, f32[2352]{0:T(1024)S(1)}, u32[]{:S(2)}) copy-start(f32[2352]{0:T(1024)S(1)} %fusion.60) | copy-start | bytes 28228
  384.8 324.1 %reduce-scatter.12.cloned.1.call-start = ((), (), s32[]{:S(2)}) async-start(), calls=%async_computation.7 | async-start | bytes 983040 | tf_op jit(solution)/shard_map/reduce_scatter | solution.py:321
  685.3 52.4 %reduce-scatter.20.cloned.1.call-start = ((), (), s32[]{:S(2)}) async-start(), calls=%async_computation.11 | async-start | bytes 1310720 | tf_op jit(solution)/shard_map/reduce_scatter | solution.py:324
  690.4 75.3 %reduce-scatter.16.cloned.1.call-start = ((), (), s32[]{:S(2)}) async-start(), calls=%async_computation.9 | async-start | bytes 1310720 | tf_op jit(solution)/shard_map/reduce_scatter | solution.py:323
  697.0 103.8 %reduce-scatter.22.cloned.1.call-start = ((), (), s32[]{:S(2)}) async-start(), calls=%async_computation.12 | async-start | bytes 147456
  703.5 36.3 %copy-start.9 = (bf16[2352,256]{1,0:T(8,128)(2,1)S(1)}, bf16[2352,256]{1,0:T(8,128)(2,1)}, u32[]{:S(2)}) copy-start(bf16[2352,256]{1,0:T(8,128)(2,1)} %param.16) | copy-start | bytes 3612676
  703.5 36.3 %copy-start.27 = (bf16[2352,256]{1,0:T(8,128)(2,1)S(1)}, bf16[2352,256]{1,0:T(8,128)(2,1)}, u32[]{:S(2)}) copy-start(bf16[2352,256]{1,0:T(8,128)(2,1)} %param.17) | copy-start | bytes 3612676
  703.5 36.2 %copy-start.59 = (f32[2352]{0:T(1024)S(1)}, f32[2352]{0:T(1024)}, u32[]{:S(2)}) copy-start(f32[2352]{0:T(1024)} %copy-done.58) | copy-start | bytes 28228
  706.7 151.7 %all-reduce.42.cloned.1.call-start = ((), (), s32[]{:S(2)}) async-start(), calls=%async_computation.14 | async-start | bytes 1048576
  710.9 183.8 %reduce-scatter.24.cloned.1.call-start = ((), (), s32[]{:S(2)}) async-start(), calls=%async_computation.13 | async-start | bytes 294912
  739.6 194.4 %copy-start.119 = (f32[1024]{0:T(1024)S(1)}, f32[1024]{0:T(1024)}, u32[]{:S(2)}) copy-start(f32[1024]{0:T(1024)} %get-tuple-element.330) | copy-start | bytes 12292
  739.6 239.4 %copy-start.74 = (f32[6,256]{1,0:T(8,128)S(1)}, f32[6,256]{1,0:T(8,128)}, u32[]{:S(2)}) copy-start(f32[6,256]{1,0:T(8,128)} %param.26) | copy-start | bytes 18436
  739.6 240.7 %copy-start.68 = (f32[10,256]{1,0:T(8,128)S(1)}, f32[10,256]{1,0:T(8,128)}, u32[]{:S(2)}) copy-start(f32[10,256]{1,0:T(8,128)} %param.28) | copy-start | bytes 30724
  739.6 246.3 %copy-start.49 = (f32[3,32,64]{2,1,0:T(8,128)S(1)}, f32[3,32,64]{2,1,0:T(8,128)}, u32[]{:S(2)}) copy-start(f32[3,32,64]{2,1,0:T(8,128)} %param.18) | copy-start | bytes 73732
  739.6 248.4 %copy-start.50 = (f32[2,32,256]{2,1,0:T(8,128)S(1)}, f32[2,32,256]{2,1,0:T(8,128)}, u32[]{:S(2)}) copy-start(f32[2,32,256]{2,1,0:T(8,128)} %param.23) | copy-start | bytes 196612
  739.6 249.1 %copy-start.54 = (f32[32,256]{1,0:T(8,128)S(1)}, f32[32,256]{1,0:T(8,128)}, u32[]{:S(2)}) copy-start(f32[32,256]{1,0:T(8,128)} %param.22) | copy-start | bytes 98308
  739.7 191.6 %reduce-scatter.18.cloned.1.call-start = ((), (), s32[]{:S(2)}) async-start(), calls=%async_computation.10 | async-start | bytes 294912 | tf_op jit(solution)/shard_map/reduce_scatter | solution.py:329
  745.0 246.8 %copy-start.118 = (f32[1024]{0:T(1024)S(1)}, f32[1024]{0:T(1024)}, u32[]{:S(2)}) copy-start(f32[1024]{0:T(1024)} %param.30) | copy-start | bytes 12292
  (102 other events, 914.2 us)
Sparse Core Ops, SparseCore 0:
  384.9 19.7 reduce-scatter.13
  685.4 23.4 reduce-scatter.11
  711.3 26.3 reduce-scatter.19
  739.9 25.7 reduce-scatter.15
  768.8 32.0 reduce-scatter.21
  803.8 54.5 all-reduce.41
  861.7 32.8 reduce-scatter.23
  897.7 33.5 reduce-scatter.17
where the time goes:
time: 1010 us; the launch traced here: 1000 us
  local copies, waits for them, and re-layouts  343 us (34%)
  waiting for transfers between devices  205 us (20%)
  other arithmetic  188 us (19%)
  blocking collectives  139 us (14%)
  matrix products  103 us (10%)
  between operations  23.6 us (2%)
    unnamed x11, waiting for transfers between devices  120 us
    another operation x4, local copies, waits for them, and re-layouts, join_heads(): return jnp.stack(merged, -2).reshape(images * GRID * GRID, channels)  49.1 us
    slice x4, local copies, waits for them, and re-layouts, split_heads(): rows_in.reshape(images, GRID, GRID, halves, 2, HD)[:, :, :, :, branch]  48.1 us
    reduce_sum x4, other arithmetic, position_term(): padded[:, offset // 3:offset // 3 + height, offset % 3:offset % 3 + across]  44.5 us
    another operation x4, local copies, waits for them, and re-layouts, shards(): jnp.stack([grad_query, grad_key, grad_value], 0).astype(jnp.bfloat16)  42.4 us
    unnamed x326, local copies, waits for them, and re-layouts  40.1 us
    psum x1, blocking collectives, shards(): lax.psum(matrix_square, ('batch', 'tensor')) + small_square  40 us
    reduce_scatter x1, waiting for transfers between devices, shards(): lax.psum_scatter(grad_fc1, 'batch', scatter_dimension=0, tiled=True)  35.2 us
  transfers between devices with their start and end apart: 8, of which 7 were waited for; matrix products, arithmetic and copies ran while one was open for 34% of the time, Pallas kernels for 0%

commit v1 on v0

v1 whole, which is shorter than its diff:
```python
import functools, math
import numpy as np
import jax, jax.numpy as jnp
from jax import lax
from jax.experimental import pallas as pl
from jax.experimental.pallas import tpu as pltpu
from jax.sharding import PartitionSpec as P

HD = 32
STEP = 10
NPARAM = 791552
CLIP_SCALE = 6.0
BETA_ONE = 0.9
BETA_TWO = 0.999
ADAM_EPS = 1e-08
DECAY_RATE = 0.05
RATE_MATRIX = 0.1
RATE_VECTOR = 0.6
GRID = 14
SPLIT = 7
CELLS = 196
PAD = 112
D = 256
FF = 1024
NORM_EPS = 1e-5
BF = jnp.bfloat16
F32 = jnp.float32
SCALE = HD ** -0.5
LOG2E = 1.4426950408889634


def slot_of(branch, cell):
    row, col = divmod(cell, GRID)
    if branch == 0:
        return row * 16 + col
    stripe, inner = divmod(col, SPLIT)
    return stripe * PAD + row * 8 + inner


def spread_tables():
    into = np.zeros((2, 4, 2 * PAD, 208), np.float32)
    for branch in range(2):
        for cell in range(CELLS):
            for j in range(4):
                into[branch, j, slot_of(branch, cell), cell + 4 * j] = 1.0
    return into.reshape(8, 2 * PAD, 208), into.transpose(0, 1, 3, 2).reshape(8, 208, 2 * PAD)


def key_mask():
    mask = np.full((2, PAD, 128), -1e30, np.float32)
    for branch in range(2):
        for cell in range(CELLS):
            slot = slot_of(branch, cell)
            if slot < PAD:
                mask[branch, slot] = 0.0
    return mask


def lane_table(tensor):
    heads = 4 // tensor
    assert heads == 1
    table = np.zeros((512, 512), np.float32)
    for t in range(4):
        for j in range(2):
            for b in range(2):
                for e in range(HD):
                    table[t * 128 + j * 64 + b * 32 + e, b * 256 + j * 128 + t * 32 + e] = 1.0
    return table


def dot(a, b):
    return lax.dot_general(a, b, (((1,), (0,)), ((), ())), preferred_element_type=F32)


def dot_nt(a, b):
    return lax.dot_general(a, b, (((1,), (1,)), ((), ())), preferred_element_type=F32)


def norm_stats(v):
    centre = jnp.mean(v, -1, keepdims=True)
    centred = v - centre
    spread = jnp.mean(centred * centred, -1, keepdims=True)
    rate = lax.rsqrt(spread + NORM_EPS)
    return centred * rate, rate


def norm_back(grad, gain, xhat, rate):
    gx = grad * gain
    first = jnp.mean(gx, -1, keepdims=True)
    second = jnp.mean(gx * xhat, -1, keepdims=True)
    return rate * (gx - first - xhat * second)


def fold8(v):
    return jnp.sum(v.reshape(v.shape[0] // 8, 8, v.shape[1]), axis=0)


def gelu_pair(h):
    e = jnp.exp2(h * h * (-0.5 * LOG2E))
    t = 1.0 / (1.0 + (0.3275911 * math.sqrt(0.5)) * jnp.abs(h))
    poly = t * (0.5 * 0.254829592 + t * (0.5 * -0.284496736 + t * (0.5 * 1.421413741 + t * (0.5 * -1.453152027 + t * (0.5 * 1.061405429)))))
    tail = poly * e
    phi = jnp.where(h < 0, tail, 1.0 - tail)
    return h * phi, phi + h * e * (1.0 / math.sqrt(2 * math.pi))


def head_masks():
    lane = lax.broadcasted_iota(jnp.int32, (128, 128), 1) // HD
    return [jnp.where(lane == h, 1.0, 0.0).astype(BF) for h in range(4)]


def head_blocks(z, masks):
    zp = jnp.concatenate([z, jnp.zeros((16, 128), BF)], 0)
    return [zp * masks[h] for h in range(4)]


def col_shift(v):
    return pltpu.roll(v, 1, 0), v, pltpu.roll(v, PAD - 1, 0)


def row_up(u, pitch):
    return jnp.concatenate([u[pitch:], jnp.zeros((pitch, 128), F32)], 0)


def row_down(u, pitch):
    return jnp.concatenate([jnp.zeros((pitch, 128), F32), u[:-pitch]], 0)


def window_sum(v, taps, pitch):
    cols = col_shift(v)
    rows = [sum(taps[3 * i + j] * cols[j] for j in range(3)) for i in range(3)]
    return row_down(rows[0], pitch) + rows[1] + row_up(rows[2], pitch)


def window_sum_back(d, taps, pitch):
    cols = col_shift(d)
    rows = [sum(taps[3 * i + j] * cols[2 - j] for j in range(3)) for i in range(3)]
    return row_up(rows[0], pitch) + rows[1] + row_down(rows[2], pitch)


def tap_sums(d, v, pitch):
    cols = col_shift(v)
    out = []
    for i in range(3):
        moved = row_up(d, pitch) if i == 0 else (d if i == 1 else row_down(d, pitch))
        for j in range(3):
            out.append(fold8(moved * cols[j]))
    return out


MT = 336
NT_TILES = 7


def compute_kernel(
    x_ref, cot_ref, w_ref, norm_ref, lepe_ref, bias_ref, into_ref, outof_ref, mask_ref, lane_ref,
    out_ref, ig_ref, grad_ref, small_ref,
    fc1_s, fc2_s, wcat_s, proj_s, lepe_s, n1_s, q_s, k_s, v_s, a_s, p_s, att_s, n2_s, act_s, gh_s, gb_s, ga_s, do_s, dqkv_s, acc_s, tacc_s, pack_s,
):
    rows = x_ref.shape[0]
    images = rows // CELLS
    chunks = images // 4

    parts, depth = w_ref.shape[0], w_ref.shape[2]
    for t in range(4):
        for n in range(parts):
            at = slice(n * depth, (n + 1) * depth)
            fc1_s[at, t * 256:(t + 1) * 256] = w_ref[n, t, :, 0:256]
            fc2_s[at, t * 256:(t + 1) * 256] = w_ref[n, t, :, 256:512]
            pack_s[0, at, t * 128:(t + 1) * 128] = w_ref[n, t, :, 512:640]
            pack_s[1, at, t * 128:(t + 1) * 128] = w_ref[n, t, :, 640:768]
    for half in range(2):
        work = dot(pack_s[half], lane_ref[...]).astype(BF)
        for b in range(2):
            if half == 0:
                wcat_s[:, b * 384:b * 384 + 256] = work[:, b * 256:b * 256 + 256]
            else:
                wcat_s[:, b * 384 + 256:b * 384 + 384] = work[:, b * 256:b * 256 + 128]
                proj_s[:, b * 128:b * 128 + 128] = work[:, b * 256 + 128:b * 256 + 256]
    lp = lepe_ref[...]
    lepe_s[0:10, :] = jnp.concatenate([lp[:, h * 64 + b * 32:h * 64 + b * 32 + 32] for b in range(2) for h in range(4)], 1)
    acc_s[...] = jnp.zeros_like(acc_s)
    tacc_s[...] = jnp.zeros_like(tacc_s)

    @pl.loop(0, NT_TILES)
    def _(i):
        sl = pl.ds(pl.multiple_of(i * MT, 16), MT)
        xhat, rate = norm_stats(x_ref[sl, :].astype(F32))
        n1_s[sl, :] = (xhat * norm_ref[0:1, :] + norm_ref[1:2, :]).astype(BF)

    @pl.loop(0, chunks)
    def _(c):
        for j in range(4):
            window = n1_s[pl.ds(pl.multiple_of(c * 784 + 192 * j, 16), 208), :]
            for b in range(2):
                spread = dot(into_ref[b * 4 + j], window).astype(BF)
                qkv = dot(spread, wcat_s[:, b * 384:(b + 1) * 384]).astype(BF)
                for s in range(2):
                    at = c * 8 + j * 2 + s
                    q_s[b, at] = qkv[s * PAD:(s + 1) * PAD, 0:128]
                    k_s[b, at] = qkv[s * PAD:(s + 1) * PAD, 128:256]
                    v_s[b, at] = qkv[s * PAD:(s + 1) * PAD, 256:384]

    masks = head_masks()

    @pl.loop(0, images * 2)
    def _(i):
        for b in range(2):
            pitch = 16 - 8 * b
            q, k, v = q_s[b, i], k_s[b, i], v_s[b, i]
            qb = head_blocks(q, masks)
            vt = jnp.transpose(v)
            ots = []
            for h in range(4):
                s = dot_nt(k, qb[h]) * (SCALE * LOG2E) + mask_ref[b]
                m = jnp.max(s, 0, keepdims=True)
                p = jnp.exp2(s - m)
                r = 1.0 / jnp.sum(p, 0, keepdims=True)
                pn = (p * r).astype(BF)
                p_s[b, i, :, h * 128:(h + 1) * 128] = pn
                ots.append(dot(vt[h * HD:(h + 1) * HD], pn))
            mixed = jnp.transpose(jnp.concatenate(ots, 0))[:PAD]
            taps = [lepe_s[n:n + 1, b * 128:(b + 1) * 128] for n in range(10)]
            local = window_sum(v.astype(F32), taps, pitch) + taps[9]
            a_s[b, i] = (mixed + local).astype(BF)

    def gather_rows(source, c, dest, lanes):
        for b in range(2):
            tail = None
            for j in range(4):
                both = jnp.concatenate([source(b, c * 8 + j * 2), source(b, c * 8 + j * 2 + 1)], 0)
                got = dot(outof_ref[b * 4 + j], both)
                head = got[0:16] if tail is None else got[0:16] + tail
                base = c * 784 + 192 * j
                cols = slice(b * lanes, (b + 1) * lanes)
                dest[pl.ds(pl.multiple_of(base, 16), 16), cols] = head.astype(BF)
                dest[pl.ds(pl.multiple_of(base + 16, 16), 176), cols] = got[16:192].astype(BF)
                tail = got[192:208]
                if j == 3:
                    dest[pl.ds(pl.multiple_of(base + 192, 16), 16), cols] = tail.astype(BF)

    @pl.loop(0, chunks)
    def _(c):
        gather_rows(lambda b, at: a_s[b, at], c, att_s, 128)

    @pl.loop(0, NT_TILES)
    def _(i):
        sl = pl.ds(pl.multiple_of(i * MT, 16), MT)
        one = dot_nt(att_s[sl, :], proj_s[...]) + norm_ref[2:3, :]
        middle = x_ref[sl, :].astype(F32) + one
        xhat, rate = norm_stats(middle)
        n2 = (xhat * norm_ref[3:4, :] + norm_ref[4:5, :]).astype(BF)
        n2_s[sl, :] = n2
        cot = cot_ref[sl, :]
        two = jnp.zeros((MT, D), F32)
        gn = jnp.zeros((MT, D), F32)
        for f in range(4):
            fs = slice(f * 256, (f + 1) * 256)
            hidden = dot(n2, fc1_s[:, fs]) + bias_ref[f:f + 1, :]
            gelu, slope = gelu_pair(hidden)
            act = gelu.astype(BF)
            act_s[sl, fs] = act
            two = two + dot_nt(act, fc2_s[:, fs])
            gh_f = dot(cot, fc2_s[:, fs]) * slope
            gh = gh_f.astype(BF)
            gh_s[sl, fs] = gh
            acc_s[10 + f] += fold8(gh.astype(F32))
            gn = gn + dot_nt(gh, fc1_s[:, fs])
        two = two + norm_ref[5:6, :]
        result = middle + two
        out_ref[sl, :] = result.astype(BF)
        acc_s[6] += fold8(one * one)
        acc_s[7] += fold8(middle * middle)
        acc_s[8] += fold8(two * two)
        acc_s[9] += fold8(result * result)
        cotf = cot.astype(F32)
        acc_s[5] += fold8(cotf)
        acc_s[3] += fold8(gn * xhat)
        acc_s[4] += fold8(gn)
        gm = cotf + norm_back(gn, norm_ref[3:4, :], xhat, rate)
        ig_ref[sl, :] = gm
        gb = gm.astype(BF)
        gb_s[sl, :] = gb
        acc_s[2] += fold8(gb.astype(F32))
        ga_s[sl, :] = dot(gb, proj_s[...]).astype(BF)

    def weight_grad(left, right):
        return lax.dot_general(left, right, (((0,), (0,)), ((), ())), preferred_element_type=F32)

    def put_rows(value, t, off):
        for n in range(parts):
            grad_ref[n, t, :, off:off + value.shape[1]] = value[n * depth:(n + 1) * depth]

    def put_mlp(left, right, off):
        for t in range(4):
            value = weight_grad(left[...], right[:, t * 256:(t + 1) * 256]).astype(BF)
            put_rows(value, t, off)

    put_mlp(n2_s, gh_s, 0)
    put_mlp(cot_ref, act_s, 256)

    @pl.loop(0, chunks)
    def _(c):
        for j in range(4):
            window = ga_s[pl.ds(pl.multiple_of(c * 784 + 192 * j, 16), 208), :]
            for b in range(2):
                spread = dot(into_ref[b * 4 + j], window[:, b * 128:(b + 1) * 128]).astype(BF)
                for s in range(2):
                    do_s[b, c * 8 + j * 2 + s] = spread[s * PAD:(s + 1) * PAD]

    @pl.loop(0, images * 2)
    def _(i):
        for b in range(2):
            pitch = 16 - 8 * b
            q, k, v, do = q_s[b, i], k_s[b, i], v_s[b, i], do_s[b, i]
            qb = head_blocks(q, masks)
            db = head_blocks(do, masks)
            kt = jnp.transpose(k)
            dqt = []
            dk = jnp.zeros((PAD, 128), F32)
            dv = jnp.zeros((PAD, 128), F32)
            for h in range(4):
                pn = p_s[b, i, :, h * 128:(h + 1) * 128]
                pf = pn.astype(F32)
                t = pf * dot_nt(v, db[h])
                ds = (t - pf * jnp.sum(t, 0, keepdims=True)).astype(BF)
                dv = dv + dot(pn, db[h])
                dk = dk + dot(ds, qb[h])
                dqt.append(dot(kt[h * HD:(h + 1) * HD], ds))
            dq = jnp.transpose(jnp.concatenate(dqt, 0))[:PAD]
            taps = [lepe_s[n:n + 1, b * 128:(b + 1) * 128] for n in range(10)]
            dof, vf = do.astype(F32), v.astype(F32)
            dv = dv + window_sum_back(dof, taps, pitch)
            for n, part in enumerate(tap_sums(dof, vf, pitch)):
                tacc_s[b, n] += part
            tacc_s[b, 9] += fold8(dof)
            q_s[b, i] = (dq * SCALE).astype(BF)
            k_s[b, i] = (dk * SCALE).astype(BF)
            v_s[b, i] = dv.astype(BF)

    @pl.loop(0, chunks)
    def _(c):
        gather_rows(lambda b, at: jnp.concatenate([q_s[b, at], k_s[b, at], v_s[b, at]], 1), c, dqkv_s, 384)

    @pl.loop(0, NT_TILES)
    def _(i):
        sl = pl.ds(pl.multiple_of(i * MT, 16), MT)
        gn = dot_nt(dqkv_s[sl, :], wcat_s[...])
        xhat, rate = norm_stats(x_ref[sl, :].astype(F32))
        acc_s[0] += fold8(gn * xhat)
        acc_s[1] += fold8(gn)
        ig_ref[sl, :] = ig_ref[sl, :] + norm_back(gn, norm_ref[0:1, :], xhat, rate)

    gw = weight_grad(n1_s[...], dqkv_s[...]).astype(BF)
    gp = weight_grad(gb_s[...], att_s[...]).astype(BF)
    work0 = jnp.concatenate([gw[:, 0:256], gw[:, 384:640]], 1)
    work1 = jnp.concatenate([gw[:, 256:384], gp[:, 0:128], gw[:, 640:768], gp[:, 128:256]], 1)
    for half, work in enumerate((work0, work1)):
        packed = dot_nt(work, lane_ref[...]).astype(BF)
        for t in range(4):
            put_rows(packed[:, t * 128:(t + 1) * 128], t, 512 + 128 * half)
    for n in range(14):
        small_ref[n:n + 1, :] = jnp.sum(acc_s[n], 0, keepdims=True)
    for n in range(10):
        row = jnp.concatenate([jnp.sum(tacc_s[b, n], 0, keepdims=True) for b in range(2)], 1)
        small_ref[14 + n:15 + n, :] = jnp.concatenate([row[:, b * 128 + h * 32:b * 128 + h * 32 + 32] for h in range(4) for b in range(2)], 1)


def compute_call(x, cot, w, norm, lepe, bias):
    rows = x.shape[0]
    n = rows // CELLS * 2
    into, outof = spread_tables()
    args = (x, cot, w, norm, lepe, bias.reshape(4, 256), jnp.asarray(into, BF), jnp.asarray(outof, BF), jnp.asarray(key_mask()), jnp.asarray(lane_table(4), BF))
    V = pltpu.VMEM
    return pl.pallas_call(
        compute_kernel,
        out_shape=(
            jax.ShapeDtypeStruct((rows, D), BF),
            jax.ShapeDtypeStruct((rows, D), F32),
            jax.ShapeDtypeStruct(w.shape, BF),
            jax.ShapeDtypeStruct((24, D), F32),
        ),
        in_specs=[pl.BlockSpec(memory_space=V)] * len(args),
        out_specs=tuple([pl.BlockSpec(memory_space=V)] * 4),
        scratch_shapes=[
            V((D, FF), BF), V((D, FF), BF), V((D, 768), BF), V((D, D), BF), V((16, D), F32),
            V((rows, D), BF),
            V((2, n, PAD, 128), BF), V((2, n, PAD, 128), BF), V((2, n, PAD, 128), BF), V((2, n, PAD, 128), BF),
            V((2, n, PAD, 512), BF),
            V((rows, D), BF), V((rows, D), BF), V((rows, FF), BF), V((rows, FF), BF), V((rows, D), BF), V((rows, D), BF),
            V((2, n, PAD, 128), BF), V((rows, 768), BF),
            V((14, 8, D), F32), V((2, 10, 8, 128), F32), V((2, D, 512), BF),
        ],
        compiler_params=pltpu.CompilerParams(vmem_limit_bytes=60 * 2**20),
    )(*args)


MESH = pl.DeviceIdType.MESH


def ring_peers(batch, tensor):
    me_b, me_t = lax.axis_index("batch"), lax.axis_index("tensor")
    along_b = [(lax.rem(me_b + k, batch), me_t) for k in range(1, batch)]
    along_t = [(me_b, lax.rem(me_t + k, tensor)) for k in range(1, tensor)]
    return me_b, me_t, along_b, along_t


def greet(peers):
    barrier = pltpu.get_barrier_semaphore()
    for peer in peers:
        pl.semaphore_signal(barrier, inc=1, device_id=peer, device_id_type=MESH)
    pl.semaphore_wait(barrier, len(peers))


def gather_kernel(batch, tensor, qkv_ref, proj_ref, fc1_ref, fc2_ref, full_ref, own_s, keep_sem, send_t, recv_t, send_b, recv_b):
    me_b, me_t, along_b, along_t = ring_peers(batch, tensor)
    own_s[:, 0:256] = fc1_ref[...].astype(BF)
    own_s[:, 256:512] = jnp.transpose(fc2_ref[...]).astype(BF)
    own_s[:, 512:640] = jnp.concatenate([qkv_ref[0], qkv_ref[1]], 1).astype(BF)
    own_s[:, 640:768] = jnp.concatenate([qkv_ref[2], jnp.transpose(proj_ref[...])], 1).astype(BF)
    greet(along_b + along_t)
    mine = full_ref.at[me_b, me_t]
    keep = pltpu.make_async_copy(own_s, mine, keep_sem)
    keep.start()
    across = []
    for k, peer in enumerate(along_t):
        copy = pltpu.make_async_remote_copy(src_ref=own_s, dst_ref=mine, send_sem=send_t.at[k], recv_sem=recv_t.at[k], device_id=peer, device_id_type=MESH)
        copy.start()
        across.append(copy)
    passed = []
    for n in range(tensor):
        if n == 0:
            source, slot = own_s, me_t
        else:
            across[n - 1].wait_recv()
            slot = lax.rem(me_t + tensor - n, tensor)
            source = full_ref.at[me_b, slot]
        for k, peer in enumerate(along_b):
            copy = pltpu.make_async_remote_copy(src_ref=source, dst_ref=full_ref.at[me_b, slot], send_sem=send_b.at[n, k], recv_sem=recv_b.at[n, k], device_id=peer, device_id_type=MESH)
            copy.start()
            passed.append(copy)
    keep.wait()
    for copy in across:
        copy.wait_send()
    for copy in passed:
        copy.wait()


def gather_call(batch, tensor, qkv, proj, fc1, fc2):
    rows = fc1.shape[0]
    V = pltpu.VMEM
    dma = pltpu.SemaphoreType.DMA
    return pl.pallas_call(
        functools.partial(gather_kernel, batch, tensor),
        out_shape=jax.ShapeDtypeStruct((batch, tensor, rows, 768), BF),
        in_specs=[pl.BlockSpec(memory_space=V)] * 4,
        out_specs=pl.BlockSpec(memory_space=V),
        scratch_shapes=[V((rows, 768), BF), dma, dma((tensor - 1,)), dma((tensor - 1,)), dma((tensor, batch - 1)), dma((tensor, batch - 1))],
        compiler_params=pltpu.CompilerParams(collective_id=0, has_side_effects=True, vmem_limit_bytes=32 * 2**20),
    )(qkv, proj, fc1, fc2)


def reduce_kernel(
    batch, tensor, grad_ref, small_ref, shard_ref, total_ref, norm_ref,
    in_b, mid_s, in_t, small_b, small_t, square_b, square_t,
    send_b, recv_b, send_t, recv_t, send_sb, recv_sb, send_st, recv_st, send_qb, recv_qb, send_qt, recv_qt,
):
    me_b, me_t, along_b, along_t = ring_peers(batch, tensor)
    greet(along_b + along_t)

    def push(source, dest, peer, send_sem, recv_sem):
        copy = pltpu.make_async_remote_copy(src_ref=source, dst_ref=dest, send_sem=send_sem, recv_sem=recv_sem, device_id=peer, device_id_type=MESH)
        copy.start()
        return copy

    first = [push(grad_ref.at[peer[0]], in_b.at[k], peer, send_b.at[k], recv_b.at[k]) for k, peer in enumerate(along_b)]
    small_b[me_b] = small_ref[...]
    small_first = [push(small_ref, small_b.at[me_b], peer, send_sb.at[k], recv_sb.at[k]) for k, peer in enumerate(along_b)]
    for copy in small_first:
        copy.wait()
    part = small_b[0]
    for n in range(1, batch):
        part = part + small_b[n]
    total_ref[...] = part
    small_t[me_t] = part
    small_second = [push(total_ref, small_t.at[me_t], peer, send_st.at[k], recv_st.at[k]) for k, peer in enumerate(along_t)]
    for copy in first:
        copy.wait()

    for n in range(tensor):
        value = grad_ref[me_b, n].astype(F32)
        for k in range(batch - 1):
            value = value + in_b[k, n].astype(F32)
        mid_s[n] = value.astype(mid_s.dtype)

    second = [push(mid_s.at[peer[1]], in_t.at[k], peer, send_t.at[k], recv_t.at[k]) for k, peer in enumerate(along_t)]
    for copy in small_second:
        copy.wait()
    part = small_t[0]
    for n in range(1, tensor):
        part = part + small_t[n]
    total_ref[...] = part
    for copy in second:
        copy.wait()
    shard = mid_s[me_t].astype(F32)
    for k in range(tensor - 1):
        shard = shard + in_t[k].astype(F32)
    shard_ref[...] = shard
    squares = fold8(shard * shard)
    lanes = squares[:, 0:128]
    for n in range(1, 6):
        lanes = lanes + squares[:, n * 128:(n + 1) * 128]
    square_b[me_b] = lanes
    norm_ref[...] = lanes
    last = [push(norm_ref, square_b.at[me_b], peer, send_qb.at[k], recv_qb.at[k]) for k, peer in enumerate(along_b)]
    for copy in last:
        copy.wait()
    lanes = square_b[0]
    for n in range(1, batch):
        lanes = lanes + square_b[n]
    square_t[me_t] = lanes
    norm_ref[...] = lanes
    last = [push(norm_ref, square_t.at[me_t], peer, send_qt.at[k], recv_qt.at[k]) for k, peer in enumerate(along_t)]
    for copy in last:
        copy.wait()
    lanes = square_t[0]
    for n in range(1, tensor):
        lanes = lanes + square_t[n]
    matrix = jnp.sum(jnp.sum(lanes, 0, keepdims=True), 1, keepdims=True)
    vectors = total_ref[...]
    row = lax.broadcasted_iota(jnp.int32, vectors.shape, 0)
    vectors = jnp.where((row < 6) | (row >= 10), vectors, 0.0)
    vector = jnp.sum(jnp.sum(vectors * vectors, 0, keepdims=True), 1, keepdims=True)
    norm_ref[...] = jnp.broadcast_to(jnp.sqrt(matrix + vector), (8, 128))


def reduce_call(batch, tensor, grad, small, mid=BF):
    rows = grad.shape[2]
    V = pltpu.VMEM
    dma = pltpu.SemaphoreType.DMA
    pair = lambda n: [dma((n - 1,)), dma((n - 1,))]
    return pl.pallas_call(
        functools.partial(reduce_kernel, batch, tensor),
        out_shape=(jax.ShapeDtypeStruct((rows, 768), F32), jax.ShapeDtypeStruct((24, 256), F32), jax.ShapeDtypeStruct((8, 128), F32)),
        in_specs=[pl.BlockSpec(memory_space=V)] * 2,
        out_specs=tuple([pl.BlockSpec(memory_space=V)] * 3),
        scratch_shapes=[
            V((batch - 1, tensor, rows, 768), BF), V((tensor, rows, 768), mid), V((tensor - 1, rows, 768), mid),
            V((batch, 24, 256), F32), V((tensor, 24, 256), F32), V((batch, 8, 128), F32), V((tensor, 8, 128), F32),
        ] + pair(batch) + pair(tensor) + pair(batch) + pair(tensor) + pair(batch) + pair(tensor),
        compiler_params=pltpu.CompilerParams(collective_id=1, has_side_effects=True, vmem_limit_bytes=32 * 2**20),
    )(grad, small)


def adam(master, first, second, clipped, rate, decay):
    first = BETA_ONE * first + (1.0 - BETA_ONE) * clipped
    second = BETA_TWO * second + (1.0 - BETA_TWO) * clipped * clipped
    hat = first * (1.0 / (1.0 - BETA_ONE**STEP))
    spread = second * (1.0 / (1.0 - BETA_TWO**STEP))
    return master - rate * (hat / (jnp.sqrt(spread) + ADAM_EPS) + decay * master), first, second


def update_kernel(
    all_tokens, shard_ref, total_ref, norm_ref,
    qkv_w, qkv_m, proj_w, proj_m, fc1_w, fc1_m, fc2_w, fc2_m, norm_w, norm_m, lepe_w, lepe_m, bias_w, bias_m,
    qkv_g, qkv_n, qkv_l, qkv_o, proj_g, proj_n, proj_l, proj_o, fc1_g, fc1_n, fc1_l, fc1_o, fc2_g, fc2_n, fc2_l, fc2_o,
    norm_g, norm_n, norm_o, lepe_g, lepe_n, lepe_o, bias_g, bias_n, bias_o, size_o, rms_o,
):
    size = norm_ref[0:1, 0:1]
    factor = jnp.minimum(1.0, CLIP_SCALE * math.sqrt(NPARAM) / (size + 1e-06))
    size_o[...] = size

    def one(grad, w, m, g_o, n_o, l_o, m_o, at, rate, decay):
        clipped = grad * factor
        new, first, second = adam(w[at], m[(0,) + at], m[(1,) + at], clipped, rate, decay)
        g_o[at] = clipped
        n_o[at] = new
        if l_o is not None:
            l_o[at] = new.astype(BF)
        m_o[(0,) + at] = first
        m_o[(1,) + at] = second

    every = (slice(None), slice(None))
    one(shard_ref[:, 0:256], fc1_w, fc1_m, fc1_g, fc1_n, fc1_l, fc1_o, every, RATE_MATRIX, DECAY_RATE)
    one(jnp.transpose(shard_ref[:, 256:512]), fc2_w, fc2_m, fc2_g, fc2_n, fc2_l, fc2_o, every, RATE_MATRIX, DECAY_RATE)
    for j in range(3):
        one(shard_ref[:, 512 + 64 * j:576 + 64 * j], qkv_w, qkv_m, qkv_g, qkv_n, qkv_l, qkv_o, (j,) + every, RATE_MATRIX, DECAY_RATE)
    one(jnp.transpose(shard_ref[:, 704:768]), proj_w, proj_m, proj_g, proj_n, proj_l, proj_o, every, RATE_MATRIX, DECAY_RATE)
    one(total_ref[0:6], norm_w, norm_m, norm_g, norm_n, None, norm_o, every, RATE_VECTOR, 0.0)
    one(total_ref[14:24], lepe_w, lepe_m, lepe_g, lepe_n, None, lepe_o, every, RATE_VECTOR, 0.0)
    one(total_ref[10:14], bias_w, bias_m, bias_g, bias_n, None, bias_o, every, RATE_VECTOR, 0.0)
    sums = jnp.sum(total_ref[6:10], 1, keepdims=True)
    rms_o[...] = jnp.sqrt(sums * (1.0 / (all_tokens * D)))


def update_call(all_tokens, shard, total, norm, arrays):
    arrays = list(arrays)
    arrays[12], arrays[13] = arrays[12].reshape(4, 256), arrays[13].reshape(2, 4, 256)
    V = pltpu.VMEM
    like = lambda a, dt=F32: jax.ShapeDtypeStruct(a.shape, dt)
    outs = []
    for n in range(4):
        w, m = arrays[2 * n], arrays[2 * n + 1]
        outs += [like(w), like(w), like(w, BF), like(m)]
    for n in range(4, 7):
        w, m = arrays[2 * n], arrays[2 * n + 1]
        outs += [like(w), like(w), like(m)]
    outs += [jax.ShapeDtypeStruct((1, 1), F32), jax.ShapeDtypeStruct((4, 1), F32)]
    got = list(pl.pallas_call(
        functools.partial(update_kernel, all_tokens),
        out_shape=tuple(outs),
        in_specs=[pl.BlockSpec(memory_space=V)] * (3 + len(arrays)),
        out_specs=tuple([pl.BlockSpec(memory_space=V)] * len(outs)),
    )(shard, total, norm, *arrays))
    got[22], got[23], got[24] = got[22].reshape(1024), got[23].reshape(1024), got[24].reshape(2, 1024)
    got[25], got[26] = got[25].reshape(()), got[26].reshape(4)
    return got


def shards(block_input, cotangent, *arrays):
    batch, tensor = lax.axis_size("batch"), lax.axis_size("tensor")
    qkv, _, proj, _, fc1, _, fc2, _, norm, _, lepe, _, bias, _ = arrays
    full = gather_call(batch, tensor, qkv, proj, fc1, fc2)
    output, input_grad, grads, small = compute_call(block_input, cotangent, full, norm, lepe, bias)
    shard, total, size = reduce_call(batch, tensor, grads, small)
    rest = update_call(block_input.shape[0] * batch * tensor, shard, total, size, arrays)
    return (output, input_grad, *rest)


def solution(mesh):
    token, matrix, moment = P(("batch", "tensor"), None), P("batch", "tensor"), P(None, "batch", "tensor")
    back, back_moment = P("tensor", "batch"), P(None, "tensor", "batch")
    stack, stack_moment = P(None, "batch", "tensor"), P(None, None, "batch", "tensor")
    return jax.shard_map(
        shards,
        mesh=mesh,
        in_specs=(token, token, stack, stack_moment, back, back_moment, matrix, moment, back, back_moment) + (P(),) * 6,
        out_specs=(token, token) + (stack,) * 3 + (stack_moment,) + (back,) * 3 + (back_moment,) + (matrix,) * 3 + (moment,) + (back,) * 3 + (back_moment,) + (P(),) * 11,
        check_vma=False,
    )
```

time: 1010 us -> 217 us (0.21)
  local copies, waits for them, and re-layouts: 343 us -> 31.1 us
  waiting for transfers between devices: 205 us -> 0 us
  other arithmetic: 188 us -> 1.29 us
  Pallas kernels: 0 us -> 182 us
  blocking collectives: 139 us -> 0 us
  matrix products: 103 us -> 0 us
  between operations: 23.6 us -> 0.77 us
    pallas_call x0 -> x4, Pallas kernels: none -> 182 us  [the longest x1 117 us: compute_call(): pl.pallas_call(compute_kernel, out_shape=(jax.ShapeDtypeStruct((rows, D),...]
    another operation x25 -> x0, local copies, waits for them, and re-layouts: 140 us -> none  [the longest x4 49.1 us: join_heads(): return jnp.stack(merged, -2).reshape(images * GRID * GRID, channels)]
    unnamed x11 -> x0, waiting for transfers between devices: 120 us -> none
    dot_general x26 -> x0, matrix products: 103 us -> none  [the longest x1 24.9 us: shards(): jnp.dot(normed_two, fc1_full, preferred_element_type=jnp.float32) + fc1_bias]
    all_gather x8 -> x0, blocking collectives: 99.3 us -> none  [the longest x1 16.6 us: shards(): lax.all_gather(fc1_full, 'tensor', axis=1, tiled=True)]
    reduce_scatter x5 -> x0, waiting for transfers between devices: 84.7 us -> none  [the longest x1 35.2 us: shards(): lax.psum_scatter(grad_fc1, 'batch', scatter_dimension=0, tiled=True)]
    reduce_sum x20 -> x0, other arithmetic: 66.8 us -> none  [the longest x4 44.5 us: position_term(): padded[:, offset // 3:offset // 3 + height, offset % 3:offset % 3 + across]]
    reshape x11 -> x2, local copies, waits for them, and re-layouts: 51.3 us -> 1.21 us  [the longest x1 0.61 us: update_call(): arrays[13].reshape(2, 4, 256)]
  transfers between devices with their start and end apart: 8 -> 0, of which waited for: 7 -> 0; matrix products, arithmetic and copies ran while one was open for 34% -> 0% of each run, Pallas kernels for 0% -> 0%
where the time goes in v1:
time: 217 us; the launch traced here: 215 us
  Pallas kernels  182 us (84%)
  local copies, waits for them, and re-layouts  31.1 us (14%)
    pallas_call x1, Pallas kernels, compute_call(): pl.pallas_call(compute_kernel, out_shape=(jax.ShapeDtypeStruct((rows, D),...  117 us
    pallas_call x1, Pallas kernels, reduce_call(): pl.pallas_call(functools.partial(reduce_kernel, batch, tensor), out_shape...  39 us
    unnamed x51, local copies, waits for them, and re-layouts  29.9 us
    pallas_call x1, Pallas kernels, gather_call(): pl.pallas_call(functools.partial(gather_kernel, batch, tensor), out_shape...  24.1 us

profile of v1, /device:TPU:0, one launch (start us, length us, event | category | flops | bytes accessed | tf_op | source)
XLA Modules:
  0.0 215.5 jit_solution(6030832556599275263)
XLA Ops:
  0.7 0.0 copy-start.15
  0.7 0.9 copy.68.fc2_ref.fc2_w
  1.5 0.0 copy-start.2
  1.5 0.8 copy.67.proj_ref.proj_w
  2.4 0.8 copy-done.4
  3.2 0.8 copy-done.5
  3.9 24.1 %shard_map.419.w_ref = bf16[8,4,32,768]{3,2,1,0:T(8,128)(2,1)S(1)} custom-call(f32[3,32,64]{2,1,0:T(8,128)S(1)} %copy-done.4, f32[64,32]{1,0:T(8,128)S(1)} %copy.67.proj_ref.proj_w, f32[32,256]{1,0:T(8,128)S(1)} %copy-done.5, f32[256,32]{1,0:T(8,128)S(1)} %copy.68.fc2_ref.fc2_w), custom_call_target="tpu_custom_call" | custom-call | tf_op jit(solution)/shard_map/pallas_call | solution.py:453
  28.0 0.0 copy-start
  28.0 1.2 copy-done
  29.2 0.0 copy-done.15
  29.2 0.6 reshape.80.bias_ref.bias_w
  29.8 0.0 copy-start.14
  29.8 116.7 %shard_map.420 = (bf16[2352,256]{1,0:T(8,128)(2,1)}, f32[2352,256]{1,0:T(8,128)}, bf16[8,4,32,768]{3,2,1,0:T(8,128)(2,1)}, f32[24,256]{1,0:T(8,128)}) custom-call(bf16[2352,256]{1,0:T(8,128)(2,1)} %x_ref.1, bf16[2352,256]{1,0:T(8,128)(2,1)} %cot_ref.1, bf16[8,4,32,768]{3,2,1,0:T(8,128)(2,1)} %copy-done, f32[6,256]{1,0:T(8,128)} %norm_w.1, f32[10,256]{1,0:T(8,128)} %lepe_w.1, ...), custom_call_target="tpu_custom_call" | custom-call | tf_op jit(solution)/shard_map/pallas_call | solution.py:375
  146.5 0.0 copy-done.2
  146.5 0.0 copy-done.3
  146.6 0.0 copy-start.1
  146.6 1.4 copy-done.1
  148.0 0.7 copy-done.7
  148.7 39.0 %shard_map.421 = (f32[32,768]{1,0:T(8,128)S(1)}, f32[24,256]{1,0:T(8,128)S(1)}, f32[8,128]{1,0:T(8,128)S(1)}) custom-call(bf16[8,4,32,768]{3,2,1,0:T(8,128)(2,1)S(1)} %copy-done.1, f32[24,256]{1,0:T(8,128)S(1)} %copy-done.7), custom_call_target="tpu_custom_call" | custom-call | tf_op jit(solution)/shard_map/pallas_call | solution.py:542
  187.7 0.0 copy-start.6
  187.7 0.6 copy-done.6
  188.3 0.6 copy-done.8
  188.9 0.6 copy-done.9
  189.5 0.0 copy-done.10
  189.5 0.8 copy.72.fc2_m
  190.3 0.0 copy-done.11
  190.3 0.7 copy.70.proj_m
  191.0 0.0 copy-done.12
  191.0 0.6 copy.74.lepe_m
  191.7 0.0 copy-done.13
  191.7 0.6 copy.73.norm_m
  192.3 0.0 copy-done.14
  192.3 0.6 reshape.81.bias_m
  192.9 2.5 %shard_map.422 = (f32[3,32,64]{2,1,0:T(8,128)}, f32[3,32,64]{2,1,0:T(8,128)}, bf16[3,32,64]{2,1,0:T(8,128)(2,1)}, f32[2,3,32,64]{3,2,1,0:T(8,128)}, f32[64,32]{1...) custom-call(f32[32,768]{1,0:T(8,128)} %copy-done.6, ...), custom_call_target="tpu_custom_call" | custom-call | tf_op jit(solution)/shard_map/pallas_call | solution.py:609
  195.4 1.7 copy.82
  197.1 1.5 copy.78
  198.7 1.6 copy.79
  200.2 1.6 copy.80
  201.8 1.4 copy.84
  203.2 1.4 copy.75
  204.7 1.4 copy.76
  206.1 1.5 copy.81
  207.6 1.3 copy.83
  208.9 1.3 copy.87
  210.2 1.4 copy.77
  211.6 1.3 copy.85
  212.9 1.3 copy.86
  214.2 1.3 reduce
  (10 shorter events, 0.0 us)
Async XLA Ops:
  0.7 28.5 %copy-start.15 = (f32[1024]{0:T(1024)S(1)}, f32[1024]{0:T(1024)}, u32[]{:S(2)}) copy-start(f32[1024]{0:T(1024)} %param.34) | copy-start | bytes 12292
  1.5 145.0 %copy-start.2 = (f32[256,32]{1,0:T(8,128)}, f32[256,32]{1,0:T(8,128)S(1)}, u32[]{:S(2)}) copy-start(f32[256,32]{1,0:T(8,128)S(1)} %copy.68.fc2_ref.fc2_w) | copy-start | bytes 98308
  2.4 0.8 copy-start.4
  3.2 0.8 copy-start.5
  3.9 142.6 %copy-start.3 = (f32[64,32]{1,0:T(8,128)}, f32[64,32]{1,0:T(8,128)S(1)}, u32[]{:S(2)}) copy-start(f32[64,32]{1,0:T(8,128)S(1)} %copy.67.proj_ref.proj_w) | copy-start | bytes 24580
  28.0 1.2 copy-start
  29.8 159.7 %copy-start.10 = (f32[2,256,32]{1,2,0:T(8,128)S(1)}, f32[2,256,32]{1,2,0:T(8,128)}, u32[]{:S(2)}) copy-start(f32[2,256,32]{1,2,0:T(8,128)} %param.29) | copy-start | bytes 196612
  29.8 160.5 %copy-start.11 = (f32[2,64,32]{1,2,0:T(8,128)S(1)}, f32[2,64,32]{1,2,0:T(8,128)}, u32[]{:S(2)}) copy-start(f32[2,64,32]{1,2,0:T(8,128)} %param.25) | copy-start | bytes 49156
  29.8 161.2 %copy-start.12 = (f32[2,10,256]{2,0,1:T(2,128)S(1)}, f32[2,10,256]{2,0,1:T(2,128)}, u32[]{:S(2)}) copy-start(f32[2,10,256]{2,0,1:T(2,128)} %param.33) | copy-start | bytes 61444
  29.8 161.9 %copy-start.13 = (f32[2,6,256]{2,0,1:T(2,128)S(1)}, f32[2,6,256]{2,0,1:T(2,128)}, u32[]{:S(2)}) copy-start(f32[2,6,256]{2,0,1:T(2,128)} %param.31) | copy-start | bytes 36868
  29.8 162.5 %copy-start.14 = (f32[2,1024]{1,0:T(2,128)S(1)}, f32[2,1024]{1,0:T(2,128)}, u32[]{:S(2)}) copy-start(f32[2,1024]{1,0:T(2,128)} %param.35) | copy-start | bytes 24580
  146.6 1.4 copy-start.1
  148.0 0.7 copy-start.7
  187.7 0.6 copy-start.6
  188.3 0.6 copy-start.8
  188.9 0.6 copy-start.9

commit v2 on v1

--- a/solution.py
+++ b/solution.py
@@ -256,7 +256,7 @@
         gn = jnp.zeros((MT, D), F32)
         for f in range(4):
             fs = slice(f * 256, (f + 1) * 256)
-            hidden = dot(n2, fc1_s[:, fs]) + bias_ref[f:f + 1, :]
+            hidden = dot(n2, fc1_s[:, fs]) + jnp.concatenate([bias_ref[2 * f:2 * f + 1, :], bias_ref[2 * f + 1:2 * f + 2, :]], 1)
             gelu, slope = gelu_pair(hidden)
             act = gelu.astype(BF)
             act_s[sl, fs] = act
@@ -370,7 +370,7 @@
     rows = x.shape[0]
     n = rows // CELLS * 2
     into, outof = spread_tables()
-    args = (x, cot, w, norm, lepe, bias.reshape(4, 256), jnp.asarray(into, BF), jnp.asarray(outof, BF), jnp.asarray(key_mask()), jnp.asarray(lane_table(4), BF))
+    args = (x, cot, w, norm, lepe, bias, jnp.asarray(into, BF), jnp.asarray(outof, BF), jnp.asarray(key_mask()), jnp.asarray(lane_table(4), BF))
     V = pltpu.VMEM
     return pl.pallas_call(
         compute_kernel,
@@ -415,9 +415,9 @@
 def gather_kernel(batch, tensor, qkv_ref, proj_ref, fc1_ref, fc2_ref, full_ref, own_s, keep_sem, send_t, recv_t, send_b, recv_b):
     me_b, me_t, along_b, along_t = ring_peers(batch, tensor)
     own_s[:, 0:256] = fc1_ref[...].astype(BF)
-    own_s[:, 256:512] = jnp.transpose(fc2_ref[...]).astype(BF)
+    own_s[:, 256:512] = fc2_ref[...].astype(BF)
     own_s[:, 512:640] = jnp.concatenate([qkv_ref[0], qkv_ref[1]], 1).astype(BF)
-    own_s[:, 640:768] = jnp.concatenate([qkv_ref[2], jnp.transpose(proj_ref[...])], 1).astype(BF)
+    own_s[:, 640:768] = jnp.concatenate([qkv_ref[2], proj_ref[...]], 1).astype(BF)
     greet(along_b + along_t)
     mine = full_ref.at[me_b, me_t]
     keep = pltpu.make_async_copy(own_s, mine, keep_sem)
@@ -456,7 +456,7 @@
         in_specs=[pl.BlockSpec(memory_space=V)] * 4,
         out_specs=pl.BlockSpec(memory_space=V),
         scratch_shapes=[V((rows, 768), BF), dma, dma((tensor - 1,)), dma((tensor - 1,)), dma((tensor, batch - 1)), dma((tensor, batch - 1))],
-        compiler_params=pltpu.CompilerParams(collective_id=0, has_side_effects=True, vmem_limit_bytes=32 * 2**20),
+        compiler_params=pltpu.CompilerParams(collective_id=0, has_side_effects=True, vmem_limit_bytes=60 * 2**20),
     )(qkv, proj, fc1, fc2)
 
 
@@ -548,7 +548,7 @@
             V((batch - 1, tensor, rows, 768), BF), V((tensor, rows, 768), mid), V((tensor - 1, rows, 768), mid),
             V((batch, 24, 256), F32), V((tensor, 24, 256), F32), V((batch, 8, 128), F32), V((tensor, 8, 128), F32),
         ] + pair(batch) + pair(tensor) + pair(batch) + pair(tensor) + pair(batch) + pair(tensor),
-        compiler_params=pltpu.CompilerParams(collective_id=1, has_side_effects=True, vmem_limit_bytes=32 * 2**20),
+        compiler_params=pltpu.CompilerParams(collective_id=1, has_side_effects=True, vmem_limit_bytes=60 * 2**20),
     )(grad, small)
 
 
@@ -570,32 +570,37 @@
     factor = jnp.minimum(1.0, CLIP_SCALE * math.sqrt(NPARAM) / (size + 1e-06))
     size_o[...] = size
 
-    def one(grad, w, m, g_o, n_o, l_o, m_o, at, rate, decay):
+    def one(grad, w, m, g_o, n_o, l_o, m_o, at, rate, decay, pair=lambda n, at: (n,) + at):
         clipped = grad * factor
-        new, first, second = adam(w[at], m[(0,) + at], m[(1,) + at], clipped, rate, decay)
+        new, first, second = adam(w[at], m[pair(0, at)], m[pair(1, at)], clipped, rate, decay)
         g_o[at] = clipped
         n_o[at] = new
         if l_o is not None:
             l_o[at] = new.astype(BF)
-        m_o[(0,) + at] = first
-        m_o[(1,) + at] = second
+        m_o[pair(0, at)] = first
+        m_o[pair(1, at)] = second
 
     every = (slice(None), slice(None))
+    middle = lambda n, at: (at[0], n, at[1])
     one(shard_ref[:, 0:256], fc1_w, fc1_m, fc1_g, fc1_n, fc1_l, fc1_o, every, RATE_MATRIX, DECAY_RATE)
-    one(jnp.transpose(shard_ref[:, 256:512]), fc2_w, fc2_m, fc2_g, fc2_n, fc2_l, fc2_o, every, RATE_MATRIX, DECAY_RATE)
+    one(shard_ref[:, 256:512], fc2_w, fc2_m, fc2_g, fc2_n, fc2_l, fc2_o, every, RATE_MATRIX, DECAY_RATE)
     for j in range(3):
         one(shard_ref[:, 512 + 64 * j:576 + 64 * j], qkv_w, qkv_m, qkv_g, qkv_n, qkv_l, qkv_o, (j,) + every, RATE_MATRIX, DECAY_RATE)
-    one(jnp.transpose(shard_ref[:, 704:768]), proj_w, proj_m, proj_g, proj_n, proj_l, proj_o, every, RATE_MATRIX, DECAY_RATE)
-    one(total_ref[0:6], norm_w, norm_m, norm_g, norm_n, None, norm_o, every, RATE_VECTOR, 0.0)
-    one(total_ref[14:24], lepe_w, lepe_m, lepe_g, lepe_n, None, lepe_o, every, RATE_VECTOR, 0.0)
-    one(total_ref[10:14], bias_w, bias_m, bias_g, bias_n, None, bias_o, every, RATE_VECTOR, 0.0)
-    sums = jnp.sum(total_ref[6:10], 1, keepdims=True)
+    one(shard_ref[:, 704:768], proj_w, proj_m, proj_g, proj_n, proj_l, proj_o, every, RATE_MATRIX, DECAY_RATE)
+    one(total_ref[0:6], norm_w, norm_m, norm_g, norm_n, None, norm_o, every, RATE_VECTOR, 0.0, middle)
+    one(total_ref[14:24], lepe_w, lepe_m, lepe_g, lepe_n, None, lepe_o, every, RATE_VECTOR, 0.0, middle)
+    for f in range(8):
+        at = (slice(f, f + 1), slice(None))
+        part = total_ref[10 + f // 2:11 + f // 2, 128 * (f % 2):128 * (f % 2) + 128]
+        one(part, bias_w, bias_m, bias_g, bias_n, None, bias_o, at, RATE_VECTOR, 0.0, middle)
+    lane = lax.broadcasted_iota(jnp.int32, (1, 4), 1)
+    sums = jnp.zeros((1, 4), F32)
+    for n in range(4):
+        sums = jnp.where(lane == n, jnp.sum(total_ref[6 + n:7 + n], 1, keepdims=True), sums)
     rms_o[...] = jnp.sqrt(sums * (1.0 / (all_tokens * D)))
 
 
 def update_call(all_tokens, shard, total, norm, arrays):
-    arrays = list(arrays)
-    arrays[12], arrays[13] = arrays[12].reshape(4, 256), arrays[13].reshape(2, 4, 256)
     V = pltpu.VMEM
     like = lambda a, dt=F32: jax.ShapeDtypeStruct(a.shape, dt)
     outs = []
@@ -605,26 +610,38 @@
     for n in range(4, 7):
         w, m = arrays[2 * n], arrays[2 * n + 1]
         outs += [like(w), like(w), like(m)]
-    outs += [jax.ShapeDtypeStruct((1, 1), F32), jax.ShapeDtypeStruct((4, 1), F32)]
-    got = list(pl.pallas_call(
+    outs += [jax.ShapeDtypeStruct((1, 1), F32), jax.ShapeDtypeStruct((1, 4), F32)]
+    return list(pl.pallas_call(
         functools.partial(update_kernel, all_tokens),
         out_shape=tuple(outs),
         in_specs=[pl.BlockSpec(memory_space=V)] * (3 + len(arrays)),
         out_specs=tuple([pl.BlockSpec(memory_space=V)] * len(outs)),
+        compiler_params=pltpu.CompilerParams(vmem_limit_bytes=60 * 2**20),
     )(shard, total, norm, *arrays))
-    got[22], got[23], got[24] = got[22].reshape(1024), got[23].reshape(1024), got[24].reshape(2, 1024)
-    got[25], got[26] = got[25].reshape(()), got[26].reshape(4)
-    return got
+
+
+def flip(a):
+    return jnp.swapaxes(a, -1, -2)
 
 
 def shards(block_input, cotangent, *arrays):
     batch, tensor = lax.axis_size("batch"), lax.axis_size("tensor")
+    arrays = list(arrays)
+    for n in (2, 3, 6, 7):
+        arrays[n] = flip(arrays[n])
+    arrays[9], arrays[11] = jnp.swapaxes(arrays[9], 0, 1), jnp.swapaxes(arrays[11], 0, 1)
+    arrays[12], arrays[13] = arrays[12].reshape(8, 128), jnp.swapaxes(arrays[13].reshape(2, 8, 128), 0, 1)
     qkv, _, proj, _, fc1, _, fc2, _, norm, _, lepe, _, bias, _ = arrays
     full = gather_call(batch, tensor, qkv, proj, fc1, fc2)
     output, input_grad, grads, small = compute_call(block_input, cotangent, full, norm, lepe, bias)
     shard, total, size = reduce_call(batch, tensor, grads, small)
-    rest = update_call(block_input.shape[0] * batch * tensor, shard, total, size, arrays)
-    return (output, input_grad, *rest)
+    got = update_call(block_input.shape[0] * batch * tensor, shard, total, size, arrays)
+    for n in (4, 5, 6, 7, 12, 13, 14, 15):
+        got[n] = flip(got[n])
+    got[18], got[21] = jnp.swapaxes(got[18], 0, 1), jnp.swapaxes(got[21], 0, 1)
+    got[22], got[23], got[24] = got[22].reshape(1024), got[23].reshape(1024), jnp.swapaxes(got[24], 0, 1).reshape(2, 1024)
+    got[25], got[26] = got[25].reshape(()), got[26].reshape(4)
+    return (output, input_grad, *got)
 
 
 def solution(mesh):

time: 217 us -> 187 us (0.86)
  local copies, waits for them, and re-layouts: 31.1 us -> 0 us
  Pallas kernels: 182 us -> 186 us
    unnamed x51 -> x0, local copies, waits for them, and re-layouts: 29.9 us -> none
where the time goes in v2:
time: 187 us
  Pallas kernels  186 us (99%)
    pallas_call x1, Pallas kernels, compute_call(): pl.pallas_call(compute_kernel, out_shape=(jax.ShapeDtypeStruct((rows, D),...  117 us
    pallas_call x1, Pallas kernels, reduce_call(): pl.pallas_call(functools.partial(reduce_kernel, batch, tensor), out_shape...  40.9 us
    pallas_call x1, Pallas kernels, gather_call(): pl.pallas_call(functools.partial(gather_kernel, batch, tensor), out_shape...  26 us

profile of v2, /device:TPU:0, one launch (start us, length us, event | category | flops | bytes accessed | tf_op | source)
XLA Modules:
  0.0 186.7 jit_solution(8035512810123082306)
XLA Ops:
  0.7 26.0 %shard_map.419.w_ref = bf16[8,4,32,768]{3,2,1,0:T(8,128)(2,1)} custom-call(f32[3,32,64]{2,1,0:T(8,128)} %qkv_w.1, f32[32,64]{1,0:T(8,128)} %bitcast.30, f32[32,256]{1,0:T(8,128)} %fc1_w.1, f32[32,256]{1,0:T(8,128)} %bitcast.27), custom_call_target="tpu_custom_call" | custom-call | tf_op jit(solution)/shard_map/pallas_call | solution.py:453
  26.7 116.7 %shard_map.420 = (bf16[2352,256]{1,0:T(8,128)(2,1)}, f32[2352,256]{1,0:T(8,128)}, bf16[8,4,32,768]{3,2,1,0:T(8,128)(2,1)}, f32[24,256]{1,0:T(8,128)}) custom-call(bf16[2352,256]{1,0:T(8,128)(2,1)} %x_ref.1, bf16[2352,256]{1,0:T(8,128)(2,1)} %cot_ref.1, bf16[8,4,32,768]{3,2,1,0:T(8,128)(2,1)} %shard_map.419.w_ref, f32[6,256]{1,0:T(8,128)} %norm_w.1, ...), custom_call_target="tpu_custom_call" | custom-call | tf_op jit(solution)/shard_map/pallas_call | solution.py:375
  143.4 40.9 %shard_map.421 = (f32[32,768]{1,0:T(8,128)}, f32[24,256]{1,0:T(8,128)}, f32[8,128]{1,0:T(8,128)}) custom-call(bf16[8,4,32,768]{3,2,1,0:T(8,128)(2,1)} %get-tuple-element.65.grad_ref, f32[24,256]{1,0:T(8,128)} %get-tuple-element.66.small_ref), custom_call_target="tpu_custom_call" | custom-call | tf_op jit(solution)/shard_map/pallas_call | solution.py:542
  184.3 2.2 %shard_map.422 = (f32[3,32,64]{2,1,0:T(8,128)}, f32[3,32,64]{2,1,0:T(8,128)}, bf16[3,32,64]{2,1,0:T(8,128)(2,1)}, f32[2,3,32,64]{3,2,1,0:T(8,128)}, f32[32,64]{1...) custom-call(f32[32,768]{1,0:T(8,128)} %get-tuple-element.67.shard_re, ...), custom_call_target="tpu_custom_call" | custom-call | tf_op jit(solution)/shard_map/pallas_call | solution.py:614

commit v3 on v2

v3 whole, which is shorter than its diff:
```python
import functools, math
import numpy as np
import jax, jax.numpy as jnp
from jax import lax
from jax.experimental import pallas as pl
from jax.experimental.pallas import tpu as pltpu
from jax.sharding import PartitionSpec as P

HD = 32
STEP = 10
NPARAM = 791552
CLIP_SCALE = 6.0
BETA_ONE = 0.9
BETA_TWO = 0.999
ADAM_EPS = 1e-08
DECAY_RATE = 0.05
RATE_MATRIX = 0.1
RATE_VECTOR = 0.6
GRID = 14
SPLIT = 7
CELLS = 196
PAD = 112
D = 256
FF = 1024
NORM_EPS = 1e-5
BF = jnp.bfloat16
F32 = jnp.float32
SCALE = HD ** -0.5
LOG2E = 1.4426950408889634


def slot_of(branch, cell):
    row, col = divmod(cell, GRID)
    if branch == 0:
        return row * 16 + col
    stripe, inner = divmod(col, SPLIT)
    return stripe * PAD + row * 8 + inner


def spread_tables():
    into = np.zeros((2, 4, 2 * PAD, 208), np.float32)
    for branch in range(2):
        for cell in range(CELLS):
            for j in range(4):
                into[branch, j, slot_of(branch, cell), cell + 4 * j] = 1.0
    return into.reshape(8, 2 * PAD, 208), into.transpose(0, 1, 3, 2).reshape(8, 208, 2 * PAD)


def key_mask():
    mask = np.full((2, PAD, 128), -1e30, np.float32)
    for branch in range(2):
        for cell in range(CELLS):
            slot = slot_of(branch, cell)
            if slot < PAD:
                mask[branch, slot] = 0.0
    return mask


def lane_table(tensor):
    heads = 4 // tensor
    assert heads == 1
    table = np.zeros((512, 512), np.float32)
    for t in range(4):
        for j in range(2):
            for b in range(2):
                for e in range(HD):
                    table[t * 128 + j * 64 + b * 32 + e, b * 256 + j * 128 + t * 32 + e] = 1.0
    return table


def dot(a, b):
    return lax.dot_general(a, b, (((1,), (0,)), ((), ())), preferred_element_type=F32)


def dot_nt(a, b):
    return lax.dot_general(a, b, (((1,), (1,)), ((), ())), preferred_element_type=F32)


def norm_stats(v):
    centre = jnp.mean(v, -1, keepdims=True)
    centred = v - centre
    spread = jnp.mean(centred * centred, -1, keepdims=True)
    rate = lax.rsqrt(spread + NORM_EPS)
    return centred * rate, rate


def norm_back(grad, gain, xhat, rate):
    gx = grad * gain
    first = jnp.mean(gx, -1, keepdims=True)
    second = jnp.mean(gx * xhat, -1, keepdims=True)
    return rate * (gx - first - xhat * second)


def fold8(v):
    return jnp.sum(v.reshape(v.shape[0] // 8, 8, v.shape[1]), axis=0)


def gelu_pair(h):
    e = jnp.exp2(h * h * (-0.5 * LOG2E))
    t = 1.0 / (1.0 + (0.3275911 * math.sqrt(0.5)) * jnp.abs(h))
    poly = t * (0.5 * 0.254829592 + t * (0.5 * -0.284496736 + t * (0.5 * 1.421413741 + t * (0.5 * -1.453152027 + t * (0.5 * 1.061405429)))))
    tail = poly * e
    phi = jnp.where(h < 0, tail, 1.0 - tail)
    return h * phi, phi + h * e * (1.0 / math.sqrt(2 * math.pi))


def head_masks():
    lane = lax.broadcasted_iota(jnp.int32, (128, 128), 1) // HD
    return [jnp.where(lane == h, 1.0, 0.0).astype(BF) for h in range(4)]


def head_blocks(z, masks):
    zp = jnp.concatenate([z, jnp.zeros((16, 128), BF)], 0)
    return [zp * masks[h] for h in range(4)]


def col_shift(v):
    return pltpu.roll(v, 1, 0), v, pltpu.roll(v, PAD - 1, 0)


def row_up(u, pitch):
    return jnp.concatenate([u[pitch:], jnp.zeros((pitch, 128), F32)], 0)


def row_down(u, pitch):
    return jnp.concatenate([jnp.zeros((pitch, 128), F32), u[:-pitch]], 0)


def window_sum(v, taps, pitch):
    cols = col_shift(v)
    rows = [sum(taps[3 * i + j] * cols[j] for j in range(3)) for i in range(3)]
    return row_down(rows[0], pitch) + rows[1] + row_up(rows[2], pitch)


def window_sum_back(d, taps, pitch):
    cols = col_shift(d)
    rows = [sum(taps[3 * i + j] * cols[2 - j] for j in range(3)) for i in range(3)]
    return row_up(rows[0], pitch) + rows[1] + row_down(rows[2], pitch)


def tap_sums(d, v, pitch):
    cols = col_shift(v)
    out = []
    for i in range(3):
        moved = row_up(d, pitch) if i == 0 else (d if i == 1 else row_down(d, pitch))
        for j in range(3):
            out.append(fold8(moved * cols[j]))
    return out


MT = 336
NT_TILES = 7
MESH = pl.DeviceIdType.MESH


def block_kernel(
    batch, tensor, linked, *refs,
):
    names = NAMES_IN + NAMES_OUT + NAMES_SCRATCH
    r = dict(zip(names, refs))
    (x_hbm, cot_hbm, qkv_ref, proj_ref, m1_ref, m2_ref, norm_ref, lepe_ref, bias_ref, into_hbm, outof_hbm, mask_ref, lane_hbm) = [r[n] for n in NAMES_IN]
    (out_hbm, ig_hbm, shard_ref, total_ref, size_ref) = [r[n] for n in NAMES_OUT]
    (x_ref, cot_ref, out_ref, ig_ref, into_ref, outof_ref, lane_ref,
     gq_s, gm_s, hq_s, hm_s, inq_s, inm_s, midq_s, midm_s, zq_s, zm_s, small_ref, smallb_s, smallt_s, sqb_s, sqt_s,
     fc1_s, fc2_s, wcat_s, proj_s, lepe_s, n1_s, q_s, k_s, v_s, a_s, p_s, att_s, n2_s, act_s, gh_s, gb_s, ga_s, do_s,
     acc_s, tacc_s, s_s, ds_s, dk_s, dv_s) = [r[n] for n in NAMES_SCRATCH[:46]]
    dq_s, dqkv_s = a_s, gh_s
    load_sem, store_sem = r["load_sem"], r["store_sem"]

    rows = x_ref.shape[0]
    images = rows // CELLS
    chunks = images // 4
    depth = m1_ref.shape[0]

    loads = []
    for n, (source, dest) in enumerate(((x_hbm, x_ref), (into_hbm, into_ref), (lane_hbm, lane_ref), (outof_hbm, outof_ref), (cot_hbm, cot_ref))):
        copy = pltpu.make_async_copy(source, dest, load_sem.at[n])
        copy.start()
        loads.append(copy)

    if linked:
        me_b, me_t = lax.axis_index("batch"), lax.axis_index("tensor")
    else:
        me_b, me_t = 0, 0
    along_b = [(lax.rem(me_b + k, batch), me_t) for k in range(1, batch)]
    along_t = [(me_b, lax.rem(me_t + k, tensor)) for k in range(1, tensor)]

    class Push:
        def __init__(self, source, dest, peer, send, recv):
            self.copy = None
            if linked:
                self.copy = pltpu.make_async_remote_copy(src_ref=source, dst_ref=dest, send_sem=send, recv_sem=recv, device_id=peer, device_id_type=MESH)
                self.copy.start()

        def wait_recv(self):
            if self.copy is not None:
                self.copy.wait_recv()

        def wait_send(self):
            if self.copy is not None:
                self.copy.wait_send()

    sent = []

    def push(source, dest, peer, sems, *at):
        got = Push(source, dest, peer, r[sems + "_s"].at[at], r[sems + "_r"].at[at])
        sent.append(got)
        return got

    def arrive(copies):
        for copy in copies:
            copy.wait_recv()

    gq_s[me_b, me_t] = jnp.concatenate([qkv_ref[0], qkv_ref[1], qkv_ref[2], proj_ref[...]], 1).astype(BF)
    gm_s[me_b, me_t, :, 0:256] = m1_ref[...].astype(BF)
    gm_s[me_b, me_t, :, 256:512] = m2_ref[...].astype(BF)
    if linked:
        barrier = pltpu.get_barrier_semaphore()
        for peer in along_b + along_t:
            pl.semaphore_signal(barrier, inc=1, device_id=peer, device_id_type=MESH)
        pl.semaphore_wait(barrier, len(along_b) + len(along_t))
    got_q, got_m = [], []
    over = {}
    for name, ref in (("zq", gq_s), ("zm", gm_s)):
        mine = ref.at[me_b, me_t]
        over[name] = [push(mine, mine, peer, name, k) for k, peer in enumerate(along_t)]
        if name == "zq":
            got_q += [push(mine, mine, peer, "bq", 0, k) for k, peer in enumerate(along_b)]
    acc_s[...] = jnp.zeros_like(acc_s)
    lp = lepe_ref[...]
    lepe_s[0:10, :] = jnp.concatenate([lp[:, h * 64 + b * 32:h * 64 + b * 32 + 32] for b in range(2) for h in range(4)], 1)
    for n in range(1, tensor):
        over["zq"][n - 1].wait_recv()
        slot = gq_s.at[me_b, lax.rem(me_t + tensor - n, tensor)]
        got_q += [push(slot, slot, peer, "bq", n, k) for k, peer in enumerate(along_b)]
    for n in range(tensor):
        if n > 0:
            over["zm"][n - 1].wait_recv()
        slot = gm_s.at[me_b, lax.rem(me_t + tensor - n, tensor)]
        got_m += [push(slot, slot, peer, "bm", n, k) for k, peer in enumerate(along_b)]
    loads[0].wait()

    @pl.loop(0, NT_TILES)
    def _(i):
        sl = pl.ds(pl.multiple_of(i * MT, 16), MT)
        xhat, rate = norm_stats(x_ref[sl, :].astype(F32))
        n1_s[sl, :] = (xhat * norm_ref[0:1, :] + norm_ref[1:2, :]).astype(BF)

    loads[1].wait()
    loads[2].wait()
    arrive(got_q)
    for half in range(2):
        lanes = slice(half * 128, half * 128 + 128)
        packed = jnp.concatenate([jnp.concatenate([gq_s[n, t, :, lanes] for n in range(batch)], 0) for t in range(4)], 1)
        work = dot(packed, lane_ref[...]).astype(BF)
        for b in range(2):
            if half == 0:
                wcat_s[:, b * 384:b * 384 + 256] = work[:, b * 256:b * 256 + 256]
            else:
                wcat_s[:, b * 384 + 256:b * 384 + 384] = work[:, b * 256:b * 256 + 128]
                proj_s[:, b * 128:b * 128 + 128] = work[:, b * 256 + 128:b * 256 + 256]

    @pl.loop(0, chunks)
    def _(c):
        for j in range(4):
            window = n1_s[pl.ds(pl.multiple_of(c * 784 + 192 * j, 16), 208), :]
            for b in range(2):
                spread = dot(into_ref[b * 4 + j], window).astype(BF)
                qkv = dot(spread, wcat_s[:, b * 384:(b + 1) * 384]).astype(BF)
                for s in range(2):
                    at = c * 8 + j * 2 + s
                    q_s[b, at] = qkv[s * PAD:(s + 1) * PAD, 0:128]
                    k_s[b, at] = qkv[s * PAD:(s + 1) * PAD, 128:256]
                    v_s[b, at] = qkv[s * PAD:(s + 1) * PAD, 256:384]

    masks = head_masks()

    stripes = images * 2

    def scores_stage(b, at):
        s_s[b] = dot_nt(k_s[b, at], jnp.concatenate(head_blocks(q_s[b, at], masks), 0))

    def soft_stage(b, at):
        for h in range(4):
            lanes = slice(h * 128, (h + 1) * 128)
            s = s_s[b, :, lanes] * (SCALE * LOG2E) + mask_ref[b]
            p = jnp.exp2(s - jnp.max(s, 0, keepdims=True))
            p_s[b, at, :, lanes] = (p * (1.0 / jnp.sum(p, 0, keepdims=True))).astype(BF)

    def mix_stage(b, at):
        pitch = 16 - 8 * b
        v = v_s[b, at]
        vt = jnp.transpose(v)
        ots = [dot(vt[h * HD:(h + 1) * HD], p_s[b, at, :, h * 128:(h + 1) * 128]) for h in range(4)]
        mixed = jnp.transpose(jnp.concatenate(ots, 0))[:PAD]
        taps = [lepe_s[n:n + 1, b * 128:(b + 1) * 128] for n in range(10)]
        local = window_sum(v.astype(F32), taps, pitch) + taps[9]
        a_s[b, at] = (mixed + local).astype(BF)

    @pl.loop(0, stripes + 2)
    def _(i):
        first, second, third = jnp.minimum(i, stripes - 1), jnp.clip(i - 1, 0, stripes - 1), jnp.maximum(i - 2, 0)
        for b in range(2):
            mix_stage(b, third)
            soft_stage(b, second)
            scores_stage(b, first)

    def gather_rows(source, c, dest, lanes):
        for b in range(2):
            tail = None
            for j in range(4):
                both = jnp.concatenate([source(b, c * 8 + j * 2), source(b, c * 8 + j * 2 + 1)], 0)
                got = dot(outof_ref[b * 4 + j], both)
                head = got[0:16] if tail is None else got[0:16] + tail
                base = c * 784 + 192 * j
                cols = slice(b * lanes, (b + 1) * lanes)
                dest[pl.ds(pl.multiple_of(base, 16), 16), cols] = head.astype(BF)
                dest[pl.ds(pl.multiple_of(base + 16, 16), 176), cols] = got[16:192].astype(BF)
                tail = got[192:208]
                if j == 3:
                    dest[pl.ds(pl.multiple_of(base + 192, 16), 16), cols] = tail.astype(BF)

    loads[3].wait()
    loads[4].wait()

    @pl.loop(0, chunks)
    def _(c):
        gather_rows(lambda b, at: a_s[b, at], c, att_s, 128)

    arrive(got_m)
    for t in range(4):
        for n in range(batch):
            at = slice(n * depth, (n + 1) * depth)
            fc1_s[at, t * 256:(t + 1) * 256] = gm_s[n, t, :, 0:256]
            fc2_s[at, t * 256:(t + 1) * 256] = gm_s[n, t, :, 256:512]

    @pl.loop(0, NT_TILES)
    def _(i):
        sl = pl.ds(pl.multiple_of(i * MT, 16), MT)
        one = dot_nt(att_s[sl, :], proj_s[...]) + norm_ref[2:3, :]
        middle = x_ref[sl, :].astype(F32) + one
        xhat, rate = norm_stats(middle)
        n2 = (xhat * norm_ref[3:4, :] + norm_ref[4:5, :]).astype(BF)
        n2_s[sl, :] = n2
        cot = cot_ref[sl, :]
        two = jnp.zeros((MT, D), F32)
        gn = jnp.zeros((MT, D), F32)
        for f in range(4):
            fs = slice(f * 256, (f + 1) * 256)
            hidden = dot(n2, fc1_s[:, fs]) + jnp.concatenate([bias_ref[2 * f:2 * f + 1, :], bias_ref[2 * f + 1:2 * f + 2, :]], 1)
            gelu, slope = gelu_pair(hidden)
            act = gelu.astype(BF)
            act_s[sl, fs] = act
            two = two + dot_nt(act, fc2_s[:, fs])
            gh_f = dot(cot, fc2_s[:, fs]) * slope
            gh = gh_f.astype(BF)
            gh_s[sl, fs] = gh
            acc_s[10 + f] += fold8(gh.astype(F32))
            gn = gn + dot_nt(gh, fc1_s[:, fs])
        two = two + norm_ref[5:6, :]
        result = middle + two
        out_ref[sl, :] = result.astype(BF)
        acc_s[6] += fold8(one * one)
        acc_s[7] += fold8(middle * middle)
        acc_s[8] += fold8(two * two)
        acc_s[9] += fold8(result * result)
        cotf = cot.astype(F32)
        acc_s[5] += fold8(cotf)
        acc_s[3] += fold8(gn * xhat)
        acc_s[4] += fold8(gn)
        gm = cotf + norm_back(gn, norm_ref[3:4, :], xhat, rate)
        ig_ref[sl, :] = gm
        gb = gm.astype(BF)
        gb_s[sl, :] = gb
        acc_s[2] += fold8(gb.astype(F32))
        ga_s[sl, :] = dot(gb, proj_s[...]).astype(BF)

    stores = [pltpu.make_async_copy(out_ref, out_hbm, store_sem.at[0])]
    stores[0].start()

    def weight_grad(left, right):
        return lax.dot_general(left, right, (((0,), (0,)), ((), ())), preferred_element_type=F32)

    def put_rows(ref, value, t, off):
        for n in range(batch):
            ref[n, t, :, off:off + value.shape[1]] = value[n * depth:(n + 1) * depth]

    for left, right, off in ((n2_s, gh_s, 0), (cot_ref, act_s, 256)):
        for t in range(4):
            put_rows(hm_s, weight_grad(left[...], right[:, t * 256:(t + 1) * 256]).astype(BF), t, off)
    gp = weight_grad(gb_s[...], att_s[...]).astype(BF)
    sums_m = [push(hm_s.at[peer[0]], inm_s.at[k], peer, "rm", k) for k, peer in enumerate(along_b)]

    @pl.loop(0, chunks)
    def _(c):
        for j in range(4):
            window = ga_s[pl.ds(pl.multiple_of(c * 784 + 192 * j, 16), 208), :]
            for b in range(2):
                spread = dot(into_ref[b * 4 + j], window[:, b * 128:(b + 1) * 128]).astype(BF)
                for s in range(2):
                    do_s[b, c * 8 + j * 2 + s] = spread[s * PAD:(s + 1) * PAD]

    def dprobs_stage(b, at):
        s_s[b] = dot_nt(v_s[b, at], jnp.concatenate(head_blocks(do_s[b, at], masks), 0))

    def dscores_stage(b, at):
        for h in range(4):
            lanes = slice(h * 128, (h + 1) * 128)
            pf = p_s[b, at, :, lanes].astype(F32)
            t = pf * s_s[b, :, lanes]
            ds_s[b, :, lanes] = (t - pf * jnp.sum(t, 0, keepdims=True)).astype(BF)

    def dqkv_stage(b, at):
        pitch = 16 - 8 * b
        q, k, v, do = q_s[b, at], k_s[b, at], v_s[b, at], do_s[b, at]
        kt = jnp.transpose(k)
        dqt = [dot(kt[h * HD:(h + 1) * HD], ds_s[b, :, h * 128:(h + 1) * 128]) for h in range(4)]
        dv = dot(p_s[b, at], jnp.concatenate(head_blocks(do, masks), 0))
        dk = dot(ds_s[b], jnp.concatenate(head_blocks(q, masks), 0))
        dq = jnp.transpose(jnp.concatenate(dqt, 0))[:PAD]
        taps = [lepe_s[n:n + 1, b * 128:(b + 1) * 128] for n in range(10)]
        dof, vf = do.astype(F32), v.astype(F32)
        dv = dv + window_sum_back(dof, taps, pitch)
        for n, part in enumerate(tap_sums(dof, vf, pitch)):
            tacc_s[b, n] += part
        tacc_s[b, 9] += fold8(dof)
        dq_s[b, at] = (dq * SCALE).astype(BF)
        dk_s[b, at] = (dk * SCALE).astype(BF)
        dv_s[b, at] = dv.astype(BF)

    @pl.loop(0, stripes + 2)
    def _(i):
        first, second, third = jnp.minimum(i, stripes - 1), jnp.clip(i - 1, 0, stripes - 1), jnp.maximum(i - 2, 0)
        for b in range(2):
            @pl.when(i == 2)
            def _():
                tacc_s[b] = jnp.zeros((10, 8, 128), F32)
            dqkv_stage(b, third)
            dscores_stage(b, second)
            dprobs_stage(b, first)

    def add_up(own, into, mid):
        for n in range(tensor):
            value = own[me_b, n].astype(F32)
            for k in range(batch - 1):
                value = value + into[k, n].astype(F32)
            mid[n] = value.astype(BF)

    arrive(sums_m)
    add_up(hm_s, inm_s, midm_s)
    last_m = [push(midm_s.at[peer[1]], zm_s.at[k], peer, "tm", k) for k, peer in enumerate(along_t)]

    @pl.loop(0, chunks)
    def _(c):
        gather_rows(lambda b, at: jnp.concatenate([dq_s[b, at], dk_s[b, at], dv_s[b, at]], 1), c, dqkv_s, 384)

    gw = weight_grad(n1_s[...], dqkv_s[:, 0:768]).astype(BF)
    work0 = jnp.concatenate([gw[:, 0:256], gw[:, 384:640]], 1)
    work1 = jnp.concatenate([gw[:, 256:384], gp[:, 0:128], gw[:, 640:768], gp[:, 128:256]], 1)
    for half, work in enumerate((work0, work1)):
        packed = dot_nt(work, lane_ref[...]).astype(BF)
        for t in range(4):
            put_rows(hq_s, packed[:, t * 128:(t + 1) * 128], t, 128 * half)
    sums_q = [push(hq_s.at[peer[0]], inq_s.at[k], peer, "rq", k) for k, peer in enumerate(along_b)]

    @pl.loop(0, NT_TILES)
    def _(i):
        sl = pl.ds(pl.multiple_of(i * MT, 16), MT)
        gn = dot_nt(dqkv_s[sl, 0:768], wcat_s[...])
        xhat, rate = norm_stats(x_ref[sl, :].astype(F32))
        acc_s[0] += fold8(gn * xhat)
        acc_s[1] += fold8(gn)
        ig_ref[sl, :] = ig_ref[sl, :] + norm_back(gn, norm_ref[0:1, :], xhat, rate)

    stores.append(pltpu.make_async_copy(ig_ref, ig_hbm, store_sem.at[1]))
    stores[1].start()
    for n in range(14):
        small_ref[n:n + 1, :] = jnp.sum(acc_s[n], 0, keepdims=True)
    for n in range(10):
        row = jnp.concatenate([jnp.sum(tacc_s[b, n], 0, keepdims=True) for b in range(2)], 1)
        small_ref[14 + n:15 + n, :] = jnp.concatenate([row[:, b * 128 + h * 32:b * 128 + h * 32 + 32] for h in range(4) for b in range(2)], 1)


    smallb_s[me_b] = small_ref[...]
    small_b = [push(small_ref, smallb_s.at[me_b], peer, "sb", k) for k, peer in enumerate(along_b)]
    arrive(sums_q)
    add_up(hq_s, inq_s, midq_s)
    last_q = [push(midq_s.at[peer[1]], zq_s.at[k], peer, "tq", k) for k, peer in enumerate(along_t)]
    arrive(small_b)

    def in_order(ref, count):
        part = ref[0]
        for n in range(1, count):
            part = part + ref[n]
        return part

    part = in_order(smallb_s, batch)
    total_ref[...] = part
    smallt_s[me_t] = part
    small_t = [push(total_ref, smallt_s.at[me_t], peer, "st", k) for k, peer in enumerate(along_t)]
    arrive(last_m)
    arrive(last_q)
    lanes = jnp.zeros((8, 128), F32)
    for mid, into, off in ((midm_s, zm_s, 0), (midq_s, zq_s, 512)):
        shard = mid[me_t].astype(F32)
        for k in range(tensor - 1):
            shard = shard + into[k].astype(F32)
        shard_ref[:, off:off + shard.shape[1]] = shard
        squares = fold8(shard * shard)
        for n in range(shard.shape[1] // 128):
            lanes = lanes + squares[:, n * 128:(n + 1) * 128]
    sqb_s[me_b] = lanes
    size_ref[...] = lanes
    square_b = [push(size_ref, sqb_s.at[me_b], peer, "qb", k) for k, peer in enumerate(along_b)]
    arrive(square_b)
    lanes = in_order(sqb_s, batch)
    sqt_s[me_t] = lanes
    for copy in square_b:
        copy.wait_send()
        sent.remove(copy)
    size_ref[...] = lanes
    square_t = [push(size_ref, sqt_s.at[me_t], peer, "qt", k) for k, peer in enumerate(along_t)]
    arrive(small_t)
    for copy in small_t:
        copy.wait_send()
        sent.remove(copy)
    vectors = in_order(smallt_s, tensor)
    total_ref[...] = vectors
    row = lax.broadcasted_iota(jnp.int32, vectors.shape, 0)
    vectors = jnp.where((row < 6) | (row >= 10), vectors, 0.0)
    vector = jnp.sum(jnp.sum(vectors * vectors, 0, keepdims=True), 1, keepdims=True)
    arrive(square_t)
    for copy in sent:
        copy.wait_send()
    matrix = jnp.sum(jnp.sum(in_order(sqt_s, tensor), 0, keepdims=True), 1, keepdims=True)
    size_ref[...] = jnp.broadcast_to(jnp.sqrt(matrix + vector), (8, 128))
    for copy in stores:
        copy.wait()


NAMES_IN = ["x_hbm", "cot_hbm", "qkv", "proj", "m1", "m2", "norm", "lepe", "bias", "into_hbm", "outof_hbm", "mask", "lane_hbm"]
NAMES_OUT = ["out_hbm", "ig_hbm", "shard", "total", "size"]


def scratch_list(batch, tensor, rows, depth):
    n = rows // CELLS * 2
    V = pltpu.VMEM
    dma = pltpu.SemaphoreType.DMA
    stripe = (2, n, PAD, 128)
    items = [
        ("x", V((rows, D), BF)), ("cot", V((rows, D), BF)), ("out", V((rows, D), BF)), ("ig", V((rows, D), F32)),
        ("into", V((8, 2 * PAD, 208), BF)), ("outof", V((8, 208, 2 * PAD), BF)), ("lane", V((512, 512), BF)),
        ("gq", V((batch, tensor, depth, 256), BF)), ("gm", V((batch, tensor, depth, 512), BF)),
        ("hq", V((batch, tensor, depth, 256), BF)), ("hm", V((batch, tensor, depth, 512), BF)),
        ("inq", V((batch - 1, tensor, depth, 256), BF)), ("inm", V((batch - 1, tensor, depth, 512), BF)),
        ("midq", V((tensor, depth, 256), BF)), ("midm", V((tensor, depth, 512), BF)),
        ("zqb", V((tensor - 1, depth, 256), BF)), ("zmb", V((tensor - 1, depth, 512), BF)),
        ("small", V((24, D), F32)), ("smallb", V((batch, 24, D), F32)), ("smallt", V((tensor, 24, D), F32)),
        ("sqb", V((batch, 8, 128), F32)), ("sqt", V((tensor, 8, 128), F32)),
        ("fc1", V((D, FF), BF)), ("fc2", V((D, FF), BF)), ("wcat", V((D, 768), BF)), ("proj_w", V((D, D), BF)), ("lepe_w", V((16, D), F32)),
        ("n1", V((rows, D), BF)), ("q", V(stripe, BF)), ("k", V(stripe, BF)), ("v", V(stripe, BF)), ("a", V(stripe, BF)),
        ("p", V((2, n, PAD, 512), BF)), ("att", V((rows, D), BF)), ("n2", V((rows, D), BF)), ("act", V((rows, FF), BF)), ("gh", V((rows, FF), BF)),
        ("gb", V((rows, D), BF)), ("ga", V((rows, D), BF)), ("do", V(stripe, BF)),
        ("acc", V((14, 8, D), F32)), ("tacc", V((2, 10, 8, 128), F32)),
        ("s", V((2, PAD, 512), F32)), ("ds", V((2, PAD, 512), BF)), ("dk", V(stripe, BF)), ("dv", V(stripe, BF)),
        ("load_sem", dma((5,))), ("store_sem", dma((2,))),
    ]
    b, t = batch - 1, tensor - 1
    for name, shape in (("zq", (t,)), ("zm", (t,)), ("bq", (tensor, b)), ("bm", (tensor, b)), ("rm", (b,)), ("rq", (b,)), ("tm", (t,)), ("tq", (t,)), ("sb", (b,)), ("st", (t,)), ("qb", (b,)), ("qt", (t,))):
        items += [(name + "_s", dma(shape)), (name + "_r", dma(shape))]
    return items


NAMES_SCRATCH = [name for name, _ in scratch_list(8, 4, 2352, 32)]


def block_call(batch, tensor, linked, x, cot, qkv, proj, fc1, fc2, norm, lepe, bias):
    rows, depth = x.shape[0], fc1.shape[0]
    into, outof = spread_tables()
    args = (x, cot, qkv, proj, fc1, fc2, norm, lepe, bias, jnp.asarray(into, BF), jnp.asarray(outof, BF), jnp.asarray(key_mask()), jnp.asarray(lane_table(4), BF))
    V = pl.BlockSpec(memory_space=pltpu.VMEM)
    H = pl.BlockSpec(memory_space=pl.ANY)
    extra = dict(collective_id=0, has_side_effects=True) if linked else {}
    return pl.pallas_call(
        functools.partial(block_kernel, batch, tensor, linked),
        out_shape=(
            jax.ShapeDtypeStruct((rows, D), BF),
            jax.ShapeDtypeStruct((rows, D), F32),
            jax.ShapeDtypeStruct((depth, 768), F32),
            jax.ShapeDtypeStruct((24, D), F32),
            jax.ShapeDtypeStruct((8, 128), F32),
        ),
        in_specs=[H, H] + [V] * 7 + [H, H, V, H],
        out_specs=(H, H, V, V, V),
        scratch_shapes=[shape for _, shape in scratch_list(batch, tensor, rows, depth)],
        compiler_params=pltpu.CompilerParams(vmem_limit_bytes=62 * 2**20, **extra),
    )(*args)


def adam(master, first, second, clipped, rate, decay):
    first = BETA_ONE * first + (1.0 - BETA_ONE) * clipped
    second = BETA_TWO * second + (1.0 - BETA_TWO) * clipped * clipped
    hat = first * (1.0 / (1.0 - BETA_ONE**STEP))
    spread = second * (1.0 / (1.0 - BETA_TWO**STEP))
    return master - rate * (hat / (jnp.sqrt(spread) + ADAM_EPS) + decay * master), first, second


def update_kernel(
    all_tokens, out_in, ig_in, shard_ref, total_ref, norm_ref,
    qkv_w, qkv_m, proj_w, proj_m, fc1_w, fc1_m, fc2_w, fc2_m, norm_w, norm_m, lepe_w, lepe_m, bias_w, bias_m,
    out_o, ig_o, qkv_g, qkv_n, qkv_l, qkv_o, proj_g, proj_n, proj_l, proj_o, fc1_g, fc1_n, fc1_l, fc1_o, fc2_g, fc2_n, fc2_l, fc2_o,
    norm_g, norm_n, norm_o, lepe_g, lepe_n, lepe_o, bias_g, bias_n, bias_o, size_o, rms_o, sems,
):
    copies = [pltpu.make_async_copy(out_in, out_o, sems.at[0]), pltpu.make_async_copy(ig_in, ig_o, sems.at[1])]
    for copy in copies:
        copy.start()
    size = norm_ref[0:1, 0:1]
    factor = jnp.minimum(1.0, CLIP_SCALE * math.sqrt(NPARAM) / (size + 1e-06))
    size_o[...] = size

    def one(grad, w, m, g_o, n_o, l_o, m_o, at, rate, decay, pair=lambda n, at: (n,) + at):
        clipped = grad * factor
        new, first, second = adam(w[at], m[pair(0, at)], m[pair(1, at)], clipped, rate, decay)
        g_o[at] = clipped
        n_o[at] = new
        if l_o is not None:
            l_o[at] = new.astype(BF)
        m_o[pair(0, at)] = first
        m_o[pair(1, at)] = second

    every = (slice(None), slice(None))
    middle = lambda n, at: (at[0], n, at[1])
    one(shard_ref[:, 0:256], fc1_w, fc1_m, fc1_g, fc1_n, fc1_l, fc1_o, every, RATE_MATRIX, DECAY_RATE)
    one(shard_ref[:, 256:512], fc2_w, fc2_m, fc2_g, fc2_n, fc2_l, fc2_o, every, RATE_MATRIX, DECAY_RATE)
    for j in range(3):
        one(shard_ref[:, 512 + 64 * j:576 + 64 * j], qkv_w, qkv_m, qkv_g, qkv_n, qkv_l, qkv_o, (j,) + every, RATE_MATRIX, DECAY_RATE)
    one(shard_ref[:, 704:768], proj_w, proj_m, proj_g, proj_n, proj_l, proj_o, every, RATE_MATRIX, DECAY_RATE)
    one(total_ref[0:6], norm_w, norm_m, norm_g, norm_n, None, norm_o, every, RATE_VECTOR, 0.0, middle)
    one(total_ref[14:24], lepe_w, lepe_m, lepe_g, lepe_n, None, lepe_o, every, RATE_VECTOR, 0.0, middle)
    for f in range(8):
        at = (slice(f, f + 1), slice(None))
        part = total_ref[10 + f // 2:11 + f // 2, 128 * (f % 2):128 * (f % 2) + 128]
        one(part, bias_w, bias_m, bias_g, bias_n, None, bias_o, at, RATE_VECTOR, 0.0, middle)
    lane = lax.broadcasted_iota(jnp.int32, (1, 4), 1)
    sums = jnp.zeros((1, 4), F32)
    for n in range(4):
        sums = jnp.where(lane == n, jnp.sum(total_ref[6 + n:7 + n], 1, keepdims=True), sums)
    rms_o[...] = jnp.sqrt(sums * (1.0 / (all_tokens * D)))
    for copy in copies:
        copy.wait()


def update_call(all_tokens, out, ig, shard, total, norm, arrays):
    V = pltpu.VMEM
    like = lambda a, dt=F32: jax.ShapeDtypeStruct(a.shape, dt)
    outs = [like(out, BF), like(ig)]
    H = pl.BlockSpec(memory_space=pl.ANY)
    for n in range(4):
        w, m = arrays[2 * n], arrays[2 * n + 1]
        outs += [like(w), like(w), like(w, BF), like(m)]
    for n in range(4, 7):
        w, m = arrays[2 * n], arrays[2 * n + 1]
        outs += [like(w), like(w), like(m)]
    outs += [jax.ShapeDtypeStruct((1, 1), F32), jax.ShapeDtypeStruct((1, 4), F32)]
    return list(pl.pallas_call(
        functools.partial(update_kernel, all_tokens),
        out_shape=tuple(outs),
        in_specs=[H, H] + [pl.BlockSpec(memory_space=V)] * (3 + len(arrays)),
        out_specs=tuple([H, H] + [pl.BlockSpec(memory_space=V)] * (len(outs) - 2)),
        scratch_shapes=[pltpu.SemaphoreType.DMA((2,))],
        compiler_params=pltpu.CompilerParams(vmem_limit_bytes=60 * 2**20),
    )(out, ig, shard, total, norm, *arrays))


def flip(a):
    return jnp.swapaxes(a, -1, -2)


def shards(block_input, cotangent, *arrays):
    batch, tensor = lax.axis_size("batch"), lax.axis_size("tensor")
    arrays = list(arrays)
    for n in (2, 3, 6, 7):
        arrays[n] = flip(arrays[n])
    arrays[9], arrays[11] = jnp.swapaxes(arrays[9], 0, 1), jnp.swapaxes(arrays[11], 0, 1)
    arrays[12], arrays[13] = arrays[12].reshape(8, 128), jnp.swapaxes(arrays[13].reshape(2, 8, 128), 0, 1)
    qkv, _, proj, _, fc1, _, fc2, _, norm, _, lepe, _, bias, _ = arrays
    output, input_grad, shard, total, size = block_call(batch, tensor, True, block_input, cotangent, qkv, proj, fc1, fc2, norm, lepe, bias)
    output, input_grad, *got = update_call(block_input.shape[0] * batch * tensor, output, input_grad, shard, total, size, arrays)
    for n in (4, 5, 6, 7, 12, 13, 14, 15):
        got[n] = flip(got[n])
    got[18], got[21] = jnp.swapaxes(got[18], 0, 1), jnp.swapaxes(got[21], 0, 1)
    got[22], got[23], got[24] = got[22].reshape(1024), got[23].reshape(1024), jnp.swapaxes(got[24], 0, 1).reshape(2, 1024)
    got[25], got[26] = got[25].reshape(()), got[26].reshape(4)
    return (output, input_grad, *got)


def solution(mesh):
    token, matrix, moment = P(("batch", "tensor"), None), P("batch", "tensor"), P(None, "batch", "tensor")
    back, back_moment = P("tensor", "batch"), P(None, "tensor", "batch")
    stack, stack_moment = P(None, "batch", "tensor"), P(None, None, "batch", "tensor")
    return jax.shard_map(
        shards,
        mesh=mesh,
        in_specs=(token, token, stack, stack_moment, back, back_moment, matrix, moment, back, back_moment) + (P(),) * 6,
        out_specs=(token, token) + (stack,) * 3 + (stack_moment,) + (back,) * 3 + (back_moment,) + (matrix,) * 3 + (moment,) + (back,) * 3 + (back_moment,) + (P(),) * 11,
        check_vma=False,
    )
```

time: 187 us -> 213 us (1.14)
  Pallas kernels: 186 us -> 212 us
    pallas_call x1, Pallas kernels: 2.24 us -> 113 us  [update_call(): pl.pallas_call(functools.partial(update_kernel, all_tokens), out_shape=tu...]
    pallas_call x3 -> x1, Pallas kernels: 184 us -> 99.2 us  [block_call(): pl.pallas_call(functools.partial(block_kernel, batch, tensor, linked), ou...]
where the time goes in v3:
time: 213 us
  Pallas kernels  212 us (100%)
    pallas_call x1, Pallas kernels, update_call(): pl.pallas_call(functools.partial(update_kernel, all_tokens), out_shape=tu...  113 us
    pallas_call x1, Pallas kernels, block_call(): pl.pallas_call(functools.partial(block_kernel, batch, tensor, linked), ou...  99.2 us

profile of v3, /device:TPU:0, one launch (start us, length us, event | category | flops | bytes accessed | tf_op | source)
XLA Modules:
  0.0 212.5 jit_solution(14488854394709259554)
XLA Ops:
  0.7 99.2 %shard_map.419 = (bf16[2352,256]{1,0:T(8,128)(2,1)}, f32[2352,256]{1,0:T(8,128)}, f32[32,768]{1,0:T(8,128)}, f32[24,256]{1,0:T(8,128)}, f32[8,128]{1,0:T(8,128)}) custom-call(bf16[2352,256]{1,0:T(8,128)(2,1)} %refs_0_.1, bf16[2352,256]{1,0:T(8,128)(2,1)} %refs_1_.1, f32[3,32,64]{2,1,0:T(8,128)} %qkv_w.1, f32[32,64]{1,0:T(8,128)} %bitcast.30, ...), custom_call_target="tpu_custom_call" | custom-call | tf_op jit(solution)/shard_map/pallas_call | solution.py:584
  99.9 112.7 %shard_map.420 = (bf16[2352,256]{1,0:T(8,128)(2,1)}, f32[2352,256]{1,0:T(8,128)}, f32[3,32,64]{2,1,0:T(8,128)}, f32[3,32,64]{2,1,0:T(8,128)}, bf16[3,32,64]{2,1,...) custom-call(bf16[2352,256]{1,0:T(8,128)(2,1)} %get-tuple-element.63., ...), custom_call_target="tpu_custom_call" | custom-call | tf_op jit(solution)/shard_map/pallas_call | solution.py:665

commit v4 on v3

--- a/solution.py
+++ b/solution.py
@@ -609,11 +609,16 @@
     all_tokens, out_in, ig_in, shard_ref, total_ref, norm_ref,
     qkv_w, qkv_m, proj_w, proj_m, fc1_w, fc1_m, fc2_w, fc2_m, norm_w, norm_m, lepe_w, lepe_m, bias_w, bias_m,
     out_o, ig_o, qkv_g, qkv_n, qkv_l, qkv_o, proj_g, proj_n, proj_l, proj_o, fc1_g, fc1_n, fc1_l, fc1_o, fc2_g, fc2_n, fc2_l, fc2_o,
-    norm_g, norm_n, norm_o, lepe_g, lepe_n, lepe_o, bias_g, bias_n, bias_o, size_o, rms_o, sems,
+    norm_g, norm_n, norm_o, lepe_g, lepe_n, lepe_o, bias_g, bias_n, bias_o, size_o, rms_o, out_s, ig_s, sems,
 ):
-    copies = [pltpu.make_async_copy(out_in, out_o, sems.at[0]), pltpu.make_async_copy(ig_in, ig_o, sems.at[1])]
-    for copy in copies:
-        copy.start()
+    moves = []
+    for source, held, dest in ((out_in, out_s, out_o), (ig_in, ig_s, ig_o)):
+        step = held.shape[0] // 3
+        for n in range(3):
+            at = pl.ds(n * step, step)
+            moves.append([pltpu.make_async_copy(source.at[at], held.at[at], sems.at[0, len(moves)]), pltpu.make_async_copy(held.at[at], dest.at[at], sems.at[1, len(moves)])])
+    for into, _ in moves:
+        into.start()
     size = norm_ref[0:1, 0:1]
     factor = jnp.minimum(1.0, CLIP_SCALE * math.sqrt(NPARAM) / (size + 1e-06))
     size_o[...] = size
@@ -628,6 +633,9 @@
         m_o[pair(0, at)] = first
         m_o[pair(1, at)] = second
 
+    for into, away in moves:
+        into.wait()
+        away.start()
     every = (slice(None), slice(None))
     middle = lambda n, at: (at[0], n, at[1])
     one(shard_ref[:, 0:256], fc1_w, fc1_m, fc1_g, fc1_n, fc1_l, fc1_o, every, RATE_MATRIX, DECAY_RATE)
@@ -646,8 +654,8 @@
     for n in range(4):
         sums = jnp.where(lane == n, jnp.sum(total_ref[6 + n:7 + n], 1, keepdims=True), sums)
     rms_o[...] = jnp.sqrt(sums * (1.0 / (all_tokens * D)))
-    for copy in copies:
-        copy.wait()
+    for _, away in moves:
+        away.wait()
 
 
 def update_call(all_tokens, out, ig, shard, total, norm, arrays):
@@ -667,7 +675,7 @@
         out_shape=tuple(outs),
         in_specs=[H, H] + [pl.BlockSpec(memory_space=V)] * (3 + len(arrays)),
         out_specs=tuple([H, H] + [pl.BlockSpec(memory_space=V)] * (len(outs) - 2)),
-        scratch_shapes=[pltpu.SemaphoreType.DMA((2,))],
+        scratch_shapes=[V(out.shape, BF), V(ig.shape, F32), pltpu.SemaphoreType.DMA((2, 6))],
         compiler_params=pltpu.CompilerParams(vmem_limit_bytes=60 * 2**20),
     )(out, ig, shard, total, norm, *arrays))
 

time: 213 us -> 105 us (0.49)
  Pallas kernels: 212 us -> 104 us
    pallas_call x1, Pallas kernels: 113 us -> 5.25 us  [update_call(): pl.pallas_call(functools.partial(update_kernel, all_tokens), out_shape=tu...]
where the time goes in v4:
time: 105 us
  Pallas kernels  104 us (99%)
    pallas_call x1, Pallas kernels, block_call(): pl.pallas_call(functools.partial(block_kernel, batch, tensor, linked), ou...  99.2 us
    pallas_call x1, Pallas kernels, update_call(): pl.pallas_call(functools.partial(update_kernel, all_tokens), out_shape=tu...  5.25 us

profile of v4, /device:TPU:0, one launch (start us, length us, event | category | flops | bytes accessed | tf_op | source)
XLA Modules:
  0.0 105.1 jit_solution(4131146062588977803)
XLA Ops:
  0.7 99.2 %shard_map.419 = (bf16[2352,256]{1,0:T(8,128)(2,1)}, f32[2352,256]{1,0:T(8,128)}, f32[32,768]{1,0:T(8,128)}, f32[24,256]{1,0:T(8,128)}, f32[8,128]{1,0:T(8,128)}) custom-call(bf16[2352,256]{1,0:T(8,128)(2,1)} %refs_0_.1, bf16[2352,256]{1,0:T(8,128)(2,1)} %refs_1_.1, f32[3,32,64]{2,1,0:T(8,128)} %qkv_w.1, f32[32,64]{1,0:T(8,128)} %bitcast.30, ...), custom_call_target="tpu_custom_call" | custom-call | tf_op jit(solution)/shard_map/pallas_call | solution.py:584
  99.9 5.3 %shard_map.420 = (bf16[2352,256]{1,0:T(8,128)(2,1)}, f32[2352,256]{1,0:T(8,128)}, f32[3,32,64]{2,1,0:T(8,128)}, f32[3,32,64]{2,1,0:T(8,128)}, bf16[3,32,64]{2,1,...) custom-call(bf16[2352,256]{1,0:T(8,128)(2,1)} %get-tuple-element.63., ...), custom_call_target="tpu_custom_call" | custom-call | tf_op jit(solution)/shard_map/pallas_call | solution.py:673

commit v5 on v4

v5 whole, which is shorter than its diff:
```python
import functools, math
import numpy as np
import jax, jax.numpy as jnp
from jax import lax
from jax.experimental import pallas as pl
from jax.experimental.pallas import tpu as pltpu
from jax.sharding import PartitionSpec as P

HD = 32
STEP = 10
NPARAM = 791552
CLIP_SCALE = 6.0
BETA_ONE = 0.9
BETA_TWO = 0.999
ADAM_EPS = 1e-08
DECAY_RATE = 0.05
RATE_MATRIX = 0.1
RATE_VECTOR = 0.6
GRID = 14
SPLIT = 7
CELLS = 196
PAD = 112
D = 256
FF = 1024
NORM_EPS = 1e-5
BF = jnp.bfloat16
F32 = jnp.float32
SCALE = HD ** -0.5
LOG2E = 1.4426950408889634


def slot_of(branch, cell):
    row, col = divmod(cell, GRID)
    if branch == 0:
        return row * 16 + col
    stripe, inner = divmod(col, SPLIT)
    return stripe * PAD + row * 8 + inner


def spread_tables():
    into = np.zeros((2, 4, 2 * PAD, 208), np.float32)
    for branch in range(2):
        for cell in range(CELLS):
            for j in range(4):
                into[branch, j, slot_of(branch, cell), cell + 4 * j] = 1.0
    return into.reshape(8, 2 * PAD, 208), into.transpose(0, 1, 3, 2).reshape(8, 208, 2 * PAD)


def key_mask():
    mask = np.full((2, PAD, 128), -1e30, np.float32)
    for branch in range(2):
        for cell in range(CELLS):
            slot = slot_of(branch, cell)
            if slot < PAD:
                mask[branch, slot] = 0.0
    return mask


def lane_table():
    table = np.zeros((512, 512), np.float32)
    for t in range(4):
        for j in range(4):
            for e in range(HD):
                table[t * 128 + j * 32 + e, j * 128 + t * 32 + e] = 1.0
    return table


def dot(a, b):
    return lax.dot_general(a, b, (((1,), (0,)), ((), ())), preferred_element_type=F32)


def dot_nt(a, b):
    return lax.dot_general(a, b, (((1,), (1,)), ((), ())), preferred_element_type=F32)


def norm_stats(v):
    centre = jnp.mean(v, -1, keepdims=True)
    centred = v - centre
    spread = jnp.mean(centred * centred, -1, keepdims=True)
    rate = lax.rsqrt(spread + NORM_EPS)
    return centred * rate, rate


def norm_back(grad, gain, xhat, rate):
    gx = grad * gain
    first = jnp.mean(gx, -1, keepdims=True)
    second = jnp.mean(gx * xhat, -1, keepdims=True)
    return rate * (gx - first - xhat * second)


def fold8(v):
    return jnp.sum(v.reshape(v.shape[0] // 8, 8, v.shape[1]), axis=0)


def gelu_pair(h):
    e = jnp.exp2(h * h * (-0.5 * LOG2E))
    t = 1.0 / (1.0 + (0.3275911 * math.sqrt(0.5)) * jnp.abs(h))
    poly = t * (0.5 * 0.254829592 + t * (0.5 * -0.284496736 + t * (0.5 * 1.421413741 + t * (0.5 * -1.453152027 + t * (0.5 * 1.061405429)))))
    tail = poly * e
    phi = jnp.where(h < 0, tail, 1.0 - tail)
    return h * phi, phi + h * e * (1.0 / math.sqrt(2 * math.pi))


def head_masks():
    lane = lax.broadcasted_iota(jnp.int32, (128, 128), 1) // HD
    return [jnp.where(lane == h, 1.0, 0.0).astype(BF) for h in range(4)]


def head_blocks(z, masks):
    zp = jnp.concatenate([z, jnp.zeros((16, 128), BF)], 0)
    return [zp * masks[h] for h in range(4)]


def col_shift(v):
    return pltpu.roll(v, 1, 0), v, pltpu.roll(v, PAD - 1, 0)


def row_up(u, pitch):
    return jnp.concatenate([u[pitch:], jnp.zeros((pitch, 128), F32)], 0)


def row_down(u, pitch):
    return jnp.concatenate([jnp.zeros((pitch, 128), F32), u[:-pitch]], 0)


def window_sum(v, taps, pitch):
    cols = col_shift(v)
    rows = [sum(taps[3 * i + j] * cols[j] for j in range(3)) for i in range(3)]
    return row_down(rows[0], pitch) + rows[1] + row_up(rows[2], pitch)


def window_sum_back(d, taps, pitch):
    cols = col_shift(d)
    rows = [sum(taps[3 * i + j] * cols[2 - j] for j in range(3)) for i in range(3)]
    return row_up(rows[0], pitch) + rows[1] + row_down(rows[2], pitch)


def tap_sums(d, v, pitch):
    cols = col_shift(v)
    out = []
    for i in range(3):
        moved = row_up(d, pitch) if i == 0 else (d if i == 1 else row_down(d, pitch))
        for j in range(3):
            out.append(fold8(moved * cols[j]))
    return out


MT = 784
NT_TILES = 3
MESH = pl.DeviceIdType.MESH


def block_kernel(batch, tensor, linked, *refs):
    r = dict(zip(NAMES, refs))
    x_ref, cot_ref, out_ref, ig_ref = r["x"], r["cot"], r["out"], r["ig"]
    into_ref, outof_ref, lane_ref, mask_ref = r["into"], r["outof"], r["lane"], r["mask"]
    norm_ref, lepe_ref, bias_ref = r["norm"], r["lepe"], r["bias"]
    gather_s = [r["g0"], r["g1"], r["gm"]]
    wire_s = [r["h0"], r["h1"], r["hm"]]
    in_s = [r["in0"], r["in1"], r["inm"]]
    mid_s = [r["mid0"], r["mid1"], r["midm"]]
    last_s = [r["last0"], r["last1"], r["lastm"]]
    fc1_s, fc2_s, wcat_s, proj_s, lepe_s = r["fc1"], r["fc2"], r["wcat"], r["projw"], r["lepew"]
    n1_s, n1t_s, cott_s, q_s, k_s, v_s, a_s, p_s = r["n1"], r["n1t"], r["cott"], r["q"], r["k"], r["v"], r["a"], r["p"]
    att_s, n2_s, act_s, gh_s, gb_s, ga_s, do_s = r["att"], r["n2"], r["act"], r["gh"], r["gb"], r["ga"], r["do"]
    acc_s, tacc_s, s_s, ds_s, dk_s, dv_s = r["acc"], r["tacc"], r["s"], r["ds"], r["dk"], r["dv"]
    sq_s, rows_s = r["sq"], r["rows"]
    shard_ref, total_ref, size_ref = r["shard"], r["total"], r["size"]
    dq_s, dqkv_s = a_s, gh_s

    rows = x_ref.shape[0]
    images = rows // CELLS
    chunks = images // 4
    depth = r["m1"].shape[0]

    loads = []
    for n, name in enumerate(("x", "cot", "into", "lane", "outof")):
        copy = pltpu.make_async_copy(r[name + "_hbm"], r[name], r["load_sem"].at[n])
        copy.start()
        loads.append(copy)

    if linked:
        me_b, me_t = lax.axis_index("batch"), lax.axis_index("tensor")
    else:
        me_b, me_t = 0, 0
    along_b = [(lax.rem(me_b + k, batch), me_t) for k in range(1, batch)]
    along_t = [(me_b, lax.rem(me_t + k, tensor)) for k in range(1, tensor)]
    beyond = [(lax.rem(me_b + k, batch), lax.rem(me_t + n, tensor)) for n in range(1, tensor) for k in range(1, batch)]
    sent = []

    class Push:
        def __init__(self, source, dest, peer, send, recv):
            self.copy = None
            if linked:
                self.copy = pltpu.make_async_remote_copy(src_ref=source, dst_ref=dest, send_sem=send, recv_sem=recv, device_id=peer, device_id_type=MESH)
                self.copy.start()

        def wait_recv(self):
            if self.copy is not None:
                self.copy.wait_recv()

        def wait_send(self):
            if self.copy is not None:
                self.copy.wait_send()

    def push(source, dest, peer, sems, *at):
        got = Push(source, dest, peer, r[sems + "_s"].at[at], r[sems + "_r"].at[at])
        sent.append(got)
        return got

    def arrive(copies):
        for copy in copies:
            copy.wait_recv()

    q, k, v, p = r["qkv"][0], r["qkv"][1], r["qkv"][2], r["proj"][...]
    for b in range(2):
        at = slice(b * HD, (b + 1) * HD)
        gather_s[b][me_b, me_t] = jnp.concatenate([q[:, at], k[:, at], v[:, at], p[:, at]], 1).astype(BF)
    gather_s[2][me_b, me_t, :, 0:256] = r["m1"][...].astype(BF)
    gather_s[2][me_b, me_t, :, 256:512] = r["m2"][...].astype(BF)
    if linked:
        barrier = pltpu.get_barrier_semaphore()
        everyone = along_b + along_t + beyond
        for peer in everyone:
            pl.semaphore_signal(barrier, inc=1, device_id=peer, device_id_type=MESH)
        pl.semaphore_wait(barrier, len(everyone))

    plane = [(2 * k, n) for n in range(tensor) for k in range(batch // 2) if k + n > 0]
    pair = (me_b + 1 - 2 * lax.rem(me_b, 2), me_t)
    mine = gather_s[0].at[me_b, me_t]
    first = [push(mine, mine, (lax.rem(me_b + k, batch), lax.rem(me_t + n, tensor)), "gp", at) for at, (k, n) in enumerate(plane)]
    paired = [push(mine, mine, pair, "gc", 0)]

    acc_s[...] = jnp.zeros_like(acc_s)
    lp = lepe_ref[...]
    lepe_s[0:10, :] = jnp.concatenate([lp[:, h * 64 + b * 32:h * 64 + b * 32 + 32] for b in range(2) for h in range(4)], 1)
    loads[0].wait()

    @pl.loop(0, NT_TILES, unroll=NT_TILES)
    def _(i):
        sl = pl.ds(pl.multiple_of(i * MT, 16), MT)
        xhat, rate = norm_stats(x_ref[sl, :].astype(F32))
        n1_s[sl, :] = (xhat * norm_ref[0:1, :] + norm_ref[1:2, :]).astype(BF)

    masks = head_masks()

    def spread_rows(b, c, j, source, lanes):
        return dot(into_ref[b * 4 + j], source[pl.ds(pl.multiple_of(c * 784 + 192 * j, 16), 208), lanes]).astype(BF)

    for copy in loads[1:]:
        copy.wait()
    n1t_s[...] = jnp.transpose(n1_s[...])

    for c in range(chunks):
        for j in range(4):
            for b in range(2):
                rows_s[b, c * 4 + j] = spread_rows(b, c, j, n1_s, slice(None))

    for at, (k, n) in enumerate(plane):
        first[at].wait_recv()
        slot = gather_s[0].at[lax.rem(me_b + batch - k, batch), lax.rem(me_t + tensor - n, tensor)]
        paired.append(push(slot, slot, pair, "gc", at + 1))
    got = {0: paired}
    over = [[push(gather_s[n].at[me_b, me_t], gather_s[n].at[me_b, me_t], peer, "gt", n - 1, k) for k, peer in enumerate(along_t)] for n in (1, 2)]
    cott_s[...] = jnp.transpose(cot_ref[...])

    def onward():
        for n in (1, 2):
            arrive(over[n - 1])
            row = gather_s[n].at[me_b]
            got[n] = [push(row, row, peer, "gb", n - 1, k) for k, peer in enumerate(along_b)]

    def dense_rows(b, source, dest, width):
        lanes = slice(b * width, (b + 1) * width)

        for c in range(chunks):
            tail = None
            for j in range(4):
                both = jnp.concatenate([source(c * 8 + j * 2), source(c * 8 + j * 2 + 1)], 0)
                got = dot(outof_ref[b * 4 + j], both)
                head = got[0:16] if tail is None else got[0:16] + tail
                base = c * 784 + 192 * j
                dest[pl.ds(pl.multiple_of(base, 16), 16), lanes] = head.astype(BF)
                dest[pl.ds(pl.multiple_of(base + 16, 16), 176), lanes] = got[16:192].astype(BF)
                tail = got[192:208]
                if j == 3:
                    dest[pl.ds(pl.multiple_of(base + 192, 16), 16), lanes] = tail.astype(BF)

    def scores_stage(b, s, at):
        s_s[s] = dot_nt(k_s[b, at], jnp.concatenate(head_blocks(q_s[b, at], masks), 0))

    def soft_stage(b, s, at):
        for h in range(4):
            lanes = slice(h * 128, (h + 1) * 128)
            score = s_s[s, :, lanes] * (SCALE * LOG2E) + mask_ref[b]
            e = jnp.exp2(score - jnp.max(score, 0, keepdims=True))
            p_s[b, at, :, lanes] = (e * (1.0 / jnp.sum(e, 0, keepdims=True))).astype(BF)

    def mix_stage(b, s, at):
        pitch = 16 - 8 * b
        v = v_s[b, at]
        vt = jnp.transpose(v)
        ots = [dot(vt[h * HD:(h + 1) * HD], p_s[b, at, :, h * 128:(h + 1) * 128]) for h in range(4)]
        mixed = jnp.transpose(jnp.concatenate(ots, 0))[:PAD]
        taps = [lepe_s[n:n + 1, b * 128:(b + 1) * 128] for n in range(10)]
        local = window_sum(v.astype(F32), taps, pitch) + taps[9]
        a_s[b, at] = (mixed + local).astype(BF)

    def qkv_stage(b):
        for c in range(images // 4):
            flat = jnp.concatenate([rows_s[b, c * 4 + j] for j in range(4)], 0)
            value = dot(flat, wcat_s[:, b * 384:b * 384 + 384]).astype(BF)
            for dest, at in ((q_s, 0), (k_s, 128), (v_s, 256)):
                for n in range(8):
                    dest[b, c * 8 + n] = value[n * PAD:(n + 1) * PAD, at:at + 128]

    for b in range(2):
        arrive(got[b])
        packed = jnp.concatenate([jnp.concatenate([gather_s[b][n, t] for n in range(batch)], 0) for t in range(4)], 1)
        work = dot(packed, lane_ref[...]).astype(BF)
        wcat_s[:, b * 384:(b + 1) * 384] = work[:, 0:384]
        proj_s[:, b * 128:(b + 1) * 128] = work[:, 384:512]
        qkv_stage(b)
        if b == 0:
            onward()
        for s in range(2):
            scores_stage(b, s, s)

        @pl.loop(0, images, unroll=2)
        def _(i):
            before, after = jnp.maximum(i - 1, 0), jnp.minimum(i + 1, images - 1)
            for s in range(2):
                mix_stage(b, s, before * 2 + s)
                soft_stage(b, s, i * 2 + s)
                scores_stage(b, s, after * 2 + s)

        for s in range(2):
            mix_stage(b, s, images * 2 - 2 + s)
        dense_rows(b, lambda at: a_s[b, at], att_s, 128)

    arrive(got[2])
    for t in range(4):
        for n in range(batch):
            at = slice(n * depth, (n + 1) * depth)
            fc1_s[at, t * 256:(t + 1) * 256] = gather_s[2][n, t, :, 0:256]
            fc2_s[at, t * 256:(t + 1) * 256] = gather_s[2][n, t, :, 256:512]

    @pl.loop(0, NT_TILES, unroll=NT_TILES)
    def _(i):
        sl = pl.ds(pl.multiple_of(i * MT, 16), MT)
        one = dot_nt(att_s[sl, :], proj_s[...]) + norm_ref[2:3, :]
        middle = x_ref[sl, :].astype(F32) + one
        xhat, rate = norm_stats(middle)
        n2 = (xhat * norm_ref[3:4, :] + norm_ref[4:5, :]).astype(BF)
        n2_s[sl, :] = n2
        cot = cot_ref[sl, :]
        two = jnp.zeros((MT, D), F32)
        gn = jnp.zeros((MT, D), F32)
        for f in range(4):
            fs = slice(f * 256, (f + 1) * 256)
            hidden = dot(n2, fc1_s[:, fs]) + jnp.concatenate([bias_ref[2 * f:2 * f + 1, :], bias_ref[2 * f + 1:2 * f + 2, :]], 1)
            gelu, slope = gelu_pair(hidden)
            act = gelu.astype(BF)
            act_s[sl, fs] = act
            two = two + dot_nt(act, fc2_s[:, fs])
            gh_f = dot(cot, fc2_s[:, fs]) * slope
            gh = gh_f.astype(BF)
            gh_s[sl, fs] = gh
            acc_s[10 + f] += fold8(gh.astype(F32))
            gn = gn + dot_nt(gh, fc1_s[:, fs])
        two = two + norm_ref[5:6, :]
        result = middle + two
        out_ref[sl, :] = result.astype(BF)
        acc_s[6] += fold8(one * one)
        acc_s[7] += fold8(middle * middle)
        acc_s[8] += fold8(two * two)
        acc_s[9] += fold8(result * result)
        cotf = cot.astype(F32)
        acc_s[5] += fold8(cotf)
        acc_s[3] += fold8(gn * xhat)
        acc_s[4] += fold8(gn)
        gm = cotf + norm_back(gn, norm_ref[3:4, :], xhat, rate)
        ig_ref[sl, :] = gm
        gb = gm.astype(BF)
        gb_s[sl, :] = gb
        acc_s[2] += fold8(gb.astype(F32))
        ga_s[sl, :] = dot(gb, proj_s[...]).astype(BF)

    stores = [pltpu.make_async_copy(out_ref, r["out_hbm"], r["store_sem"].at[0])]
    stores[0].start()

    def put_rows(ref, value, t, off):
        for n in range(batch):
            ref[n, t, :, off:off + value.shape[1]] = value[n * depth:(n + 1) * depth]

    def scatter_sum(n):
        return [push(wire_s[n].at[peer[0]], in_s[n].at[k], peer, "rb", n, k) for k, peer in enumerate(along_b)]

    def add_up(n, copies):
        arrive(copies)
        for t in range(tensor):
            value = wire_s[n][me_b, t].astype(F32)
            for k in range(batch - 1):
                value = value + in_s[n][k, t].astype(F32)
            mid_s[n][t] = value.astype(BF)
        return [push(mid_s[n].at[peer[1]], last_s[n].at[k], peer, "rt", n, k) for k, peer in enumerate(along_t)]

    def finish(n, copies, off):
        arrive(copies)
        shard = mid_s[n][me_t].astype(F32)
        for k in range(tensor - 1):
            shard = shard + last_s[n][k].astype(F32)
        shard_ref[:, off:off + shard.shape[1]] = shard
        squares = fold8(shard * shard)
        return sum(squares[:, m * 128:(m + 1) * 128] for m in range(shard.shape[1] // 128))

    n2t = jnp.transpose(n2_s[...])
    n1_s_t = r["n2t"]
    n1_s_t[...] = n2t
    for left, right, off in ((n1_s_t, gh_s, 0), (cott_s, act_s, 256)):
        for t in range(4):
            put_rows(wire_s[2], dot(left[...], right[:, t * 256:(t + 1) * 256]).astype(BF), t, off)
    sums_m = scatter_sum(2)
    gp = dot(jnp.transpose(gb_s[...]), att_s[...]).astype(BF)
    r["gp"][...] = gp

    def spread_do(b):
        for c in range(chunks):
            for j in range(4):
                rows_in = spread_rows(b, c, j, ga_s, slice(b * 128, (b + 1) * 128))
                for s in range(2):
                    do_s[b, c * 8 + j * 2 + s] = rows_in[s * PAD:(s + 1) * PAD]

    def dprobs_stage(b, s, at):
        s_s[s] = dot_nt(v_s[b, at], jnp.concatenate(head_blocks(do_s[b, at], masks), 0))

    def dscores_stage(b, s, at):
        for h in range(4):
            lanes = slice(h * 128, (h + 1) * 128)
            pf = p_s[b, at, :, lanes].astype(F32)
            t = pf * s_s[s, :, lanes]
            ds_s[s, :, lanes] = (t - pf * jnp.sum(t, 0, keepdims=True)).astype(BF)

    def dqkv_stage(b, s, at):
        pitch = 16 - 8 * b
        q, k, v, do = q_s[b, at], k_s[b, at], v_s[b, at], do_s[b, at]
        kt = jnp.transpose(k)
        dqt = [dot(kt[h * HD:(h + 1) * HD], ds_s[s, :, h * 128:(h + 1) * 128]) for h in range(4)]
        dv = dot(p_s[b, at], jnp.concatenate(head_blocks(do, masks), 0))
        dk = dot(ds_s[s], jnp.concatenate(head_blocks(q, masks), 0))
        dq = jnp.transpose(jnp.concatenate(dqt, 0))[:PAD]
        taps = [lepe_s[n:n + 1, b * 128:(b + 1) * 128] for n in range(10)]
        dof, vf = do.astype(F32), v.astype(F32)
        dv = dv + window_sum_back(dof, taps, pitch)
        for n, part in enumerate(tap_sums(dof, vf, pitch)):
            tacc_s[b, n] += part
        tacc_s[b, 9] += fold8(dof)
        dq_s[b, at] = (dq * SCALE).astype(BF)
        dk_s[b, at] = (dk * SCALE).astype(BF)
        dv_s[b, at] = dv.astype(BF)

    def branch_back(b):
        spread_do(b)
        for s in range(2):
            dprobs_stage(b, s, s)

        @pl.loop(0, images, unroll=2)
        def _(i):
            before, after = jnp.maximum(i - 1, 0), jnp.minimum(i + 1, images - 1)

            @pl.when(i == 1)
            def _():
                tacc_s[b] = jnp.zeros((10, 8, 128), F32)

            for s in range(2):
                dqkv_stage(b, s, before * 2 + s)
                dscores_stage(b, s, i * 2 + s)
                dprobs_stage(b, s, after * 2 + s)

        for s in range(2):
            dqkv_stage(b, s, images * 2 - 2 + s)
        if b == 1:
            smalls.append(small_out("l", pairs_of_taps(1)))
        dense_rows(b, lambda at: jnp.concatenate([dq_s[b, at], dk_s[b, at], dv_s[b, at]], 1), dqkv_s, 384)
        gw = dot(n1t_s[...], dqkv_s[:, b * 384:(b + 1) * 384]).astype(BF)
        packed = dot_nt(jnp.concatenate([gw, r["gp"][:, b * 128:(b + 1) * 128]], 1), lane_ref[...]).astype(BF)
        for t in range(4):
            for n in range(batch):
                part = packed[n * depth:(n + 1) * depth, t * 128:(t + 1) * 128]
                if b == 0:
                    wire_s[0][n, t] = part
                else:
                    wire_s[1][n % 2, n // 2, t] = part

    def pairs_of_taps(b):
        taps = jnp.sum(tacc_s[b], axis=1)
        return [jnp.concatenate([taps[2 * n:2 * n + 1], taps[2 * n + 1:2 * n + 2]], 1) for n in range(5)]

    def small_out(g, parts):
        own = r["small" + g]
        own[...] = jnp.zeros_like(own)
        for n, part in enumerate(parts):
            own[n:n + 1, :] = part
        r["smallb" + g][me_b] = own[...]
        return [push(own, r["smallb" + g].at[me_b], peer, "sb" + g, k) for k, peer in enumerate(along_b)]

    def in_order(ref, count):
        part = ref[0]
        for n in range(1, count):
            part = part + ref[n]
        return part

    def small_on(g, copies):
        arrive(copies)
        part = in_order(r["smallb" + g], batch)
        own = r["smalln" + g]
        own[...] = part
        r["smallt" + g][me_t] = part
        return [push(own, r["smallt" + g].at[me_t], peer, "st" + g, k) for k, peer in enumerate(along_t)]

    smalls = []
    branch_back(0)
    sums_0 = scatter_sum(0)
    sums = jnp.sum(acc_s[2:14], axis=1)
    smalls.append(small_out("e", [sums[n:n + 1] for n in range(12)] + pairs_of_taps(0)))
    branch_back(1)
    side = lax.rem(me_b, 2)
    across = push(wire_s[1].at[1 - side], in_s[1], pair, "rc", 0)
    last_m = add_up(2, sums_m)
    across.wait_recv()
    for n in range(batch // 2):
        mid_s[1][n] = (wire_s[1][side, n].astype(F32) + in_s[1][n].astype(F32)).astype(BF)
    half = lax.div(me_b, 2)
    last_1 = []
    for at, (k, n) in enumerate(plane):
        to_b, to_t = lax.rem(half + k // 2, batch // 2), lax.rem(me_t + n, tensor)
        last_1.append(push(mid_s[1].at[to_b, to_t], last_s[1].at[at], (2 * to_b + side, to_t), "rp", at))
    last_0 = add_up(0, sums_0)
    early, late = small_on("e", smalls[0]), small_on("l", smalls[1])

    @pl.loop(0, NT_TILES, unroll=NT_TILES)
    def _(i):
        sl = pl.ds(pl.multiple_of(i * MT, 16), MT)
        gn = dot_nt(dqkv_s[sl, 0:768], wcat_s[...])
        xhat, rate = norm_stats(x_ref[sl, :].astype(F32))
        acc_s[0] += fold8(gn * xhat)
        acc_s[1] += fold8(gn)
        ig_ref[sl, :] = ig_ref[sl, :] + norm_back(gn, norm_ref[0:1, :], xhat, rate)

    stores.append(pltpu.make_async_copy(ig_ref, r["ig_hbm"], r["store_sem"].at[1]))
    stores[1].start()
    lanes = finish(2, last_m, 0) + finish(0, last_0, 512)
    sums = jnp.sum(acc_s[0:2], axis=1)
    arrive(last_1)
    shard = mid_s[1][half, me_t].astype(F32)
    for at in range(len(plane)):
        shard = shard + last_s[1][at].astype(F32)
    shard_ref[:, 640:768] = shard
    lanes = jnp.sum(lanes + fold8(shard * shard), 0, keepdims=True)
    own = r["all"]
    own[...] = jnp.concatenate([lanes, sums[0:1], sums[1:2]], 1)
    me = me_b * tensor + me_t
    sq_s[me] = own[...]
    everyone = along_b + along_t + beyond
    square = [push(own, sq_s.at[me], peer, "sq", k) for k, peer in enumerate(everyone)]
    arrive(early)
    arrive(late)
    first_sums, last_sums = in_order(r["smallte"], tensor), in_order(r["smalltl"], tensor)
    total_ref[2:14, :] = first_sums[0:12]
    for n in range(10):
        halves = [part[:, n % 2 * 128:n % 2 * 128 + 128] for part in (first_sums[12 + n // 2:13 + n // 2], last_sums[n // 2:1 + n // 2])]
        total_ref[14 + n:15 + n, :] = jnp.concatenate([halves[b][:, h * HD:(h + 1) * HD] for h in range(4) for b in range(2)], 1)
    row = lax.broadcasted_iota(jnp.int32, first_sums.shape, 0)
    first_sums = jnp.where((row < 4) | (row >= 8), first_sums, 0.0)
    vector = jnp.sum(first_sums * first_sums, 0, keepdims=True) + jnp.sum(last_sums * last_sums, 0, keepdims=True)
    vector = jnp.sum(vector, 1, keepdims=True)
    arrive(square)
    for copy in sent:
        copy.wait_send()
    whole = in_order(sq_s, batch * tensor)
    total_ref[0:1, :] = whole[:, 128:384]
    total_ref[1:2, :] = whole[:, 384:640]
    lane = lax.broadcasted_iota(jnp.int32, whole.shape, 1)
    matrix = jnp.sum(jnp.where(lane < 128, whole, whole * whole), 1, keepdims=True)
    size_ref[...] = jnp.broadcast_to(jnp.sqrt(matrix + vector), (8, 128))
    for copy in stores:
        copy.wait()


NAMES_IN = ["x_hbm", "cot_hbm", "qkv", "proj", "m1", "m2", "norm", "lepe", "bias", "into_hbm", "outof_hbm", "mask", "lane_hbm"]
NAMES_OUT = ["out_hbm", "ig_hbm", "shard", "total", "size"]


def scratch_list(batch, tensor, rows, depth):
    n = rows // CELLS * 2
    V = pltpu.VMEM
    dma = pltpu.SemaphoreType.DMA
    stripe = (2, n, PAD, 128)
    items = [
        ("x", V((rows, D), BF)), ("cot", V((rows, D), BF)), ("out", V((rows, D), BF)), ("ig", V((rows, D), F32)),
        ("into", V((8, 2 * PAD, 208), BF)), ("outof", V((8, 208, 2 * PAD), BF)), ("lane", V((512, 512), BF)),
    ]
    for name, width in (("0", 128), ("m", 512)):
        items += [
            ("g" + name, V((batch, tensor, depth, width), BF)), ("h" + name, V((batch, tensor, depth, width), BF)), ("in" + name, V((batch - 1, tensor, depth, width), BF)),
            ("mid" + name, V((tensor, depth, width), BF)), ("last" + name, V((tensor - 1, depth, width), BF)),
        ]
    half = (batch // 2, tensor, depth, 128)
    items += [("g1", V((batch, tensor, depth, 128), BF)), ("h1", V((2,) + half, BF)), ("in1", V(half, BF)), ("mid1", V(half, BF)), ("last1", V((batch // 2 * tensor - 1, depth, 128), BF))]
    for name, count in (("e", 24), ("l", 8)):
        items += [("small" + name, V((count, D), F32)), ("smallb" + name, V((batch, count, D), F32)), ("smalln" + name, V((count, D), F32)), ("smallt" + name, V((tensor, count, D), F32))]
    items += [
        ("sq", V((batch * tensor, 1, 640), F32)), ("all", V((1, 640), F32)), ("rows", V((2, n // 2, 2 * PAD, D), BF)),
        ("fc1", V((D, FF), BF)), ("fc2", V((D, FF), BF)), ("wcat", V((D, 768), BF)), ("projw", V((D, D), BF)), ("lepew", V((16, D), F32)), ("gp", V((D, D), BF)),
        ("n1", V((rows, D), BF)), ("n1t", V((D, rows), BF)), ("cott", V((D, rows), BF)), ("n2t", V((D, rows), BF)),
        ("q", V(stripe, BF)), ("k", V(stripe, BF)), ("v", V(stripe, BF)), ("a", V(stripe, BF)),
        ("p", V((2, n, PAD, 512), BF)), ("att", V((rows, D), BF)), ("n2", V((rows, D), BF)), ("act", V((rows, FF), BF)), ("gh", V((rows, FF), BF)),
        ("gb", V((rows, D), BF)), ("ga", V((rows, D), BF)), ("do", V(stripe, BF)),
        ("acc", V((14, 8, D), F32)), ("tacc", V((2, 10, 8, 128), F32)),
        ("s", V((2, PAD, 512), F32)), ("ds", V((2, PAD, 512), BF)), ("dk", V(stripe, BF)), ("dv", V(stripe, BF)),
        ("load_sem", dma((5,))), ("store_sem", dma((2,))),
    ]
    b, t = batch - 1, tensor - 1
    for name, shape in (("gp", (batch // 2 * tensor - 1,)), ("gc", (batch // 2 * tensor,)), ("gt", (2, t)), ("gb", (2, b)), ("rb", (3, b)), ("rt", (3, t)), ("rc", (1,)), ("rp", (batch // 2 * tensor - 1,)), ("sbe", (b,)), ("ste", (t,)), ("sbl", (b,)), ("stl", (t,)), ("sq", (batch * tensor - 1,))):
        items += [(name + "_s", dma(shape)), (name + "_r", dma(shape))]
    return items


NAMES = NAMES_IN + NAMES_OUT + [name for name, _ in scratch_list(8, 4, 2352, 32)]


def block_call(batch, tensor, linked, x, cot, qkv, proj, fc1, fc2, norm, lepe, bias):
    rows, depth = x.shape[0], fc1.shape[0]
    into, outof = spread_tables()
    args = (x, cot, qkv, proj, fc1, fc2, norm, lepe, bias, jnp.asarray(into, BF), jnp.asarray(outof, BF), jnp.asarray(key_mask()), jnp.asarray(lane_table(), BF))
    V = pl.BlockSpec(memory_space=pltpu.VMEM)
    H = pl.BlockSpec(memory_space=pl.ANY)
    extra = dict(collective_id=0, has_side_effects=True) if linked else {}
    return pl.pallas_call(
        functools.partial(block_kernel, batch, tensor, linked),
        out_shape=(
            jax.ShapeDtypeStruct((rows, D), BF),
            jax.ShapeDtypeStruct((rows, D), F32),
            jax.ShapeDtypeStruct((depth, 768), F32),
            jax.ShapeDtypeStruct((24, D), F32),
            jax.ShapeDtypeStruct((8, 128), F32),
        ),
        in_specs=[H, H] + [V] * 7 + [H, H, V, H],
        out_specs=(H, H, V, V, V),
        scratch_shapes=[shape for _, shape in scratch_list(batch, tensor, rows, depth)],
        compiler_params=pltpu.CompilerParams(vmem_limit_bytes=62 * 2**20, **extra),
    )(*args)


def adam(master, first, second, clipped, rate, decay):
    first = BETA_ONE * first + (1.0 - BETA_ONE) * clipped
    second = BETA_TWO * second + (1.0 - BETA_TWO) * clipped * clipped
    hat = first * (1.0 / (1.0 - BETA_ONE**STEP))
    spread = second * (1.0 / (1.0 - BETA_TWO**STEP))
    return master - rate * (hat / (jnp.sqrt(spread) + ADAM_EPS) + decay * master), first, second


def update_kernel(
    all_tokens, out_in, ig_in, shard_ref, total_ref, norm_ref,
    qkv_w, qkv_m, proj_w, proj_m, fc1_w, fc1_m, fc2_w, fc2_m, norm_w, norm_m, lepe_w, lepe_m, bias_w, bias_m,
    out_o, ig_o, qkv_g, qkv_n, qkv_l, qkv_o, proj_g, proj_n, proj_l, proj_o, fc1_g, fc1_n, fc1_l, fc1_o, fc2_g, fc2_n, fc2_l, fc2_o,
    norm_g, norm_n, norm_o, lepe_g, lepe_n, lepe_o, bias_g, bias_n, bias_o, size_o, rms_o, out_s, ig_s, sems,
):
    moves = []
    for source, held, dest in ((out_in, out_s, out_o), (ig_in, ig_s, ig_o)):
        step = held.shape[0] // 3
        for n in range(3):
            at = pl.ds(n * step, step)
            moves.append([pltpu.make_async_copy(source.at[at], held.at[at], sems.at[0, len(moves)]), pltpu.make_async_copy(held.at[at], dest.at[at], sems.at[1, len(moves)])])
    for into, _ in moves:
        into.start()
    size = norm_ref[0:1, 0:1]
    factor = jnp.minimum(1.0, CLIP_SCALE * math.sqrt(NPARAM) / (size + 1e-06))
    size_o[...] = size

    def one(grad, w, m, g_o, n_o, l_o, m_o, at, rate, decay, pair=lambda n, at: (n,) + at):
        clipped = grad * factor
        new, first, second = adam(w[at], m[pair(0, at)], m[pair(1, at)], clipped, rate, decay)
        g_o[at] = clipped
        n_o[at] = new
        if l_o is not None:
            l_o[at] = new.astype(BF)
        m_o[pair(0, at)] = first
        m_o[pair(1, at)] = second

    for into, away in moves:
        into.wait()
        away.start()
    every = (slice(None), slice(None))
    middle = lambda n, at: (at[0], n, at[1])
    one(shard_ref[:, 0:256], fc1_w, fc1_m, fc1_g, fc1_n, fc1_l, fc1_o, every, RATE_MATRIX, DECAY_RATE)
    one(shard_ref[:, 256:512], fc2_w, fc2_m, fc2_g, fc2_n, fc2_l, fc2_o, every, RATE_MATRIX, DECAY_RATE)
    lanes = lambda j: jnp.concatenate([shard_ref[:, 512 + 32 * j:544 + 32 * j], shard_ref[:, 640 + 32 * j:672 + 32 * j]], 1)
    for j in range(3):
        one(lanes(j), qkv_w, qkv_m, qkv_g, qkv_n, qkv_l, qkv_o, (j,) + every, RATE_MATRIX, DECAY_RATE)
    one(lanes(3), proj_w, proj_m, proj_g, proj_n, proj_l, proj_o, every, RATE_MATRIX, DECAY_RATE)
    one(total_ref[0:6], norm_w, norm_m, norm_g, norm_n, None, norm_o, every, RATE_VECTOR, 0.0, middle)
    one(total_ref[14:24], lepe_w, lepe_m, lepe_g, lepe_n, None, lepe_o, every, RATE_VECTOR, 0.0, middle)
    for f in range(8):
        at = (slice(f, f + 1), slice(None))
        part = total_ref[10 + f // 2:11 + f // 2, 128 * (f % 2):128 * (f % 2) + 128]
        one(part, bias_w, bias_m, bias_g, bias_n, None, bias_o, at, RATE_VECTOR, 0.0, middle)
    lane = lax.broadcasted_iota(jnp.int32, (1, 4), 1)
    sums = jnp.zeros((1, 4), F32)
    for n in range(4):
        sums = jnp.where(lane == n, jnp.sum(total_ref[6 + n:7 + n], 1, keepdims=True), sums)
    rms_o[...] = jnp.sqrt(sums * (1.0 / (all_tokens * D)))
    for _, away in moves:
        away.wait()


def update_call(all_tokens, out, ig, shard, total, norm, arrays):
    V = pltpu.VMEM
    like = lambda a, dt=F32: jax.ShapeDtypeStruct(a.shape, dt)
    outs = [like(out, BF), like(ig)]
    H = pl.BlockSpec(memory_space=pl.ANY)
    for n in range(4):
        w, m = arrays[2 * n], arrays[2 * n + 1]
        outs += [like(w), like(w), like(w, BF), like(m)]
    for n in range(4, 7):
        w, m = arrays[2 * n], arrays[2 * n + 1]
        outs += [like(w), like(w), like(m)]
    outs += [jax.ShapeDtypeStruct((1, 1), F32), jax.ShapeDtypeStruct((1, 4), F32)]
    return list(pl.pallas_call(
        functools.partial(update_kernel, all_tokens),
        out_shape=tuple(outs),
        in_specs=[H, H] + [pl.BlockSpec(memory_space=V)] * (3 + len(arrays)),
        out_specs=tuple([H, H] + [pl.BlockSpec(memory_space=V)] * (len(outs) - 2)),
        scratch_shapes=[V(out.shape, BF), V(ig.shape, F32), pltpu.SemaphoreType.DMA((2, 6))],
        compiler_params=pltpu.CompilerParams(vmem_limit_bytes=60 * 2**20),
    )(out, ig, shard, total, norm, *arrays))


def flip(a):
    return jnp.swapaxes(a, -1, -2)


def shards(block_input, cotangent, *arrays):
    batch, tensor = lax.axis_size("batch"), lax.axis_size("tensor")
    arrays = list(arrays)
    for n in (2, 3, 6, 7):
        arrays[n] = flip(arrays[n])
    arrays[9], arrays[11] = jnp.swapaxes(arrays[9], 0, 1), jnp.swapaxes(arrays[11], 0, 1)
    arrays[12], arrays[13] = arrays[12].reshape(8, 128), jnp.swapaxes(arrays[13].reshape(2, 8, 128), 0, 1)
    qkv, _, proj, _, fc1, _, fc2, _, norm, _, lepe, _, bias, _ = arrays
    output, input_grad, shard, total, size = block_call(batch, tensor, True, block_input, cotangent, qkv, proj, fc1, fc2, norm, lepe, bias)
    output, input_grad, *got = update_call(block_input.shape[0] * batch * tensor, output, input_grad, shard, total, size, arrays)
    for n in (4, 5, 6, 7, 12, 13, 14, 15):
        got[n] = flip(got[n])
    got[18], got[21] = jnp.swapaxes(got[18], 0, 1), jnp.swapaxes(got[21], 0, 1)
    got[22], got[23], got[24] = got[22].reshape(1024), got[23].reshape(1024), jnp.swapaxes(got[24], 0, 1).reshape(2, 1024)
    got[25], got[26] = got[25].reshape(()), got[26].reshape(4)
    return (output, input_grad, *got)


def solution(mesh):
    token, matrix, moment = P(("batch", "tensor"), None), P("batch", "tensor"), P(None, "batch", "tensor")
    back, back_moment = P("tensor", "batch"), P(None, "tensor", "batch")
    stack, stack_moment = P(None, "batch", "tensor"), P(None, None, "batch", "tensor")
    return jax.shard_map(
        shards,
        mesh=mesh,
        in_specs=(token, token, stack, stack_moment, back, back_moment, matrix, moment, back, back_moment) + (P(),) * 6,
        out_specs=(token, token) + (stack,) * 3 + (stack_moment,) + (back,) * 3 + (back_moment,) + (matrix,) * 3 + (moment,) + (back,) * 3 + (back_moment,) + (P(),) * 11,
        check_vma=False,
    )
```

time: 105 us -> 91.5 us (0.87)
  Pallas kernels: 104 us -> 90.4 us
    pallas_call x1, Pallas kernels: 99.2 us -> 85.2 us  [block_call(): pl.pallas_call(functools.partial(block_kernel, batch, tensor, linked), ou...]
where the time goes in v5:
time: 91.5 us; the launch traced here: 91.3 us
  Pallas kernels  90.4 us (99%)
    pallas_call x1, Pallas kernels, block_call(): pl.pallas_call(functools.partial(block_kernel, batch, tensor, linked), ou...  85.2 us
    pallas_call x1, Pallas kernels, update_call(): pl.pallas_call(functools.partial(update_kernel, all_tokens), out_shape=tu...  5.25 us

profile of v5, /device:TPU:0, one launch (start us, length us, event | category | flops | bytes accessed | tf_op | source)
XLA Modules:
  0.0 91.3 jit_solution(6587389443114731367)
XLA Ops:
  0.7 85.2 %shard_map.419 = (bf16[2352,256]{1,0:T(8,128)(2,1)}, f32[2352,256]{1,0:T(8,128)}, f32[32,768]{1,0:T(8,128)}, f32[24,256]{1,0:T(8,128)}, f32[8,128]{1,0:T(8,128)}) custom-call(bf16[2352,256]{1,0:T(8,128)(2,1)} %refs_0_.1, bf16[2352,256]{1,0:T(8,128)(2,1)} %refs_1_.1, f32[3,32,64]{2,1,0:T(8,128)} %qkv_w.1, f32[32,64]{1,0:T(8,128)} %bitcast.30, ...), custom_call_target="tpu_custom_call" | custom-call | tf_op jit(solution)/shard_map/pallas_call | solution.py:639
  85.8 5.2 %shard_map.420 = (bf16[2352,256]{1,0:T(8,128)(2,1)}, f32[2352,256]{1,0:T(8,128)}, f32[3,32,64]{2,1,0:T(8,128)}, f32[3,32,64]{2,1,0:T(8,128)}, bf16[3,32,64]{2,1,...) custom-call(bf16[2352,256]{1,0:T(8,128)(2,1)} %get-tuple-element.63., ...), custom_call_target="tpu_custom_call" | custom-call | tf_op jit(solution)/shard_map/pallas_call | solution.py:729

commit v6 on v5

--- a/solution.py
+++ b/solution.py
@@ -94,10 +94,7 @@
 
 def gelu_pair(h):
     e = jnp.exp2(h * h * (-0.5 * LOG2E))
-    t = 1.0 / (1.0 + (0.3275911 * math.sqrt(0.5)) * jnp.abs(h))
-    poly = t * (0.5 * 0.254829592 + t * (0.5 * -0.284496736 + t * (0.5 * 1.421413741 + t * (0.5 * -1.453152027 + t * (0.5 * 1.061405429)))))
-    tail = poly * e
-    phi = jnp.where(h < 0, tail, 1.0 - tail)
+    phi = 0.5 + 0.5 * lax.erf(h * math.sqrt(0.5))
     return h * phi, phi + h * e * (1.0 / math.sqrt(2 * math.pi))
 
 
@@ -247,6 +244,7 @@
     def spread_rows(b, c, j, source, lanes):
         return dot(into_ref[b * 4 + j], source[pl.ds(pl.multiple_of(c * 784 + 192 * j, 16), 208), lanes]).astype(BF)
 
+    over = [[push(gather_s[n].at[me_b, me_t], gather_s[n].at[me_b, me_t], peer, "gt", n - 1, k) for k, peer in enumerate(along_t)] for n in (1, 2)]
     for copy in loads[1:]:
         copy.wait()
     n1t_s[...] = jnp.transpose(n1_s[...])
@@ -261,7 +259,6 @@
         slot = gather_s[0].at[lax.rem(me_b + batch - k, batch), lax.rem(me_t + tensor - n, tensor)]
         paired.append(push(slot, slot, pair, "gc", at + 1))
     got = {0: paired}
-    over = [[push(gather_s[n].at[me_b, me_t], gather_s[n].at[me_b, me_t], peer, "gt", n - 1, k) for k, peer in enumerate(along_t)] for n in (1, 2)]
     cott_s[...] = jnp.transpose(cot_ref[...])
 
     def onward():
@@ -286,6 +283,13 @@
                 if j == 3:
                     dest[pl.ds(pl.multiple_of(base + 192, 16), 16), lanes] = tail.astype(BF)
 
+    def own_blocks(left, right):
+        parts = []
+        for g in range(2):
+            both = dot(left[64 * g:64 * g + 64], right[:, 256 * g:256 * g + 256])
+            parts += [both[0:32, 0:128], both[32:64, 128:256]]
+        return jnp.concatenate(parts, 0)
+
     def scores_stage(b, s, at):
         s_s[s] = dot_nt(k_s[b, at], jnp.concatenate(head_blocks(q_s[b, at], masks), 0))
 
@@ -300,8 +304,7 @@
         pitch = 16 - 8 * b
         v = v_s[b, at]
         vt = jnp.transpose(v)
-        ots = [dot(vt[h * HD:(h + 1) * HD], p_s[b, at, :, h * 128:(h + 1) * 128]) for h in range(4)]
-        mixed = jnp.transpose(jnp.concatenate(ots, 0))[:PAD]
+        mixed = jnp.transpose(own_blocks(vt, p_s[b, at]))[:PAD]
         taps = [lepe_s[n:n + 1, b * 128:(b + 1) * 128] for n in range(10)]
         local = window_sum(v.astype(F32), taps, pitch) + taps[9]
         a_s[b, at] = (mixed + local).astype(BF)
@@ -445,10 +448,9 @@
         pitch = 16 - 8 * b
         q, k, v, do = q_s[b, at], k_s[b, at], v_s[b, at], do_s[b, at]
         kt = jnp.transpose(k)
-        dqt = [dot(kt[h * HD:(h + 1) * HD], ds_s[s, :, h * 128:(h + 1) * 128]) for h in range(4)]
         dv = dot(p_s[b, at], jnp.concatenate(head_blocks(do, masks), 0))
         dk = dot(ds_s[s], jnp.concatenate(head_blocks(q, masks), 0))
-        dq = jnp.transpose(jnp.concatenate(dqt, 0))[:PAD]
+        dq = jnp.transpose(own_blocks(kt, ds_s[s]))[:PAD]
         taps = [lepe_s[n:n + 1, b * 128:(b + 1) * 128] for n in range(10)]
         dof, vf = do.astype(F32), v.astype(F32)
         dv = dv + window_sum_back(dof, taps, pitch)
@@ -464,8 +466,7 @@
         for s in range(2):
             dprobs_stage(b, s, s)
 
-        @pl.loop(0, images, unroll=2)
-        def _(i):
+        def step(i):
             before, after = jnp.maximum(i - 1, 0), jnp.minimum(i + 1, images - 1)
 
             @pl.when(i == 1)
@@ -476,6 +477,12 @@
                 dqkv_stage(b, s, before * 2 + s)
                 dscores_stage(b, s, i * 2 + s)
                 dprobs_stage(b, s, after * 2 + s)
+
+        pl.loop(0, images, unroll=2)(step)
+        if b == 1:
+            later["m"] = add_up(2, sums_m)
+            later["e"] = small_on("e", smalls[0])
+            later["0"] = add_up(0, sums_0)
 
         for s in range(2):
             dqkv_stage(b, s, images * 2 - 2 + s)
@@ -518,7 +525,7 @@
         r["smallt" + g][me_t] = part
         return [push(own, r["smallt" + g].at[me_t], peer, "st" + g, k) for k, peer in enumerate(along_t)]
 
-    smalls = []
+    smalls, later = [], {}
     branch_back(0)
     sums_0 = scatter_sum(0)
     sums = jnp.sum(acc_s[2:14], axis=1)
@@ -526,7 +533,6 @@
     branch_back(1)
     side = lax.rem(me_b, 2)
     across = push(wire_s[1].at[1 - side], in_s[1], pair, "rc", 0)
-    last_m = add_up(2, sums_m)
     across.wait_recv()
     for n in range(batch // 2):
         mid_s[1][n] = (wire_s[1][side, n].astype(F32) + in_s[1][n].astype(F32)).astype(BF)
@@ -535,8 +541,7 @@
     for at, (k, n) in enumerate(plane):
         to_b, to_t = lax.rem(half + k // 2, batch // 2), lax.rem(me_t + n, tensor)
         last_1.append(push(mid_s[1].at[to_b, to_t], last_s[1].at[at], (2 * to_b + side, to_t), "rp", at))
-    last_0 = add_up(0, sums_0)
-    early, late = small_on("e", smalls[0]), small_on("l", smalls[1])
+    late = small_on("l", smalls[1])
 
     @pl.loop(0, NT_TILES, unroll=NT_TILES)
     def _(i):
@@ -549,8 +554,14 @@
 
     stores.append(pltpu.make_async_copy(ig_ref, r["ig_hbm"], r["store_sem"].at[1]))
     stores[1].start()
-    lanes = finish(2, last_m, 0) + finish(0, last_0, 512)
+    everyone = along_b + along_t + beyond
+    me = me_b * tensor + me_t
     sums = jnp.sum(acc_s[0:2], axis=1)
+    final = r["final"]
+    final[...] = jnp.concatenate([sums[0:1], sums[1:2]], 1)
+    r["finals"][me] = final[...]
+    gains = [push(final, r["finals"].at[me], peer, "fn", k) for k, peer in enumerate(everyone)]
+    lanes = finish(2, later["m"], 0) + finish(0, later["0"], 512)
     arrive(last_1)
     shard = mid_s[1][half, me_t].astype(F32)
     for at in range(len(plane)):
@@ -558,12 +569,10 @@
     shard_ref[:, 640:768] = shard
     lanes = jnp.sum(lanes + fold8(shard * shard), 0, keepdims=True)
     own = r["all"]
-    own[...] = jnp.concatenate([lanes, sums[0:1], sums[1:2]], 1)
-    me = me_b * tensor + me_t
+    own[...] = lanes
     sq_s[me] = own[...]
-    everyone = along_b + along_t + beyond
     square = [push(own, sq_s.at[me], peer, "sq", k) for k, peer in enumerate(everyone)]
-    arrive(early)
+    arrive(later["e"])
     arrive(late)
     first_sums, last_sums = in_order(r["smallte"], tensor), in_order(r["smalltl"], tensor)
     total_ref[2:14, :] = first_sums[0:12]
@@ -574,14 +583,15 @@
     first_sums = jnp.where((row < 4) | (row >= 8), first_sums, 0.0)
     vector = jnp.sum(first_sums * first_sums, 0, keepdims=True) + jnp.sum(last_sums * last_sums, 0, keepdims=True)
     vector = jnp.sum(vector, 1, keepdims=True)
+    arrive(gains)
+    whole = in_order(r["finals"], batch * tensor)
+    total_ref[0:1, :] = whole[:, 0:256]
+    total_ref[1:2, :] = whole[:, 256:512]
+    vector = vector + jnp.sum(whole * whole, 1, keepdims=True)
     arrive(square)
     for copy in sent:
         copy.wait_send()
-    whole = in_order(sq_s, batch * tensor)
-    total_ref[0:1, :] = whole[:, 128:384]
-    total_ref[1:2, :] = whole[:, 384:640]
-    lane = lax.broadcasted_iota(jnp.int32, whole.shape, 1)
-    matrix = jnp.sum(jnp.where(lane < 128, whole, whole * whole), 1, keepdims=True)
+    matrix = jnp.sum(in_order(sq_s, batch * tensor), 1, keepdims=True)
     size_ref[...] = jnp.broadcast_to(jnp.sqrt(matrix + vector), (8, 128))
     for copy in stores:
         copy.wait()
@@ -610,7 +620,7 @@
     for name, count in (("e", 24), ("l", 8)):
         items += [("small" + name, V((count, D), F32)), ("smallb" + name, V((batch, count, D), F32)), ("smalln" + name, V((count, D), F32)), ("smallt" + name, V((tensor, count, D), F32))]
     items += [
-        ("sq", V((batch * tensor, 1, 640), F32)), ("all", V((1, 640), F32)), ("rows", V((2, n // 2, 2 * PAD, D), BF)),
+        ("sq", V((batch * tensor, 1, 128), F32)), ("all", V((1, 128), F32)), ("finals", V((batch * tensor, 1, 512), F32)), ("final", V((1, 512), F32)), ("rows", V((2, n // 2, 2 * PAD, D), BF)),
         ("fc1", V((D, FF), BF)), ("fc2", V((D, FF), BF)), ("wcat", V((D, 768), BF)), ("projw", V((D, D), BF)), ("lepew", V((16, D), F32)), ("gp", V((D, D), BF)),
         ("n1", V((rows, D), BF)), ("n1t", V((D, rows), BF)), ("cott", V((D, rows), BF)), ("n2t", V((D, rows), BF)),
         ("q", V(stripe, BF)), ("k", V(stripe, BF)), ("v", V(stripe, BF)), ("a", V(stripe, BF)),
@@ -621,7 +631,7 @@
         ("load_sem", dma((5,))), ("store_sem", dma((2,))),
     ]
     b, t = batch - 1, tensor - 1
-    for name, shape in (("gp", (batch // 2 * tensor - 1,)), ("gc", (batch // 2 * tensor,)), ("gt", (2, t)), ("gb", (2, b)), ("rb", (3, b)), ("rt", (3, t)), ("rc", (1,)), ("rp", (batch // 2 * tensor - 1,)), ("sbe", (b,)), ("ste", (t,)), ("sbl", (b,)), ("stl", (t,)), ("sq", (batch * tensor - 1,))):
+    for name, shape in (("gp", (batch // 2 * tensor - 1,)), ("gc", (batch // 2 * tensor,)), ("gt", (2, t)), ("gb", (2, b)), ("rb", (3, b)), ("rt", (3, t)), ("rc", (1,)), ("rp", (batch // 2 * tensor - 1,)), ("sbe", (b,)), ("ste", (t,)), ("sbl", (b,)), ("stl", (t,)), ("sq", (batch * tensor - 1,)), ("fn", (batch * tensor - 1,))):
         items += [(name + "_s", dma(shape)), (name + "_r", dma(shape))]
     return items
 
@@ -660,20 +670,35 @@
     return master - rate * (hat / (jnp.sqrt(spread) + ADAM_EPS) + decay * master), first, second
 
 
-def update_kernel(
-    all_tokens, out_in, ig_in, shard_ref, total_ref, norm_ref,
-    qkv_w, qkv_m, proj_w, proj_m, fc1_w, fc1_m, fc2_w, fc2_m, norm_w, norm_m, lepe_w, lepe_m, bias_w, bias_m,
-    out_o, ig_o, qkv_g, qkv_n, qkv_l, qkv_o, proj_g, proj_n, proj_l, proj_o, fc1_g, fc1_n, fc1_l, fc1_o, fc2_g, fc2_n, fc2_l, fc2_o,
-    norm_g, norm_n, norm_o, lepe_g, lepe_n, lepe_o, bias_g, bias_n, bias_o, size_o, rms_o, out_s, ig_s, sems,
-):
+def update_kernel(all_tokens, count_in, count_out, *refs):
+    ins, refs = refs[:count_in], refs[count_in:]
+    outs, refs = refs[:count_out], refs[count_out:]
+    size_o, rms_o, refs = refs[0], refs[1], refs[2:]
+    held_in, refs = refs[:count_in], refs[count_in:]
+    held_out, (in_sem, out_sem, move_sem) = refs[:count_out], refs[count_out:]
+
     moves = []
-    for source, held, dest in ((out_in, out_s, out_o), (ig_in, ig_s, ig_o)):
-        step = held.shape[0] // 3
-        for n in range(3):
-            at = pl.ds(n * step, step)
-            moves.append([pltpu.make_async_copy(source.at[at], held.at[at], sems.at[0, len(moves)]), pltpu.make_async_copy(held.at[at], dest.at[at], sems.at[1, len(moves)])])
+    for n in range(2):
+        step = held_in[n].shape[0] // 3
+        for m in range(3):
+            at = pl.ds(m * step, step)
+            k = len(moves)
+            moves.append((pltpu.make_async_copy(ins[n].at[at], held_in[n].at[at], move_sem.at[0, k]), pltpu.make_async_copy(held_in[n].at[at], outs[n].at[at], move_sem.at[1, k])))
+    reads = [pltpu.make_async_copy(source, held, in_sem.at[n]) for n, (source, held) in enumerate(zip(ins[2:], held_in[2:]))]
+    for copy in reads:
+        copy.start()
     for into, _ in moves:
         into.start()
+    for copy in reads:
+        copy.wait()
+    writes = []
+
+    def write(n):
+        copy = pltpu.make_async_copy(held_out[n], outs[n], out_sem.at[n - 2])
+        copy.start()
+        writes.append(copy)
+
+    shard_ref, total_ref, norm_ref = held_in[2:5]
     size = norm_ref[0:1, 0:1]
     factor = jnp.minimum(1.0, CLIP_SCALE * math.sqrt(NPARAM) / (size + 1e-06))
     size_o[...] = size
@@ -688,52 +713,60 @@
         m_o[pair(0, at)] = first
         m_o[pair(1, at)] = second
 
+    every = (slice(None), slice(None))
+    middle = lambda n, at: (at[0], n, at[1])
+    given = held_in[5:]
+    lanes = lambda j: jnp.concatenate([shard_ref[:, 512 + 32 * j:544 + 32 * j], shard_ref[:, 640 + 32 * j:672 + 32 * j]], 1)
+    grads = [[((j,) + every, lanes(j)) for j in range(3)], [(every, lanes(3))], [(every, shard_ref[:, 0:256])], [(every, shard_ref[:, 256:512])]]
+    for n in range(4):
+        made = held_out[2 + 4 * n:6 + 4 * n]
+        for at, grad in grads[n]:
+            one(grad, given[2 * n], given[2 * n + 1], *made, at, RATE_MATRIX, DECAY_RATE)
+        for k in range(4):
+            write(2 + 4 * n + k)
+    bias = [((slice(f, f + 1), slice(None)), total_ref[10 + f // 2:11 + f // 2, 128 * (f % 2):128 * (f % 2) + 128]) for f in range(8)]
+    for n, parts in enumerate(([(every, total_ref[0:6])], [(every, total_ref[14:24])], bias)):
+        made = held_out[18 + 3 * n:21 + 3 * n]
+        for at, grad in parts:
+            one(grad, given[8 + 2 * n], given[9 + 2 * n], made[0], made[1], None, made[2], at, RATE_VECTOR, 0.0, middle)
+        for k in range(3):
+            write(18 + 3 * n + k)
     for into, away in moves:
         into.wait()
         away.start()
-    every = (slice(None), slice(None))
-    middle = lambda n, at: (at[0], n, at[1])
-    one(shard_ref[:, 0:256], fc1_w, fc1_m, fc1_g, fc1_n, fc1_l, fc1_o, every, RATE_MATRIX, DECAY_RATE)
-    one(shard_ref[:, 256:512], fc2_w, fc2_m, fc2_g, fc2_n, fc2_l, fc2_o, every, RATE_MATRIX, DECAY_RATE)
-    lanes = lambda j: jnp.concatenate([shard_ref[:, 512 + 32 * j:544 + 32 * j], shard_ref[:, 640 + 32 * j:672 + 32 * j]], 1)
-    for j in range(3):
-        one(lanes(j), qkv_w, qkv_m, qkv_g, qkv_n, qkv_l, qkv_o, (j,) + every, RATE_MATRIX, DECAY_RATE)
-    one(lanes(3), proj_w, proj_m, proj_g, proj_n, proj_l, proj_o, every, RATE_MATRIX, DECAY_RATE)
-    one(total_ref[0:6], norm_w, norm_m, norm_g, norm_n, None, norm_o, every, RATE_VECTOR, 0.0, middle)
-    one(total_ref[14:24], lepe_w, lepe_m, lepe_g, lepe_n, None, lepe_o, every, RATE_VECTOR, 0.0, middle)
-    for f in range(8):
-        at = (slice(f, f + 1), slice(None))
-        part = total_ref[10 + f // 2:11 + f // 2, 128 * (f % 2):128 * (f % 2) + 128]
-        one(part, bias_w, bias_m, bias_g, bias_n, None, bias_o, at, RATE_VECTOR, 0.0, middle)
     lane = lax.broadcasted_iota(jnp.int32, (1, 4), 1)
     sums = jnp.zeros((1, 4), F32)
     for n in range(4):
         sums = jnp.where(lane == n, jnp.sum(total_ref[6 + n:7 + n], 1, keepdims=True), sums)
     rms_o[...] = jnp.sqrt(sums * (1.0 / (all_tokens * D)))
+    for copy in writes:
+        copy.wait()
     for _, away in moves:
         away.wait()
 
 
 def update_call(all_tokens, out, ig, shard, total, norm, arrays):
     V = pltpu.VMEM
+    dma = pltpu.SemaphoreType.DMA
     like = lambda a, dt=F32: jax.ShapeDtypeStruct(a.shape, dt)
     outs = [like(out, BF), like(ig)]
-    H = pl.BlockSpec(memory_space=pl.ANY)
     for n in range(4):
         w, m = arrays[2 * n], arrays[2 * n + 1]
         outs += [like(w), like(w), like(w, BF), like(m)]
     for n in range(4, 7):
         w, m = arrays[2 * n], arrays[2 * n + 1]
         outs += [like(w), like(w), like(m)]
-    outs += [jax.ShapeDtypeStruct((1, 1), F32), jax.ShapeDtypeStruct((1, 4), F32)]
+    ins = (out, ig, shard, total, norm, *arrays)
+    H = pl.BlockSpec(memory_space=pl.ANY)
+    held_out = [V((8, 128), F32)] * 2 + [V(o.shape, o.dtype) for o in outs[2:]]
     return list(pl.pallas_call(
-        functools.partial(update_kernel, all_tokens),
-        out_shape=tuple(outs),
-        in_specs=[H, H] + [pl.BlockSpec(memory_space=V)] * (3 + len(arrays)),
-        out_specs=tuple([H, H] + [pl.BlockSpec(memory_space=V)] * (len(outs) - 2)),
-        scratch_shapes=[V(out.shape, BF), V(ig.shape, F32), pltpu.SemaphoreType.DMA((2, 6))],
+        functools.partial(update_kernel, all_tokens, len(ins), len(outs)),
+        out_shape=tuple(outs + [jax.ShapeDtypeStruct((1, 1), F32), jax.ShapeDtypeStruct((1, 4), F32)]),
+        in_specs=[H] * len(ins),
+        out_specs=tuple([H] * len(outs) + [pl.BlockSpec(memory_space=V)] * 2),
+        scratch_shapes=[V(a.shape, a.dtype) for a in ins] + held_out + [dma((len(ins) - 2,)), dma((len(outs) - 2,)), dma((2, 6))],
         compiler_params=pltpu.CompilerParams(vmem_limit_bytes=60 * 2**20),
-    )(out, ig, shard, total, norm, *arrays))
+    )(*ins))
 
 
 def flip(a):

time: 91.5 us -> 86.8 us (0.949)
  Pallas kernels: 90.4 us -> 85.8 us
    pallas_call x1, Pallas kernels: 85.2 us -> 80.7 us  [block_call(): pl.pallas_call(functools.partial(block_kernel, batch, tensor, linked), ou...]
where the time goes in v6:
time: 86.8 us; the launch traced here: 86.7 us
  Pallas kernels  85.8 us (99%)
    pallas_call x1, Pallas kernels, block_call(): pl.pallas_call(functools.partial(block_kernel, batch, tensor, linked), ou...  80.7 us
    pallas_call x1, Pallas kernels, update_call(): pl.pallas_call(functools.partial(update_kernel, all_tokens, len(ins), len...  5.1 us

profile of v6, /device:TPU:0, one launch (start us, length us, event | category | flops | bytes accessed | tf_op | source)
XLA Modules:
  0.0 86.7 jit_solution(13984266699775465531)
XLA Ops:
  0.7 80.7 %shard_map.419 = (bf16[2352,256]{1,0:T(8,128)(2,1)}, f32[2352,256]{1,0:T(8,128)}, f32[32,768]{1,0:T(8,128)}, f32[24,256]{1,0:T(8,128)}, f32[8,128]{1,0:T(8,128)}) custom-call(bf16[2352,256]{1,0:T(8,128)(2,1)} %refs_0_.1, bf16[2352,256]{1,0:T(8,128)(2,1)} %refs_1_.1, f32[3,32,64]{2,1,0:T(8,128)} %refs_5_.1, f32[32,64]{1,0:T(8,128)} %bitcast.30, ...), custom_call_target="tpu_custom_call" | custom-call | tf_op jit(solution)/shard_map/pallas_call | solution.py:649
  81.4 5.1 %shard_map.420 = (bf16[2352,256]{1,0:T(8,128)(2,1)}, f32[2352,256]{1,0:T(8,128)}, f32[3,32,64]{2,1,0:T(8,128)}, f32[3,32,64]{2,1,0:T(8,128)}, bf16[3,32,64]{2,1,...) custom-call(bf16[2352,256]{1,0:T(8,128)(2,1)} %get-tuple-element.63., ...), custom_call_target="tpu_custom_call" | custom-call | tf_op jit(solution)/shard_map/pallas_call | solution.py:762

commit v7 on v6

--- a/solution.py
+++ b/solution.py
@@ -479,15 +479,13 @@
                 dprobs_stage(b, s, after * 2 + s)
 
         pl.loop(0, images, unroll=2)(step)
-        if b == 1:
-            later["m"] = add_up(2, sums_m)
-            later["e"] = small_on("e", smalls[0])
-            later["0"] = add_up(0, sums_0)
-
         for s in range(2):
             dqkv_stage(b, s, images * 2 - 2 + s)
         if b == 1:
             smalls.append(small_out("l", pairs_of_taps(1)))
+            later["m"] = add_up(2, sums_m)
+            later["e"] = small_on("e", smalls[0])
+            later["0"] = add_up(0, sums_0)
         dense_rows(b, lambda at: jnp.concatenate([dq_s[b, at], dk_s[b, at], dv_s[b, at]], 1), dqkv_s, 384)
         gw = dot(n1t_s[...], dqkv_s[:, b * 384:(b + 1) * 384]).astype(BF)
         packed = dot_nt(jnp.concatenate([gw, r["gp"][:, b * 128:(b + 1) * 128]], 1), lane_ref[...]).astype(BF)

time: 86.8 us -> 87.1 us (level)
  no operation moved by 1% of the time
where the time goes in v7:
time: 87.1 us; the launch traced here: 86.9 us
  Pallas kernels  86 us (99%)
    pallas_call x1, Pallas kernels, block_call(): pl.pallas_call(functools.partial(block_kernel, batch, tensor, linked), ou...  80.9 us
    pallas_call x1, Pallas kernels, update_call(): pl.pallas_call(functools.partial(update_kernel, all_tokens, len(ins), len...  5.1 us

profile of v7, /device:TPU:0, one launch (start us, length us, event | category | flops | bytes accessed | tf_op | source)
XLA Modules:
  0.0 86.9 jit_solution(7542888985317594475)
XLA Ops:
  0.7 80.9 %shard_map.419 = (bf16[2352,256]{1,0:T(8,128)(2,1)}, f32[2352,256]{1,0:T(8,128)}, f32[32,768]{1,0:T(8,128)}, f32[24,256]{1,0:T(8,128)}, f32[8,128]{1,0:T(8,128)}) custom-call(bf16[2352,256]{1,0:T(8,128)(2,1)} %refs_0_.1, bf16[2352,256]{1,0:T(8,128)(2,1)} %refs_1_.1, f32[3,32,64]{2,1,0:T(8,128)} %refs_5_.1, f32[32,64]{1,0:T(8,128)} %bitcast.30, ...), custom_call_target="tpu_custom_call" | custom-call | tf_op jit(solution)/shard_map/pallas_call | solution.py:647
  81.6 5.1 %shard_map.420 = (bf16[2352,256]{1,0:T(8,128)(2,1)}, f32[2352,256]{1,0:T(8,128)}, f32[3,32,64]{2,1,0:T(8,128)}, f32[3,32,64]{2,1,0:T(8,128)}, bf16[3,32,64]{2,1,...) custom-call(bf16[2352,256]{1,0:T(8,128)(2,1)} %get-tuple-element.63., ...), custom_call_target="tpu_custom_call" | custom-call | tf_op jit(solution)/shard_map/pallas_call | solution.py:760
